TPU v7x, 512 devices: a whole 4x8x8 slice. The times are simulated.
512 devices in a mesh: beam: 128 (over x, y, z_lo), slab: 4 (over z_hi, core).
Axes of the slice: x: 4, y: 8, z: 8 (z_hi: 2, z_lo: 4; z = z_hi * 4 + z_lo), core: 2. Of those that a mesh axis runs over, the one named last changes fastest.
Arguments:
- potential: float32 [4, 3, 65536], P('slab', None, 'beam'), may hold values from 0 to 3
- tilts: int32 [128, 2], replicated, may hold values from -32 to 31
- aperture: int32 [128], replicated, may hold values 0 or 1
- positions: int32 [512, 2], replicated, may hold values from 0 to 127
Outputs:
- intensity: float32 [512, 16384], P('slab', 'beam')
All inputs are finite; a program needn't handle non-finite values.
Results may differ from a plain program's by a relative error of at most 0.00016.
Values sent between devices are 32-bit elements; how exact they have to be, the bound alone decides.
No kernel may reach another device: no remote copies, remote signals or barrier semaphores. Data moves between devices by JAX's collectives and lax.ppermute only.
A program may use at most 64 MiB of HBM per device.

v0:
```python
import math

import jax
import jax.numpy as jnp
from jax import lax
from jax.sharding import PartitionSpec as P

G = 256
K = 128
SLICES = 3


fresnel_rate = 0.00019
defocus_rate = 0.01


def phase_table(freqs, points, length, sign):
    index = freqs[:, None] * points[None, :] % length
    angle = sign * 2.0 * math.pi / length * index.astype(jnp.float32)
    return (jnp.cos(angle), jnp.sin(angle))


def propagator(freqs, limit):
    square = freqs[:, None] ** 2 + freqs[None, :] ** 2
    keep = (square <= limit).astype(jnp.float32)
    angle = -fresnel_rate * square.astype(jnp.float32)
    return (jnp.cos(angle) * keep, jnp.sin(angle) * keep)


def complex_product(first, second):
    return (
        first[0] * second[0] - first[1] * second[1],
        first[0] * second[1] + first[1] * second[0],
    )


def apply_left(table, wave):

    def contract(matrix, field):
        return jnp.einsum("mx,bxy->bmy", matrix, field, precision=lax.Precision.HIGHEST)

    return (
        contract(table[0], wave[0]) - contract(table[1], wave[1]),
        contract(table[0], wave[1]) + contract(table[1], wave[0]),
    )


def apply_right(table, wave):

    def contract(matrix, field):
        return jnp.einsum("ny,bxy->bxn", matrix, field, precision=lax.Precision.HIGHEST)

    return (
        contract(table[0], wave[0]) - contract(table[1], wave[1]),
        contract(table[0], wave[1]) + contract(table[1], wave[0]),
    )


def coefficients(places, tilts, aperture, size_k):
    index = (places[:, 0:1] * tilts[None, :, 0] + places[:, 1:2] * tilts[None, :, 1]) % size_k
    square = tilts[:, 0] ** 2 + tilts[:, 1] ** 2
    angle = (
        -(2.0 * math.pi / size_k) * index.astype(jnp.float32)
        - defocus_rate * square.astype(jnp.float32)[None, :]
    )
    weight = aperture.astype(jnp.float32)[None, :] * (1.0 / math.sqrt(tilts.shape[0]))
    return (jnp.cos(angle) * weight, jnp.sin(angle) * weight)


def intensity_of(coef, waves):

    def contract(matrix, field):
        return jnp.einsum("pb,bi->pi", matrix, field, precision=lax.Precision.HIGHEST)

    real_part = contract(coef[0], waves[0]) - contract(coef[1], waves[1])
    imag_part = contract(coef[0], waves[1]) + contract(coef[1], waves[0])
    return real_part * real_part + imag_part * imag_part


def transmit(piece):
    return jnp.stack([jnp.cos(piece), jnp.sin(piece)])


def per_device(potential, tilts, aperture, positions):
    devices = lax.axis_size("beam")
    configs = lax.axis_size("slab")
    beams = tilts.shape[0]
    probes = positions.shape[0]
    beams_here = beams // devices
    quarter = probes // configs
    pixels = K * K // devices
    points = jnp.arange(G, dtype=jnp.int32)
    band = jnp.arange(K, dtype=jnp.int32)
    band_freq = jnp.where(band < K // 2, band, band - K)
    limit = (G // 3) ** 2
    forward = phase_table(points, points, G, -1.0)
    inverse = phase_table(points, points, G, 1.0)
    crop_table = phase_table(band_freq, points, G, -1.0)
    back_table = phase_table(band, band, K, 1.0)
    kernel = propagator(jnp.where(points < G // 2, points, points - G), limit)
    band_kernel = propagator(band_freq, limit)
    layers = transmit(lax.all_gather(potential[0], "beam", axis=1, tiled=True))
    own = lax.dynamic_slice_in_dim(tilts, lax.axis_index("beam") * beams_here, beams_here, 0)
    index = (
        own[:, 0, None, None] * points[None, :, None]
        + own[:, 1, None, None] * points[None, None, :]
    ) % G
    angle = 2.0 * math.pi / G * index.astype(jnp.float32)
    wave = (jnp.cos(angle), jnp.sin(angle))
    for layer in range(SLICES):
        screen = layers[:, layer]
        screen = screen.reshape(2, G, G)
        wave = complex_product(wave, (screen[0][None], screen[1][None]))
        if layer < SLICES - 1:
            spectrum = apply_right(forward, apply_left(forward, wave))
            spectrum = complex_product(spectrum, kernel)
            wave = apply_right(inverse, apply_left(inverse, spectrum))
        else:
            spectrum = apply_right(crop_table, apply_left(crop_table, wave))
            spectrum = complex_product(spectrum, band_kernel)
            wave = apply_right(back_table, apply_left(back_table, spectrum))
        wave = (wave[0] * (1.0 / (G * G)), wave[1] * (1.0 / (G * G)))
    waves = jnp.stack(wave, 1)
    coef = coefficients(positions, tilts, aperture, K)
    block = lax.all_to_all(waves, "beam", split_axis=2, concat_axis=0, tiled=True)
    terms = intensity_of(coef, (block[:, 0, 0], block[:, 1, 0]))[:, None, :]
    summed = lax.psum_scatter(terms, "slab", scatter_dimension=0, tiled=True)
    return (summed / configs).reshape(quarter, pixels)


def solution(mesh):
    return jax.shard_map(
        per_device,
        mesh=mesh,
        in_specs=(P("slab", None, "beam"), P(), P(), P()),
        out_specs=P("slab", "beam"),
        check_vma=False,
    )
```

profile of v0, /device:TPU:1, one launch (start us, length us, event | category | flops | bytes accessed | tf_op | source)
XLA Modules:
  0.0 556.2 jit_solution(15311577020809994518)
XLA Ops:
  6.5 317.4 %all-gather = f32[1,3,65536]{2,0,1:T(1,128)S(1)} all-gather(f32[1,3,512]{2,0,1:T(1,128)} %param.4), channel_id=2, replica_groups=mesh['beam'=128,'slab'=4] {'beam'}, dimensions={2}, use_global_device_ids=true | all-gather | bytes 792576 | tf_op jit(solution)/shard_map/all_gather | solution.py:102
  323.9 22.0 %fusion.354 = (f32[1,3,65536]{2,0,1:T(1,128)S(1)}, f32[1,3,65536]{2,0,1:T(1,128)S(1)}) fusion(f32[1,3,65536]{2,0,1:T(1,128)S(1)} %all-gather), kind=kLoop, calls=%fused_computation.398 | loop fusion | bytes 2359296 | tf_op jit(solution)/shard_map/sin | solution.py:81
  345.9 4.1 slice_reduce_fusion
  352.9 2.6 fusion.67
  355.5 2.6 fusion.65
  358.1 2.8 fusion.15
  362.4 2.6 fusion.14
  366.5 1.5 convolution_subtract_fusion.7
  368.0 1.5 convolution_add_fusion.7
  369.5 2.5 fusion.75
  372.0 2.9 fusion.73
  375.0 2.5 fusion.13
  379.0 2.5 fusion.12
  384.8 1.5 multiply_subtract_fusion.1
  395.1 1.7 convolution_subtract_fusion.3
  398.3 2.5 fusion.71
  400.8 2.5 fusion.69
  403.5 2.5 fusion.7
  407.5 3.0 fusion.6
  413.5 1.5 multiply_subtract_fusion
  428.9 6.3 %all-to-all-start = ((f32[1,2,128,128]{3,1,0,2:T(2,128)}), f32[1,2,128,128]{3,1,0,2:T(2,128)S(1)}, u32[]{:S(2)}, u32[]{:S(2)}) async-start(f32[1,2,128,128]{3,1,0,2:T(2,128)} %copy.5), calls=%async_computation | async-start | bytes 262144 | tf_op jit(solution)/shard_map/all_to_all | solution.py:125
  435.9 10.3 %all-to-all-done = f32[1,2,128,128]{3,1,0,2:T(2,128)S(1)} async-done(((f32[1,2,128,128]{3,1,0,2:T(2,128)}), f32[1,2,128,128]{3,1,0,2:T(2,128)S(1)}, u32[]{:S(2)}, u32[]{:S(2)}) %all-to-all-start) | async-done | bytes 131104 | tf_op jit(solution)/shard_map/all_to_all | solution.py:125
  450.5 2.4 fusion.2
  452.9 94.7 %reduce-scatter.2.cloned.1.call-done = f32[128,1,128]{2,0,1:T(8,128)} async-done(((f32[512,1,128]{2,0,1:T(8,128)}), f32[128,1,128]{2,0,1:T(8,128)}) %reduce-scatter.2.cloned.1.call-update) | async-done | bytes 65552 | tf_op jit(solution)/shard_map/reduce_scatter | solution.py:127
  (61 shorter events, 45.7 us)
Async XLA Ops:
  350.2 0.7 copy-start
  428.9 6.4 %copy-start.2 = (s32[128]{0:T(128)S(1)}, s32[128]{0:T(128)}, u32[]{:S(2)}) copy-start(s32[128]{0:T(128)} %param.6) | copy-start | bytes 1540
  428.9 17.3 %all-to-all-start = ((f32[1,2,128,128]{3,1,0,2:T(2,128)}), f32[1,2,128,128]{3,1,0,2:T(2,128)S(1)}, u32[]{:S(2)}, u32[]{:S(2)}) async-start(f32[1,2,128,128]{3,1,0,2:T(2,128)} %copy.5), calls=%async_computation | async-start | bytes 262144 | tf_op jit(solution)/shard_map/all_to_all | solution.py:125
  435.2 0.7 copy-start.1
  435.2 112.5 %reduce-scatter.2.cloned.1.call-start = ((), (), s32[]{:S(2)}) async-start(), calls=%async_computation.2 | async-start | bytes 327680 | tf_op jit(solution)/shard_map/reduce_scatter | solution.py:127
Sparse Core Ops, SparseCore 0:
  453.1 94.5 reduce-scatter.1
where the time goes:
time: 559 us; the launch traced here: 556 us
  blocking collectives  317 us (57%)
  waiting for transfers between devices  105 us (19%)
  matrix products  81 us (14%)
  local copies, waits for them, and re-layouts  29.5 us (5%)
  between operations  14.1 us (3%)
  starting transfers between devices  6.34 us (1%)
    all_gather x1, blocking collectives, per_device(): layers = transmit(lax.all_gather(potential[0], 'beam', axis=1, tiled=True))  317 us
    reduce_scatter x1, waiting for transfers between devices, per_device(): summed = lax.psum_scatter(terms, 'slab', scatter_dimension=0, tiled=True)  94.7 us
    dot_general x24, matrix products, contract(): jnp.einsum('mx,bxy->bmy', matrix, field, precision=lax.Precision.HIGHEST)  45 us
    dot_general x24, matrix products, contract(): jnp.einsum('ny,bxy->bxn', matrix, field, precision=lax.Precision.HIGHEST)  29.4 us
    sin x1, local copies, waits for them, and re-layouts, transmit(): return jnp.stack([jnp.cos(piece), jnp.sin(piece)])  22 us
  transfers between devices with their start and end apart: 2, of which 2 were waited for; matrix products, arithmetic and copies ran while one was open for 0% of the time, Pallas kernels for 0%

commit v1 on v0

v1 whole, which is shorter than its diff:
```python
import math

import jax
import jax.numpy as jnp
import ml_dtypes
import numpy as np
from jax import lax
from jax.experimental import pallas as pl
from jax.experimental.pallas import tpu as pltpu
from jax.sharding import PartitionSpec as P

G = 256
K = 128
SLICES = 3
LIMIT = (G // 3) ** 2
REACH = G // 3
ROWS = 176

FRESNEL_RATE = 0.00019
DEFOCUS_RATE = 0.01

F32 = jnp.float32
BF16 = jnp.bfloat16


def split_table(table):
    high = table.astype(ml_dtypes.bfloat16)
    low = (table - high.astype(np.float64)).astype(ml_dtypes.bfloat16)
    return high, low


def waves_of(freqs, points, length, sign):
    return np.exp(sign * 2j * math.pi / length * ((freqs[:, None] * points[None, :]) % length))


def left_form(table):
    return np.block([[table.real, -table.imag], [table.imag, table.real]])


def right_form(table):
    return np.concatenate([table.real, table.imag], axis=1)


def tables():
    xs = np.concatenate([np.arange(0, G, 2), np.arange(1, G, 2)])
    ys = np.arange(G)
    us = np.arange(-REACH, REACH + 1)
    vs = np.where(ys < G // 2, ys, ys - G)
    chirp_u = np.exp(-1j * FRESNEL_RATE * us.astype(np.float64) ** 2)
    chirp_v = np.exp(-1j * FRESNEL_RATE * vs.astype(np.float64) ** 2)
    inside = np.abs(vs) <= REACH
    ahead_left = np.zeros((ROWS, G), np.complex128)
    ahead_left[: len(us)] = chirp_u[:, None] * waves_of(us, xs, G, -1) / G
    ahead_right = waves_of(ys, vs, G, -1) * (chirp_v * inside)[None, :] / G
    back_right = waves_of(vs, ys, G, 1) * inside[:, None]
    back_left = np.zeros((G, ROWS), np.complex128)
    back_left[:, : len(us)] = waves_of(xs, us, G, 1)
    band = np.arange(K)
    band_freq = np.where(band < K // 2, band, band - K)
    chirp_b = np.exp(-1j * FRESNEL_RATE * band_freq.astype(np.float64) ** 2)
    crop_left = chirp_b[:, None] * waves_of(band_freq, xs, G, -1) / G
    crop_right = waves_of(ys, band_freq, G, -1) * chirp_b[None, :] / G
    image = waves_of(band, band, K, 1)
    last = left_form(image).reshape(2, K, 2 * K).transpose(1, 0, 2).reshape(2 * K, 2 * K)
    out = []
    for table in (
        left_form(ahead_left),
        right_form(ahead_right),
        right_form(back_right),
        left_form(back_left),
        left_form(crop_left),
        right_form(crop_right),
        right_form(image),
        last,
    ):
        out.extend(split_table(table))
    return out


def split(value):
    high = value.astype(BF16)
    return high, (value - high.astype(F32)).astype(BF16)


def from_left(high_ref, low_ref, field):
    high, low = split(field)
    table = high_ref[...]
    return jnp.dot(
        jnp.concatenate([table, table, low_ref[...]], axis=1),
        jnp.concatenate([high, low, high], axis=0),
        preferred_element_type=F32,
    )


def from_right(field, high_ref, low_ref):
    high, low = split(field)
    table = high_ref[...]
    product = jnp.dot(
        jnp.concatenate([high, low, high], axis=1),
        jnp.concatenate([table, table, low_ref[...]], axis=0),
        preferred_element_type=F32,
    )
    m, n = product.shape[0] // 2, product.shape[1] // 2
    return product[:m, :n] - product[m:, n:], product[:m, n:] + product[m:, :n]


def sine_cosine(t):
    s = t * t
    sine = jnp.full_like(t, -2.5052108e-8)
    for term in (2.7557319e-6, -1.9841270e-4, 8.3333333e-3, -1.6666667e-1, 1.0):
        sine = sine * s + term
    cosine = jnp.full_like(t, 2.0876757e-9)
    for term in (-2.7557319e-7, 2.4801587e-5, -1.3888889e-3, 4.1666667e-2, -0.5, 1.0):
        cosine = cosine * s + term
    return sine * t, cosine


def circle(steps, length):
    near = ((steps + length // 2) & (length - 1)) - length // 2
    sine, cosine = sine_cosine(near.astype(F32) * (math.pi / length))
    return 2.0 * sine * cosine, 1.0 - 2.0 * sine * sine


def prepare_kernel(tilt_ref, places_ref, tilts_ref, weight_ref, start_ref, high_ref, low_ref):
    rows = lax.broadcasted_iota(jnp.int32, (G, G), 0)
    x = jnp.where(rows < G // 2, 2 * rows, 2 * rows - (G - 1))
    y = lax.broadcasted_iota(jnp.int32, (G, G), 1)
    sine, cosine = circle(tilt_ref[0] * x + tilt_ref[1] * y, G)
    start_ref[:G, :] = cosine
    start_ref[G:, :] = sine
    probes = places_ref.shape[0]
    beams = tilts_ref.shape[1]
    steps = places_ref[:, 0:1] * tilts_ref[0:1, :] + places_ref[:, 1:2] * tilts_ref[1:2, :]
    sine, cosine = circle(-steps, K)
    weight_re, weight_im = weight_ref[0:1, :], weight_ref[1:2, :]
    real = cosine * weight_re - sine * weight_im
    imag = cosine * weight_im + sine * weight_re
    for rows, columns, part in (
        (0, 0, real),
        (0, beams, -imag),
        (probes, 0, imag),
        (probes, beams, real),
    ):
        high, low = split(part)
        high_ref[rows : rows + probes, columns : columns + beams] = high
        low_ref[rows : rows + probes, columns : columns + beams] = low


def transmission(potential_ref, layer):
    stride = 4 * SLICES
    count = G // 2

    def rows(parity):
        return jnp.concatenate(
            [
                potential_ref[pl.ds(4 * layer + 2 * parity + half, count, stride), :]
                for half in range(2)
            ],
            axis=1,
        )

    sine, cosine = sine_cosine(jnp.concatenate([rows(0), rows(1)], axis=0) - 1.5)
    cos_mid, sin_mid = math.cos(1.5), math.sin(1.5)
    return cosine * cos_mid - sine * sin_mid, sine * cos_mid + cosine * sin_mid


def propagate_kernel(potential_ref, start_ref, *refs):
    ahead_left, ahead_right, back_right, back_left = (refs[2 * i : 2 * i + 2] for i in range(4))
    crop_left, crop_right, image_right, image_left = (refs[2 * i : 2 * i + 2] for i in range(4, 8))
    out_ref = refs[16]
    u = lax.broadcasted_iota(jnp.int32, (ROWS, G), 0) - REACH
    v = lax.broadcasted_iota(jnp.int32, (ROWS, G), 1)
    v = jnp.where(v < G // 2, v, v - G)
    keep = u * u + v * v <= LIMIT
    real, imag = start_ref[:G, :], start_ref[G:, :]
    for layer in range(SLICES):
        cosine, sine = transmission(potential_ref, layer)
        real, imag = real * cosine - imag * sine, real * sine + imag * cosine
        field = jnp.concatenate([real, imag], axis=0)
        if layer < SLICES - 1:
            real, imag = from_right(from_left(*ahead_left, field), *ahead_right)
            field = jnp.concatenate([jnp.where(keep, real, 0.0), jnp.where(keep, imag, 0.0)], axis=0)
            real, imag = from_right(field, *back_right)
            field = from_left(*back_left, jnp.concatenate([real, imag], axis=0))
            real, imag = field[:G], field[G:]
        else:
            real, imag = from_right(from_left(*crop_left, field), *crop_right)
            u = lax.broadcasted_iota(jnp.int32, (K, K), 0)
            v = lax.broadcasted_iota(jnp.int32, (K, K), 1)
            u = jnp.where(u < K // 2, u, u - K)
            v = jnp.where(v < K // 2, v, v - K)
            keep = u * u + v * v <= LIMIT
            field = jnp.concatenate([jnp.where(keep, real, 0.0), jnp.where(keep, imag, 0.0)], axis=0)
            real, imag = from_right(field, *image_right)
            out_ref[...] = from_left(*image_left, jnp.concatenate([real, imag], axis=0))


def probe_kernel(block_ref, high_ref, low_ref, *out_refs):
    beams = block_ref.shape[0] // 2
    field = jnp.concatenate(
        [block_ref[pl.ds(part, beams, 2), :] for part in range(2)], axis=0
    )
    waves = from_left(high_ref, low_ref, field)
    probes = waves.shape[0] // 2
    real, imag = waves[:probes], waves[probes:]
    total = (real * real + imag * imag) * (1.0 / len(out_refs))
    quarter = probes // len(out_refs)
    for i, out_ref in enumerate(out_refs):
        out_ref[...] = total[i * quarter : (i + 1) * quarter]


VMEM = pl.BlockSpec(memory_space=pltpu.VMEM)
SMEM = pl.BlockSpec(memory_space=pltpu.SMEM)
PARAMS = pltpu.CompilerParams(vmem_limit_bytes=24 * 1024 * 1024)


def per_device(sizes, potential, tilts, aperture, positions):
    nx, ny, nz = sizes
    devices = lax.axis_size("beam")
    configs = lax.axis_size("slab")
    beams = tilts.shape[0]
    probes = positions.shape[0]
    quarter = probes // configs
    own = lax.axis_index("beam")
    slab = lax.axis_index("slab")

    piece = potential.reshape(SLICES * G * G // devices // K, K)
    near = [[x * ny * nz + i for i in range(ny * nz)] for x in range(nx)]
    far = [[x * ny * nz + i for x in range(nx)] for i in range(ny * nz)]
    part = lax.all_to_all(
        jnp.broadcast_to(piece[None], (ny * nz, *piece.shape)), "beam", 0, 0, axis_index_groups=near
    )
    part = part.reshape(ny * nz * piece.shape[0], K)
    whole = lax.all_to_all(
        jnp.broadcast_to(part[None], (nx, *part.shape)), "beam", 0, 0, axis_index_groups=far
    ).reshape(devices * piece.shape[0], K)

    order = jnp.bitwise_xor(slab, jnp.arange(configs, dtype=jnp.int32))
    places = positions.reshape(configs, quarter, 2)[order].reshape(probes, 2)
    square = (tilts[:, 0] ** 2 + tilts[:, 1] ** 2).astype(F32)
    amount = aperture.astype(F32) * (1.0 / math.sqrt(beams))
    weight = jnp.stack([jnp.cos(DEFOCUS_RATE * square) * amount, -jnp.sin(DEFOCUS_RATE * square) * amount])
    tilt = lax.dynamic_index_in_dim(tilts, own, 0, keepdims=False)
    start, coef_high, coef_low = pl.pallas_call(
        prepare_kernel,
        out_shape=(
            jax.ShapeDtypeStruct((2 * G, G), F32),
            jax.ShapeDtypeStruct((2 * probes, 2 * beams), BF16),
            jax.ShapeDtypeStruct((2 * probes, 2 * beams), BF16),
        ),
        in_specs=[SMEM, VMEM, VMEM, VMEM],
        out_specs=(VMEM, VMEM, VMEM),
        compiler_params=PARAMS,
        name="prepare",
    )(tilt, places, tilts.T, weight)

    constants = [jnp.asarray(table) for table in tables()]
    image = pl.pallas_call(
        propagate_kernel,
        out_shape=jax.ShapeDtypeStruct((2 * K, K), F32),
        in_specs=[VMEM] * (2 + len(constants)),
        out_specs=VMEM,
        compiler_params=PARAMS,
        name="propagate",
    )(whole, start, *constants)

    block = lax.all_to_all(image.reshape(K, 2, K), "beam", 0, 0).reshape(2 * beams, K)
    parts = pl.pallas_call(
        probe_kernel,
        out_shape=[jax.ShapeDtypeStruct((quarter, K), F32)] * configs,
        in_specs=[VMEM] * 3,
        out_specs=[VMEM] * configs,
        compiler_params=PARAMS,
        name="probe",
    )(block, coef_high, coef_low)

    def swap(value, bit):
        return lax.ppermute(value, "slab", [(i, i ^ bit) for i in range(configs)])

    got = swap(jnp.concatenate([parts[1], parts[3]], axis=0), 1)
    other = parts[2] + got[quarter:]
    return parts[0] + got[:quarter] + swap(other, 2)


def solution(mesh):
    def step(*args):
        return per_device((4, 8, 4), *args)

    return jax.shard_map(
        step,
        mesh=mesh,
        in_specs=(P("slab", None, "beam"), P(), P(), P()),
        out_specs=P("slab", "beam"),
        check_vma=False,
    )
```

time: 559 us -> 98.9 us (0.18)
  blocking collectives: 317 us -> 20.9 us
  waiting for transfers between devices: 105 us -> 20.9 us
  matrix products: 81 us -> 0 us
  starting transfers between devices: 6.34 us -> 30.5 us
  local copies, waits for them, and re-layouts: 29.5 us -> 14.7 us
  between operations: 14.1 us -> 0.18 us
  Pallas kernels: 0 us -> 9.45 us
    all_gather x1 -> x0, blocking collectives: 317 us -> none  [per_device(): layers = transmit(lax.all_gather(potential[0], 'beam', axis=1, tiled=True))]
    reduce_scatter x1 -> x0, waiting for transfers between devices: 94.7 us -> none  [per_device(): summed = lax.psum_scatter(terms, 'slab', scatter_dimension=0, tiled=True)]
    dot_general x52 -> x0, matrix products: 81 us -> none  [the longest x24 45 us: contract(): jnp.einsum('mx,bxy->bmy', matrix, field, precision=lax.Precision.HIGHEST)]
    sin x1 -> x0, local copies, waits for them, and re-layouts: 22 us -> none  [transmit(): return jnp.stack([jnp.cos(piece), jnp.sin(piece)])]
    all_to_all x0 -> x1, blocking collectives: none -> 20.9 us  [per_device(): lax.all_to_all(image.reshape(K, 2, K), 'beam', 0, 0).reshape(2 * beams, K)]
    ppermute x0 -> x2, starting transfers between devices: none -> 13.1 us  [swap(): return lax.ppermute(value, 'slab', [(i, i ^ bit) for i in range(configs)])]
    all_to_all x1 -> x2, starting transfers between devices: 6.3 us -> 17.5 us  [the longest x1 13.5 us: per_device(): lax.all_to_all(jnp.broadcast_to(piece[None], (ny * nz, *piece.shape)), 'b...]
    unnamed x6 -> x38, local copies, waits for them, and re-layouts: 1.27 us -> 12.1 us
  transfers between devices with their start and end apart: 2 -> 4, of which waited for: 2 -> 4; matrix products, arithmetic and copies ran while one was open for 0% -> 1% of each run, Pallas kernels for 0% -> 2%
where the time goes in v1:
time: 98.9 us; the launch traced here: 98.1 us
  starting transfers between devices  30.5 us (31%)
  waiting for transfers between devices  20.9 us (21%)
  blocking collectives  20.9 us (21%)
  local copies, waits for them, and re-layouts  14.7 us (15%)
  Pallas kernels  9.45 us (10%)
  other arithmetic  1.5 us (2%)
    all_to_all x1, blocking collectives, per_device(): lax.all_to_all(image.reshape(K, 2, K), 'beam', 0, 0).reshape(2 * beams, K)  20.9 us
    all_to_all x1, starting transfers between devices, per_device(): lax.all_to_all(jnp.broadcast_to(piece[None], (ny * nz, *piece.shape)), 'b...  13.5 us
    ppermute x2, starting transfers between devices, swap(): return lax.ppermute(value, 'slab', [(i, i ^ bit) for i in range(configs)])  13.1 us
    unnamed x38, local copies, waits for them, and re-layouts  12.1 us
    all_to_all x1, waiting for transfers between devices, per_device(): lax.all_to_all(jnp.broadcast_to(piece[None], (ny * nz, *piece.shape)), 'b...  11.5 us
    pallas_call x1, Pallas kernels, per_device(): pl.pallas_call(propagate_kernel, out_shape=jax.ShapeDtypeStruct((2 * K, K...  7.26 us
    all_to_all x1, waiting for transfers between devices, per_device(): lax.all_to_all(jnp.broadcast_to(part[None], (nx, *part.shape)), 'beam', 0...  6.26 us
    all_to_all x1, starting transfers between devices, per_device(): lax.all_to_all(jnp.broadcast_to(part[None], (nx, *part.shape)), 'beam', 0...  4.01 us
  transfers between devices with their start and end apart: 4, of which 4 were waited for; matrix products, arithmetic and copies ran while one was open for 1% of the time, Pallas kernels for 2%

profile of v1, /device:TPU:1, one launch (start us, length us, event | category | flops | bytes accessed | tf_op | source)
XLA Modules:
  0.0 98.1 jit_solution(9813906344191402668)
XLA Ops:
  1.5 13.5 %all-to-all-start = ((f32[32,12,128]{2,1,0:T(8,128)}), f32[32,12,128]{2,1,0:T(8,128)S(1)}, u32[]{:S(2)}, u32[]{:S(2)}) async-start(f32[32,12,128]{2,1,0:T(8,128)} %broadcast_in_dim.16), calls=%async_computation | async-start | bytes 524288 | tf_op jit(solution)/shard_map/all_to_all | solution.py:230
  15.0 11.5 %all-to-all-done = f32[32,12,128]{2,1,0:T(8,128)S(1)} async-done(((f32[32,12,128]{2,1,0:T(8,128)}), f32[32,12,128]{2,1,0:T(8,128)S(1)}, u32[]{:S(2)}, u32[]{:S(2)}) %all-to-all-start) | async-done | bytes 196640 | tf_op jit(solution)/shard_map/all_to_all | solution.py:230
  26.4 0.9 broadcast_in_dim.18
  27.4 4.0 %all-to-all-start.1 = ((f32[4,384,128]{2,1,0:T(8,128)}), f32[4,384,128]{2,1,0:T(8,128)S(1)}, u32[]{:S(2)}, u32[]{:S(2)}) async-start(f32[4,384,128]{2,1,0:T(8,128)} %broadcast_in_dim.18), calls=%async_computation.1 | async-start | bytes 1572864 | tf_op jit(solution)/shard_map/all_to_all | solution.py:234
  32.5 1.6 %prepare.1 = (f32[512,256]{1,0:T(8,128)S(1)}, bf16[1024,256]{1,0:T(8,128)(2,1)S(1)}, bf16[1024,256]{1,0:T(8,128)(2,1)S(1)}) custom-call(s32[2]{0:T(128)S(1)} %dynamic-slice_reduce_fusion.tilt_ref, s32[512,2]{1,0:T(8,128)S(1)} %bitcast.22, s32[2,128]{1,0:T(2,128)S(1)} %bitcast.25, f32[2,128]{1,0:T(2,128)S(1)} %pad_maximum_fusion.1.weight_ref), custom_call_target="tpu_custom_call" | custom-call | tf_op jit(solution)/shard_map/prepare/pallas_call | solution.py:244
  34.1 6.3 %all-to-all-done.1 = f32[4,384,128]{2,1,0:T(8,128)S(1)} async-done(((f32[4,384,128]{2,1,0:T(8,128)}), f32[4,384,128]{2,1,0:T(8,128)S(1)}, u32[]{:S(2)}, u32[]{:S(2)}) %all-to-all-start.1) | async-done | bytes 786464 | tf_op jit(solution)/shard_map/all_to_all | solution.py:234
  40.4 1.0 copy-done.3
  41.4 1.0 %copy-done.4 = bf16[352,512]{1,0:T(8,128)(2,1)S(1)} copy-done((bf16[352,512]{1,0:T(8,128)(2,1)S(1)}, bf16[352,512]{1,0:T(8,128)(2,1)}, u32[]{:S(2)}) %copy-start.4) | copy-done | bytes 360472
  42.4 0.9 copy-done.5
  43.3 0.9 copy-done.6
  44.3 0.9 copy-done.7
  45.2 0.9 copy-done.8
  46.2 0.9 copy-done.9
  47.1 0.9 copy-done.10
  48.1 0.9 copy-done.12
  49.0 0.9 copy-done.13
  49.9 0.9 copy-done.14
  50.8 0.8 copy-done.15
  52.5 7.3 %propagate.1 = f32[256,128]{1,0:T(8,128)S(1)} custom-call(f32[1536,128]{1,0:T(8,128)S(1)} %bitcast.21, f32[512,256]{1,0:T(8,128)S(1)} %get-tuple-element.12.start_ref, bf16[352,512]{1,0:T(8,128)(2,1)S(1)} %copy-done.4, bf16[352,512]{1,0:T(8,128)(2,1)S(1)} %copy-done.3, bf16[256,512]{1,0:T(8,128)(2,1)S(1)} %copy-done.10, bf16[256,512]{1,0:T(8,128)(2,1)S(1)} %copy-done.9, ...), custom_call_target="tpu_custom_call" | custom-call | tf_op jit(solution)/shard_map/propagate/pallas_call | solution.py:258
  59.7 20.9 %all_to_all.15 = f32[128,2,128]{2,1,0:T(2,128)S(1)} all-to-all(f32[128,2,128]{2,1,0:T(2,128)S(1)} %bitcast.23), channel_id=1, replica_groups=mesh['beam'=128,'slab'=4] {'beam'}, dimensions={0} | all-to-all | bytes 262144 | tf_op jit(solution)/shard_map/all_to_all | solution.py:267
  81.3 5.1 %collective-permute-start = (f32[256,128]{1,0:T(8,128)S(1)}, f32[256,128]{1,0:T(8,128)S(1)}, u32[]{:S(2)}, u32[]{:S(2)}) collective-permute-start(f32[256,128]{1,0:T(8,128)S(1)} %pad_maximum_fusion), channel_id=1, source_target_pairs={{0,1},{1,0},{2,3},{3,2},{4,5},{5,4},{6,7},{7,6},{8,9},{9,8},{10,11... | collective-permute-start | bytes 393224 | tf_op jit(solution)/shard_map/ppermute | solution.py:278
  86.4 1.0 collective-permute-done
  87.4 7.9 %collective-permute-start.1 = (f32[128,128]{1,0:T(8,128)S(1)}, f32[128,128]{1,0:T(8,128)S(1)}, u32[]{:S(2)}, u32[]{:S(2)}) collective-permute-start(f32[128,128]{1,0:T(8,128)S(1)} %slice_add_fusion), channel_id=1, source_target_pairs={{0,2},{1,3},{2,0},{3,1},{4,6},{5,7},{6,4},{7,5},{8,10},{9,11},{10,... | collective-permute-start | bytes 196616 | tf_op jit(solution)/shard_map/ppermute | solution.py:278
  95.3 2.2 %collective-permute-done.1 = f32[128,128]{1,0:T(8,128)S(1)} collective-permute-done((f32[128,128]{1,0:T(8,128)S(1)}, f32[128,128]{1,0:T(8,128)S(1)}, u32[]{:S(2)}, u32[]{:S(2)}) %collective-permute-start.1) | collective-permute-done | bytes 65568 | tf_op jit(solution)/shard_map/ppermute | solution.py:278
  (42 shorter events, 4.6 us)
Async XLA Ops:
  0.0 31.4 %copy-start = (s32[512,2]{0,1:T(2,128)S(1)}, s32[512,2]{0,1:T(2,128)}, u32[]{:S(2)}) copy-start(s32[512,2]{0,1:T(2,128)} %param.23) | copy-start | bytes 12292
  1.5 25.0 %all-to-all-start = ((f32[32,12,128]{2,1,0:T(8,128)}), f32[32,12,128]{2,1,0:T(8,128)S(1)}, u32[]{:S(2)}, u32[]{:S(2)}) async-start(f32[32,12,128]{2,1,0:T(8,128)} %broadcast_in_dim.16), calls=%async_computation | async-start | bytes 524288 | tf_op jit(solution)/shard_map/all_to_all | solution.py:230
  27.4 13.0 %all-to-all-start.1 = ((f32[4,384,128]{2,1,0:T(8,128)}), f32[4,384,128]{2,1,0:T(8,128)S(1)}, u32[]{:S(2)}, u32[]{:S(2)}) async-start(f32[4,384,128]{2,1,0:T(8,128)} %broadcast_in_dim.18), calls=%async_computation.1 | async-start | bytes 1572864 | tf_op jit(solution)/shard_map/all_to_all | solution.py:234
  31.4 0.8 copy-start.17
  31.4 1.0 copy-start.18
  31.4 9.0 %copy-start.2 = (bf16[512,352]{1,0:T(8,128)(2,1)S(1)}, bf16[512,352]{1,0:T(8,128)(2,1)}, u32[]{:S(2)}) copy-start(bf16[512,352]{1,0:T(8,128)(2,1)} %constant.60.clone.refs_6_) | copy-start | bytes 1081348
  32.0 8.4 %copy-start.1 = (bf16[512,352]{1,0:T(8,128)(2,1)S(1)}, bf16[512,352]{1,0:T(8,128)(2,1)}, u32[]{:S(2)}) copy-start(bf16[512,352]{1,0:T(8,128)(2,1)} %constant.61.clone.refs_7_) | copy-start | bytes 1081348
  32.5 7.9 %copy-start.11 = (bf16[256,256]{1,0:T(8,128)(2,1)S(1)}, bf16[256,256]{1,0:T(8,128)(2,1)}, u32[]{:S(2)}) copy-start(bf16[256,256]{1,0:T(8,128)(2,1)} %constant.69.clone.refs_15_) | copy-start | bytes 393220
  40.4 1.0 %copy-start.3 = (bf16[352,512]{1,0:T(8,128)(2,1)S(1)}, bf16[352,512]{1,0:T(8,128)(2,1)}, u32[]{:S(2)}) copy-start(bf16[352,512]{1,0:T(8,128)(2,1)} %constant.55.clone.refs_1_) | copy-start | bytes 1081348
  41.4 1.0 %copy-start.4 = (bf16[352,512]{1,0:T(8,128)(2,1)S(1)}, bf16[352,512]{1,0:T(8,128)(2,1)}, u32[]{:S(2)}) copy-start(bf16[352,512]{1,0:T(8,128)(2,1)} %constant.54.clone.refs_0_) | copy-start | bytes 1081348
  42.4 0.9 copy-start.5
  43.3 0.9 copy-start.6
  44.3 0.9 copy-start.7
  45.2 0.9 copy-start.8
  46.2 0.9 copy-start.9
  47.1 0.9 copy-start.10
  48.1 0.9 copy-start.12
  49.0 0.9 copy-start.13
  49.9 0.9 copy-start.14
  50.8 0.8 copy-start.15
  51.6 0.8 copy-start.16
  81.3 6.1 %collective-permute-start = (f32[256,128]{1,0:T(8,128)S(1)}, f32[256,128]{1,0:T(8,128)S(1)}, u32[]{:S(2)}, u32[]{:S(2)}) collective-permute-start(f32[256,128]{1,0:T(8,128)S(1)} %pad_maximum_fusion), channel_id=1, source_target_pairs={{0,1},{1,0},{2,3},{3,2},{4,5},{5,4},{6,7},{7,6},{8,9},{9,8},{10,11... | collective-permute-start | bytes 393224 | tf_op jit(solution)/shard_map/ppermute | solution.py:278
  87.4 10.1 %collective-permute-start.1 = (f32[128,128]{1,0:T(8,128)S(1)}, f32[128,128]{1,0:T(8,128)S(1)}, u32[]{:S(2)}, u32[]{:S(2)}) collective-permute-start(f32[128,128]{1,0:T(8,128)S(1)} %slice_add_fusion), channel_id=1, source_target_pairs={{0,2},{1,3},{2,0},{3,1},{4,6},{5,7},{6,4},{7,5},{8,10},{9,11},{10,... | collective-permute-start | bytes 196616 | tf_op jit(solution)/shard_map/ppermute | solution.py:278

commit v2 on v1

--- a/solution.py
+++ b/solution.py
@@ -1,3 +1,4 @@
+import functools
 import math
 
 import jax
@@ -15,6 +16,18 @@
 LIMIT = (G // 3) ** 2
 REACH = G // 3
 ROWS = 176
+
+WIDTH = 2 * G
+TABLES = (
+    (2 * ROWS, 2 * G),
+    (G, 2 * G),
+    (G, 2 * G),
+    (2 * G, 2 * ROWS),
+    (2 * K, 2 * G),
+    (G, 2 * K),
+    (K, 2 * K),
+    (2 * K, 2 * K),
+)
 
 FRESNEL_RATE = 0.00019
 DEFOCUS_RATE = 0.01
@@ -73,8 +86,22 @@
         right_form(image),
         last,
     ):
-        out.extend(split_table(table))
-    return out
+        high, low = split_table(table)
+        if table.shape[1] <= WIDTH // 2:
+            rows = [np.concatenate([high, low], axis=1)]
+        else:
+            rows = [np.pad(term, ((0, 0), (0, WIDTH - table.shape[1]))) for term in (high, low)]
+        out.append(np.concatenate(rows, axis=0))
+    return np.concatenate(out, axis=0)
+
+
+def table_of(ref, which):
+    shapes = TABLES[:which]
+    m, n = TABLES[which]
+    at = sum(rows * (1 if columns <= WIDTH // 2 else 2) for rows, columns in shapes)
+    if n <= WIDTH // 2:
+        return ref[at : at + m, :n], ref[at : at + m, n : 2 * n]
+    return ref[at : at + m, :n], ref[at + m : at + 2 * m, :n]
 
 
 def split(value):
@@ -82,22 +109,20 @@
     return high, (value - high.astype(F32)).astype(BF16)
 
 
-def from_left(high_ref, low_ref, field):
+def from_left(table, field):
     high, low = split(field)
-    table = high_ref[...]
     return jnp.dot(
-        jnp.concatenate([table, table, low_ref[...]], axis=1),
+        jnp.concatenate([table[0], table[0], table[1]], axis=1),
         jnp.concatenate([high, low, high], axis=0),
         preferred_element_type=F32,
     )
 
 
-def from_right(field, high_ref, low_ref):
+def from_right(field, table):
     high, low = split(field)
-    table = high_ref[...]
     product = jnp.dot(
         jnp.concatenate([high, low, high], axis=1),
-        jnp.concatenate([table, table, low_ref[...]], axis=0),
+        jnp.concatenate([table[0], table[0], table[1]], axis=0),
         preferred_element_type=F32,
     )
     m, n = product.shape[0] // 2, product.shape[1] // 2
@@ -125,7 +150,7 @@
     rows = lax.broadcasted_iota(jnp.int32, (G, G), 0)
     x = jnp.where(rows < G // 2, 2 * rows, 2 * rows - (G - 1))
     y = lax.broadcasted_iota(jnp.int32, (G, G), 1)
-    sine, cosine = circle(tilt_ref[0] * x + tilt_ref[1] * y, G)
+    sine, cosine = circle(tilt_ref[0] * (x + tilt_ref[2]) + tilt_ref[1] * y, G)
     start_ref[:G, :] = cosine
     start_ref[G:, :] = sine
     probes = places_ref.shape[0]
@@ -146,17 +171,22 @@
         low_ref[rows : rows + probes, columns : columns + beams] = low
 
 
-def transmission(potential_ref, layer):
+def transmission(potential_refs, layer):
     stride = 4 * SLICES
-    count = G // 2
 
     def rows(parity):
         return jnp.concatenate(
             [
-                potential_ref[pl.ds(4 * layer + 2 * parity + half, count, stride), :]
-                for half in range(2)
+                jnp.concatenate(
+                    [
+                        ref[pl.ds(4 * layer + 2 * parity + half, ref.shape[0] // stride, stride), :]
+                        for half in range(2)
+                    ],
+                    axis=1,
+                )
+                for ref in potential_refs
             ],
-            axis=1,
+            axis=0,
         )
 
     sine, cosine = sine_cosine(jnp.concatenate([rows(0), rows(1)], axis=0) - 1.5)
@@ -164,35 +194,40 @@
     return cosine * cos_mid - sine * sin_mid, sine * cos_mid + cosine * sin_mid
 
 
-def propagate_kernel(potential_ref, start_ref, *refs):
-    ahead_left, ahead_right, back_right, back_left = (refs[2 * i : 2 * i + 2] for i in range(4))
-    crop_left, crop_right, image_right, image_left = (refs[2 * i : 2 * i + 2] for i in range(4, 8))
-    out_ref = refs[16]
-    u = lax.broadcasted_iota(jnp.int32, (ROWS, G), 0) - REACH
-    v = lax.broadcasted_iota(jnp.int32, (ROWS, G), 1)
-    v = jnp.where(v < G // 2, v, v - G)
-    keep = u * u + v * v <= LIMIT
+def masked(real, imag, first, limit_of):
+    u = lax.broadcasted_iota(jnp.int32, real.shape, 0)
+    v = lax.broadcasted_iota(jnp.int32, real.shape, 1)
+    half = real.shape[1] // 2
+    u = u - first if first else jnp.where(u < half, u, u - 2 * half)
+    v = jnp.where(v < half, v, v - 2 * half)
+    keep = u * u + v * v <= limit_of
+    return jnp.concatenate([jnp.where(keep, real, 0.0), jnp.where(keep, imag, 0.0)], axis=0)
+
+
+def propagate_kernel(turn_ref, table_ref, start_ref, *refs):
+    potential_refs, out_ref = refs[:-1], refs[-1]
+    blocks = len(potential_refs)
+    table = functools.partial(table_of, table_ref)
     real, imag = start_ref[:G, :], start_ref[G:, :]
     for layer in range(SLICES):
-        cosine, sine = transmission(potential_ref, layer)
+        cosine, sine = transmission(potential_refs, layer)
         real, imag = real * cosine - imag * sine, real * sine + imag * cosine
         field = jnp.concatenate([real, imag], axis=0)
         if layer < SLICES - 1:
-            real, imag = from_right(from_left(*ahead_left, field), *ahead_right)
-            field = jnp.concatenate([jnp.where(keep, real, 0.0), jnp.where(keep, imag, 0.0)], axis=0)
-            real, imag = from_right(field, *back_right)
-            field = from_left(*back_left, jnp.concatenate([real, imag], axis=0))
+            field = from_left(table(0), field)
+            field = masked(*from_right(field, table(1)), REACH, LIMIT)
+            real, imag = from_right(field, table(2))
+            field = from_left(table(3), jnp.concatenate([real, imag], axis=0))
             real, imag = field[:G], field[G:]
         else:
-            real, imag = from_right(from_left(*crop_left, field), *crop_right)
-            u = lax.broadcasted_iota(jnp.int32, (K, K), 0)
-            v = lax.broadcasted_iota(jnp.int32, (K, K), 1)
-            u = jnp.where(u < K // 2, u, u - K)
-            v = jnp.where(v < K // 2, v, v - K)
-            keep = u * u + v * v <= LIMIT
-            field = jnp.concatenate([jnp.where(keep, real, 0.0), jnp.where(keep, imag, 0.0)], axis=0)
-            real, imag = from_right(field, *image_right)
-            out_ref[...] = from_left(*image_left, jnp.concatenate([real, imag], axis=0))
+            field = from_left(table(4), field)
+            field = masked(*from_right(field, table(5)), 0, LIMIT)
+            real, imag = from_right(field, table(6))
+            image = from_left(table(7), jnp.concatenate([real, imag], axis=0))
+    rows = image.shape[0] // blocks
+    for k in range(blocks):
+        place = lax.rem(turn_ref[0] + k, blocks) * rows
+        out_ref[pl.ds(pl.multiple_of(place, rows), rows), :] = image[k * rows : (k + 1) * rows]
 
 
 def probe_kernel(block_ref, high_ref, low_ref, *out_refs):
@@ -200,7 +235,7 @@
     field = jnp.concatenate(
         [block_ref[pl.ds(part, beams, 2), :] for part in range(2)], axis=0
     )
-    waves = from_left(high_ref, low_ref, field)
+    waves = from_left((high_ref[...], low_ref[...]), field)
     probes = waves.shape[0] // 2
     real, imag = waves[:probes], waves[probes:]
     total = (real * real + imag * imag) * (1.0 / len(out_refs))
@@ -225,22 +260,27 @@
     slab = lax.axis_index("slab")
 
     piece = potential.reshape(SLICES * G * G // devices // K, K)
-    near = [[x * ny * nz + i for i in range(ny * nz)] for x in range(nx)]
-    far = [[x * ny * nz + i for x in range(nx)] for i in range(ny * nz)]
+    run = ny * nz
+    near = [[x * run + i for i in range(run)] for x in range(nx)]
     part = lax.all_to_all(
-        jnp.broadcast_to(piece[None], (ny * nz, *piece.shape)), "beam", 0, 0, axis_index_groups=near
-    )
-    part = part.reshape(ny * nz * piece.shape[0], K)
-    whole = lax.all_to_all(
-        jnp.broadcast_to(part[None], (nx, *part.shape)), "beam", 0, 0, axis_index_groups=far
-    ).reshape(devices * piece.shape[0], K)
+        jnp.broadcast_to(piece[None], (run, *piece.shape)), "beam", 0, 0, axis_index_groups=near
+    ).reshape(run * piece.shape[0], K)
+
+    def fetch(k):
+        return lax.ppermute(
+            part, "beam", [((x + k) % nx * run + i, x * run + i) for x in range(nx) for i in range(run)]
+        )
+
+    blocks = [part] + [fetch(k) for k in range(1, nx)]
 
     order = jnp.bitwise_xor(slab, jnp.arange(configs, dtype=jnp.int32))
     places = positions.reshape(configs, quarter, 2)[order].reshape(probes, 2)
     square = (tilts[:, 0] ** 2 + tilts[:, 1] ** 2).astype(F32)
     amount = aperture.astype(F32) * (1.0 / math.sqrt(beams))
     weight = jnp.stack([jnp.cos(DEFOCUS_RATE * square) * amount, -jnp.sin(DEFOCUS_RATE * square) * amount])
-    tilt = lax.dynamic_index_in_dim(tilts, own, 0, keepdims=False)
+    place = own // run
+    turn = place.reshape(1)
+    tilt = jnp.concatenate([lax.dynamic_index_in_dim(tilts, own, 0, keepdims=False), turn * (G // nx)])
     start, coef_high, coef_low = pl.pallas_call(
         prepare_kernel,
         out_shape=(
@@ -254,15 +294,14 @@
         name="prepare",
     )(tilt, places, tilts.T, weight)
 
-    constants = [jnp.asarray(table) for table in tables()]
     image = pl.pallas_call(
         propagate_kernel,
         out_shape=jax.ShapeDtypeStruct((2 * K, K), F32),
-        in_specs=[VMEM] * (2 + len(constants)),
+        in_specs=[SMEM] + [VMEM] * (2 + nx),
         out_specs=VMEM,
         compiler_params=PARAMS,
         name="propagate",
-    )(whole, start, *constants)
+    )(turn, jnp.asarray(tables()), start, *blocks)
 
     block = lax.all_to_all(image.reshape(K, 2, K), "beam", 0, 0).reshape(2 * beams, K)
     parts = pl.pallas_call(
@@ -274,12 +313,10 @@
         name="probe",
     )(block, coef_high, coef_low)
 
-    def swap(value, bit):
-        return lax.ppermute(value, "slab", [(i, i ^ bit) for i in range(configs)])
-
-    got = swap(jnp.concatenate([parts[1], parts[3]], axis=0), 1)
-    other = parts[2] + got[quarter:]
-    return parts[0] + got[:quarter] + swap(other, 2)
+    total = parts[0]
+    for bit in (2, 3, 1):
+        total = total + lax.ppermute(parts[bit], "slab", [(i, i ^ bit) for i in range(configs)])
+    return total
 
 
 def solution(mesh):

time: 98.9 us -> 91.9 us (0.929)
  local copies, waits for them, and re-layouts: 14.7 us -> 5.14 us
  starting transfers between devices: 30.5 us -> 37.4 us
  waiting for transfers between devices: 20.9 us -> 15.2 us
  other arithmetic: 1.5 us -> 2.98 us
    ppermute x2 -> x6, starting transfers between devices: 13.1 us -> 24 us  [the longest x3 14.6 us: per_device(): lax.ppermute(parts[bit], 'slab', [(i, i ^ bit) for i in range(configs)])]
    all_to_all x2 -> x1, waiting for transfers between devices: 17.7 us -> 8.33 us  [per_device(): lax.all_to_all(jnp.broadcast_to(piece[None], (run, *piece.shape)), 'beam'...]
    unnamed x38 -> x6, local copies, waits for them, and re-layouts: 12.1 us -> 2.81 us
    all_to_all x2 -> x1, starting transfers between devices: 17.5 us -> 13.5 us  [per_device(): lax.all_to_all(jnp.broadcast_to(piece[None], (run, *piece.shape)), 'beam'...]
    ppermute x2 -> x6, waiting for transfers between devices: 3.12 us -> 6.85 us  [the longest x3 3.67 us: fetch(): lax.ppermute(part, 'beam', [((x + k) % nx * run + i, x * run + i) for x i...]
    another operation x3, other arithmetic: 0.1 us -> 1.51 us  [per_device(): jnp.stack([jnp.cos(DEFOCUS_RATE * square) * amount, -jnp.sin(DEFOCUS_RATE...]
  transfers between devices with their start and end apart: 4 -> 7, of which waited for: 4 -> 4; matrix products, arithmetic and copies ran while one was open for 1% -> 3% of each run, Pallas kernels for 2% -> 2%
where the time goes in v2:
time: 91.9 us; the launch traced here: 91.2 us
  starting transfers between devices  37.4 us (41%)
  blocking collectives  20.8 us (23%)
  waiting for transfers between devices  15.2 us (17%)
  Pallas kernels  9.48 us (10%)
  local copies, waits for them, and re-layouts  5.14 us (6%)
  other arithmetic  2.98 us (3%)
    all_to_all x1, blocking collectives, per_device(): lax.all_to_all(image.reshape(K, 2, K), 'beam', 0, 0).reshape(2 * beams, K)  20.8 us
    ppermute x3, starting transfers between devices, per_device(): lax.ppermute(parts[bit], 'slab', [(i, i ^ bit) for i in range(configs)])  14.6 us
    all_to_all x1, starting transfers between devices, per_device(): lax.all_to_all(jnp.broadcast_to(piece[None], (run, *piece.shape)), 'beam'...  13.5 us
    ppermute x3, starting transfers between devices, fetch(): lax.ppermute(part, 'beam', [((x + k) % nx * run + i, x * run + i) for x i...  9.33 us
    all_to_all x1, waiting for transfers between devices, per_device(): lax.all_to_all(jnp.broadcast_to(piece[None], (run, *piece.shape)), 'beam'...  8.33 us
    pallas_call x1, Pallas kernels, per_device(): pl.pallas_call(propagate_kernel, out_shape=jax.ShapeDtypeStruct((2 * K, K...  7.29 us
    ppermute x3, waiting for transfers between devices, fetch(): lax.ppermute(part, 'beam', [((x + k) % nx * run + i, x * run + i) for x i...  3.67 us
    ppermute x3, waiting for transfers between devices, per_device(): lax.ppermute(parts[bit], 'slab', [(i, i ^ bit) for i in range(configs)])  3.18 us
  transfers between devices with their start and end apart: 7, of which 4 were waited for; matrix products, arithmetic and copies ran while one was open for 3% of the time, Pallas kernels for 2%

profile of v2, /device:TPU:1, one launch (start us, length us, event | category | flops | bytes accessed | tf_op | source)
XLA Modules:
  0.0 91.2 jit_solution(3324968050838917650)
XLA Ops:
  0.0 0.7 reduce.1
  0.7 0.7 broadcast_in_dim.9
  1.5 13.5 %all-to-all-start = ((f32[32,12,128]{2,1,0:T(8,128)}), f32[32,12,128]{2,1,0:T(8,128)S(1)}, u32[]{:S(2)}, u32[]{:S(2)}) async-start(f32[32,12,128]{2,1,0:T(8,128)} %broadcast_in_dim.9), calls=%async_computation | async-start | bytes 524288 | tf_op jit(solution)/shard_map/all_to_all | solution.py:265
  15.0 0.6 gather_fusion
  15.7 0.9 dynamic-slice_reduce_fusion
  16.6 0.8 fusion.2
  17.4 0.7 fusion.1
  18.1 8.3 %all-to-all-done = f32[32,12,128]{2,1,0:T(8,128)S(1)} async-done(((f32[32,12,128]{2,1,0:T(8,128)}), f32[32,12,128]{2,1,0:T(8,128)S(1)}, u32[]{:S(2)}, u32[]{:S(2)}) %all-to-all-start) | async-done | bytes 196640 | tf_op jit(solution)/shard_map/all_to_all | solution.py:265
  26.4 4.4 %collective-permute-start = (f32[384,128]{1,0:T(8,128)S(1)}, f32[384,128]{1,0:T(8,128)S(1)}, u32[]{:S(2)}, u32[]{:S(2)}) collective-permute-start(f32[384,128]{1,0:T(8,128)S(1)} %reshape.44.refs_0_), channel_id=1, source_target_pairs={{128,0},{132,4},{136,8},{140,12},{144,16},{148,20},{152,24},{156,2... | collective-permute-start | bytes 589832 | tf_op jit(solution)/shard_map/ppermute | solution.py:270
  30.8 2.4 %collective-permute-start.1 = (f32[384,128]{1,0:T(8,128)S(1)}, f32[384,128]{1,0:T(8,128)S(1)}, u32[]{:S(2)}, u32[]{:S(2)}) collective-permute-start(f32[384,128]{1,0:T(8,128)S(1)} %reshape.44.refs_0_), channel_id=1, source_target_pairs={{256,0},{260,4},{264,8},{268,12},{272,16},{276,20},{280,24},{284,2... | collective-permute-start | bytes 589832 | tf_op jit(solution)/shard_map/ppermute | solution.py:270
  33.3 2.5 %collective-permute-start.2 = (f32[384,128]{1,0:T(8,128)S(1)}, f32[384,128]{1,0:T(8,128)S(1)}, u32[]{:S(2)}, u32[]{:S(2)}) collective-permute-start(f32[384,128]{1,0:T(8,128)S(1)} %reshape.44.refs_0_), channel_id=1, source_target_pairs={{384,0},{388,4},{392,8},{396,12},{400,16},{404,20},{408,24},{412,2... | collective-permute-start | bytes 589832 | tf_op jit(solution)/shard_map/ppermute | solution.py:270
  35.9 0.7 copy-done.2
  36.6 1.6 %prepare.1 = (f32[512,256]{1,0:T(8,128)S(1)}, bf16[1024,256]{1,0:T(8,128)(2,1)S(1)}, bf16[1024,256]{1,0:T(8,128)(2,1)S(1)}) custom-call(s32[3]{0:T(128)S(1)} %pad_add_fusion.tilt_ref, s32[512,2]{1,0:T(8,128)S(1)} %bitcast.21, s32[2,128]{1,0:T(2,128)S(1)} %bitcast.24, f32[2,128]{1,0:T(2,128)S(1)} %pad_maximum_fusion.weight_ref), custom_call_target="tpu_custom_call" | custom-call | tf_op jit(solution)/shard_map/prepare/pallas_call | solution.py:284
  38.2 0.6 collective-permute-done.1.refs_2_
  38.8 3.1 %collective-permute-done.2.refs_3_ = f32[384,128]{1,0:T(8,128)S(1)} collective-permute-done((f32[384,128]{1,0:T(8,128)S(1)}, f32[384,128]{1,0:T(8,128)S(1)}, u32[]{:S(2)}, u32[]{:S(2)}) %collective-permute-start.2) | collective-permute-done | bytes 196640 | tf_op jit(solution)/shard_map/ppermute | solution.py:270
  41.9 2.1 %copy-done.1 = bf16[3904,512]{1,0:T(8,128)(2,1)S(1)} copy-done((bf16[3904,512]{1,0:T(8,128)(2,1)S(1)}, bf16[3904,512]{1,0:T(8,128)(2,1)}, u32[]{:S(2)}) %copy-start.1) | copy-done | bytes 3997720
  44.0 7.3 %propagate.1 = f32[256,128]{1,0:T(8,128)S(1)} custom-call(s32[1]{0:T(128)} %bitcast.turn_ref, bf16[3904,512]{1,0:T(8,128)(2,1)S(1)} %copy-done.1, f32[512,256]{1,0:T(8,128)S(1)} %get-tuple-element.12.start_ref, f32[384,128]{1,0:T(8,128)S(1)} %reshape.44.refs_0_, f32[384,128]{1,0:T(8,128)S(1)} %collective-permute-done.refs_1_, ...), custom_call_target="tpu_custom_call" | custom-call | tf_op jit(solution)/shard_map/propagate/pallas_call | solution.py:297
  51.3 20.8 %all_to_all.10 = f32[128,2,128]{2,1,0:T(2,128)S(1)} all-to-all(f32[128,2,128]{2,1,0:T(2,128)S(1)} %bitcast.23), channel_id=1, replica_groups=mesh['beam'=128,'slab'=4] {'beam'}, dimensions={0} | all-to-all | bytes 262144 | tf_op jit(solution)/shard_map/all_to_all | solution.py:306
  72.1 0.6 probe.1
  72.7 7.9 %collective-permute-start.3 = (f32[128,128]{1,0:T(8,128)S(1)}, f32[128,128]{1,0:T(8,128)S(1)}, u32[]{:S(2)}, u32[]{:S(2)}) collective-permute-start(f32[128,128]{1,0:T(8,128)S(1)} %get-tuple-element.16), channel_id=1, source_target_pairs={{0,2},{1,3},{2,0},{3,1},{4,6},{5,7},{6,4},{7,5},{8,10},{9,11},{10,... | collective-permute-start | bytes 196616 | tf_op jit(solution)/shard_map/ppermute | solution.py:318
  80.7 4.4 %collective-permute-start.4 = (f32[128,128]{1,0:T(8,128)S(1)}, f32[128,128]{1,0:T(8,128)S(1)}, u32[]{:S(2)}, u32[]{:S(2)}) collective-permute-start(f32[128,128]{1,0:T(8,128)S(1)} %get-tuple-element.17), channel_id=1, source_target_pairs={{0,3},{1,2},{2,1},{3,0},{4,7},{5,6},{6,5},{7,4},{8,11},{9,10},{10,... | collective-permute-start | bytes 196616 | tf_op jit(solution)/shard_map/ppermute | solution.py:318
  85.0 2.3 %collective-permute-start.5 = (f32[128,128]{1,0:T(8,128)S(1)}, f32[128,128]{1,0:T(8,128)S(1)}, u32[]{:S(2)}, u32[]{:S(2)}) collective-permute-start(f32[128,128]{1,0:T(8,128)S(1)} %get-tuple-element.18), channel_id=1, source_target_pairs={{0,1},{1,0},{2,3},{3,2},{4,5},{5,4},{6,7},{7,6},{8,9},{9,8},{10,11... | collective-permute-start | bytes 196616 | tf_op jit(solution)/shard_map/ppermute | solution.py:318
  87.4 3.2 %collective-permute-done.4 = f32[128,128]{1,0:T(8,128)S(1)} collective-permute-done((f32[128,128]{1,0:T(8,128)S(1)}, f32[128,128]{1,0:T(8,128)S(1)}, u32[]{:S(2)}, u32[]{:S(2)}) %collective-permute-start.4) | collective-permute-done | bytes 65568 | tf_op jit(solution)/shard_map/ppermute | solution.py:318
  90.5 0.6 add_add_fusion
  (14 shorter events, 0.3 us)
Async XLA Ops:
  0.0 15.0 %copy-start = (s32[512,2]{0,1:T(2,128)S(1)}, s32[512,2]{0,1:T(2,128)}, u32[]{:S(2)}) copy-start(s32[512,2]{0,1:T(2,128)} %param.8) | copy-start | bytes 12292
  1.5 25.0 %all-to-all-start = ((f32[32,12,128]{2,1,0:T(8,128)}), f32[32,12,128]{2,1,0:T(8,128)S(1)}, u32[]{:S(2)}, u32[]{:S(2)}) async-start(f32[32,12,128]{2,1,0:T(8,128)} %broadcast_in_dim.9), calls=%async_computation | async-start | bytes 524288 | tf_op jit(solution)/shard_map/all_to_all | solution.py:265
  26.4 11.7 %collective-permute-start = (f32[384,128]{1,0:T(8,128)S(1)}, f32[384,128]{1,0:T(8,128)S(1)}, u32[]{:S(2)}, u32[]{:S(2)}) collective-permute-start(f32[384,128]{1,0:T(8,128)S(1)} %reshape.44.refs_0_), channel_id=1, source_target_pairs={{128,0},{132,4},{136,8},{140,12},{144,16},{148,20},{152,24},{156,2... | collective-permute-start | bytes 589832 | tf_op jit(solution)/shard_map/ppermute | solution.py:270
  30.8 7.9 %collective-permute-start.1 = (f32[384,128]{1,0:T(8,128)S(1)}, f32[384,128]{1,0:T(8,128)S(1)}, u32[]{:S(2)}, u32[]{:S(2)}) collective-permute-start(f32[384,128]{1,0:T(8,128)S(1)} %reshape.44.refs_0_), channel_id=1, source_target_pairs={{256,0},{260,4},{264,8},{268,12},{272,16},{276,20},{280,24},{284,2... | collective-permute-start | bytes 589832 | tf_op jit(solution)/shard_map/ppermute | solution.py:270
  33.3 8.6 %collective-permute-start.2 = (f32[384,128]{1,0:T(8,128)S(1)}, f32[384,128]{1,0:T(8,128)S(1)}, u32[]{:S(2)}, u32[]{:S(2)}) collective-permute-start(f32[384,128]{1,0:T(8,128)S(1)} %reshape.44.refs_0_), channel_id=1, source_target_pairs={{384,0},{388,4},{392,8},{396,12},{400,16},{404,20},{408,24},{412,2... | collective-permute-start | bytes 589832 | tf_op jit(solution)/shard_map/ppermute | solution.py:270
  35.9 0.7 copy-start.2
  41.9 2.1 %copy-start.1 = (bf16[3904,512]{1,0:T(8,128)(2,1)S(1)}, bf16[3904,512]{1,0:T(8,128)(2,1)}, u32[]{:S(2)}) copy-start(bf16[3904,512]{1,0:T(8,128)(2,1)} %constant.41.clone.table_ref) | copy-start | bytes 11993092
  72.7 14.7 %collective-permute-start.3 = (f32[128,128]{1,0:T(8,128)S(1)}, f32[128,128]{1,0:T(8,128)S(1)}, u32[]{:S(2)}, u32[]{:S(2)}) collective-permute-start(f32[128,128]{1,0:T(8,128)S(1)} %get-tuple-element.16), channel_id=1, source_target_pairs={{0,2},{1,3},{2,0},{3,1},{4,6},{5,7},{6,4},{7,5},{8,10},{9,11},{10,... | collective-permute-start | bytes 196616 | tf_op jit(solution)/shard_map/ppermute | solution.py:318
  80.7 9.9 %collective-permute-start.4 = (f32[128,128]{1,0:T(8,128)S(1)}, f32[128,128]{1,0:T(8,128)S(1)}, u32[]{:S(2)}, u32[]{:S(2)}) collective-permute-start(f32[128,128]{1,0:T(8,128)S(1)} %get-tuple-element.17), channel_id=1, source_target_pairs={{0,3},{1,2},{2,1},{3,0},{4,7},{5,6},{6,5},{7,4},{8,11},{9,10},{10,... | collective-permute-start | bytes 196616 | tf_op jit(solution)/shard_map/ppermute | solution.py:318
  85.0 5.5 %collective-permute-start.5 = (f32[128,128]{1,0:T(8,128)S(1)}, f32[128,128]{1,0:T(8,128)S(1)}, u32[]{:S(2)}, u32[]{:S(2)}) collective-permute-start(f32[128,128]{1,0:T(8,128)S(1)} %get-tuple-element.18), channel_id=1, source_target_pairs={{0,1},{1,0},{2,3},{3,2},{4,5},{5,4},{6,7},{7,6},{8,9},{9,8},{10,11... | collective-permute-start | bytes 196616 | tf_op jit(solution)/shard_map/ppermute | solution.py:318

commit v3 on v2

--- a/solution.py
+++ b/solution.py
@@ -150,7 +150,7 @@
     rows = lax.broadcasted_iota(jnp.int32, (G, G), 0)
     x = jnp.where(rows < G // 2, 2 * rows, 2 * rows - (G - 1))
     y = lax.broadcasted_iota(jnp.int32, (G, G), 1)
-    sine, cosine = circle(tilt_ref[0] * (x + tilt_ref[2]) + tilt_ref[1] * y, G)
+    sine, cosine = circle(tilt_ref[0] * x + tilt_ref[1] * y, G)
     start_ref[:G, :] = cosine
     start_ref[G:, :] = sine
     probes = places_ref.shape[0]
@@ -171,27 +171,24 @@
         low_ref[rows : rows + probes, columns : columns + beams] = low
 
 
-def transmission(potential_refs, layer):
-    stride = 4 * SLICES
-
-    def rows(parity):
-        return jnp.concatenate(
-            [
-                jnp.concatenate(
-                    [
-                        ref[pl.ds(4 * layer + 2 * parity + half, ref.shape[0] // stride, stride), :]
-                        for half in range(2)
-                    ],
-                    axis=1,
-                )
-                for ref in potential_refs
-            ],
-            axis=0,
-        )
-
-    sine, cosine = sine_cosine(jnp.concatenate([rows(0), rows(1)], axis=0) - 1.5)
+def screened(wave, potential_ref, layer):
+    count = G // 2
+    stride = potential_ref.shape[0] // count
+    potential = jnp.concatenate(
+        [
+            jnp.concatenate(
+                [potential_ref[pl.ds(4 * layer + 2 * parity + half, count, stride), :] for half in range(2)],
+                axis=1,
+            )
+            for parity in range(2)
+        ],
+        axis=0,
+    )
+    sine, cosine = sine_cosine(potential - 1.5)
     cos_mid, sin_mid = math.cos(1.5), math.sin(1.5)
-    return cosine * cos_mid - sine * sin_mid, sine * cos_mid + cosine * sin_mid
+    cosine, sine = cosine * cos_mid - sine * sin_mid, sine * cos_mid + cosine * sin_mid
+    real, imag = wave[:G], wave[G:]
+    return jnp.concatenate([real * cosine - imag * sine, real * sine + imag * cosine], axis=0)
 
 
 def masked(real, imag, first, limit_of):
@@ -204,44 +201,42 @@
     return jnp.concatenate([jnp.where(keep, real, 0.0), jnp.where(keep, imag, 0.0)], axis=0)
 
 
-def propagate_kernel(turn_ref, table_ref, start_ref, *refs):
-    potential_refs, out_ref = refs[:-1], refs[-1]
-    blocks = len(potential_refs)
+def step(field, table):
+    field = from_left(table(0), field)
+    field = masked(*from_right(field, table(1)), REACH, LIMIT)
+    real, imag = from_right(field, table(2))
+    return from_left(table(3), jnp.concatenate([real, imag], axis=0))
+
+
+def propagate_kernel(table_ref, wave_ref, potential_ref, out_ref):
     table = functools.partial(table_of, table_ref)
-    real, imag = start_ref[:G, :], start_ref[G:, :]
-    for layer in range(SLICES):
-        cosine, sine = transmission(potential_refs, layer)
-        real, imag = real * cosine - imag * sine, real * sine + imag * cosine
-        field = jnp.concatenate([real, imag], axis=0)
-        if layer < SLICES - 1:
-            field = from_left(table(0), field)
-            field = masked(*from_right(field, table(1)), REACH, LIMIT)
-            real, imag = from_right(field, table(2))
-            field = from_left(table(3), jnp.concatenate([real, imag], axis=0))
-            real, imag = field[:G], field[G:]
-        else:
-            field = from_left(table(4), field)
-            field = masked(*from_right(field, table(5)), 0, LIMIT)
-            real, imag = from_right(field, table(6))
-            image = from_left(table(7), jnp.concatenate([real, imag], axis=0))
-    rows = image.shape[0] // blocks
-    for k in range(blocks):
-        place = lax.rem(turn_ref[0] + k, blocks) * rows
-        out_ref[pl.ds(pl.multiple_of(place, rows), rows), :] = image[k * rows : (k + 1) * rows]
-
-
-def probe_kernel(block_ref, high_ref, low_ref, *out_refs):
-    beams = block_ref.shape[0] // 2
+    wave = wave_ref[...]
+    for layer in range(SLICES - 1):
+        wave = step(screened(wave, potential_ref, layer), table)
+    field = from_left(table(4), screened(wave, potential_ref, SLICES - 1))
+    field = masked(*from_right(field, table(5)), 0, LIMIT)
+    real, imag = from_right(field, table(6))
+    out_ref[...] = from_left(table(7), jnp.concatenate([real, imag], axis=0))
+
+
+def probe_kernel(configs, block_ref, high_ref, low_ref, mine_ref, other_ref):
+    here = block_ref.shape[0] // (2 * K)
     field = jnp.concatenate(
-        [block_ref[pl.ds(part, beams, 2), :] for part in range(2)], axis=0
+        [
+            jnp.concatenate(
+                [block_ref[pl.ds(2 * K * config + part, K, 2), :] for part in range(2)], axis=0
+            )
+            for config in range(here)
+        ],
+        axis=1,
     )
     waves = from_left((high_ref[...], low_ref[...]), field)
     probes = waves.shape[0] // 2
     real, imag = waves[:probes], waves[probes:]
-    total = (real * real + imag * imag) * (1.0 / len(out_refs))
-    quarter = probes // len(out_refs)
-    for i, out_ref in enumerate(out_refs):
-        out_ref[...] = total[i * quarter : (i + 1) * quarter]
+    power = real * real + imag * imag
+    total = sum(power[:, K * config : K * config + K] for config in range(here)) * (1.0 / configs)
+    mine_ref[...] = total[: probes // 2]
+    other_ref[...] = total[probes // 2 :]
 
 
 VMEM = pl.BlockSpec(memory_space=pltpu.VMEM)
@@ -249,47 +244,38 @@
 PARAMS = pltpu.CompilerParams(vmem_limit_bytes=24 * 1024 * 1024)
 
 
-def per_device(sizes, potential, tilts, aperture, positions):
-    nx, ny, nz = sizes
-    devices = lax.axis_size("beam")
-    configs = lax.axis_size("slab")
+def per_device(potential, tilts, aperture, positions):
+    nx, near = lax.axis_size("x"), lax.axis_size("y") * lax.axis_size("z")
+    pairs, cores = lax.axis_size("far"), lax.axis_size("core")
+    configs = pairs * cores
     beams = tilts.shape[0]
     probes = positions.shape[0]
     quarter = probes // configs
-    own = lax.axis_index("beam")
-    slab = lax.axis_index("slab")
-
-    piece = potential.reshape(SLICES * G * G // devices // K, K)
-    run = ny * nz
-    near = [[x * run + i for i in range(run)] for x in range(nx)]
-    part = lax.all_to_all(
-        jnp.broadcast_to(piece[None], (run, *piece.shape)), "beam", 0, 0, axis_index_groups=near
-    ).reshape(run * piece.shape[0], K)
-
-    def fetch(k):
-        return lax.ppermute(
-            part, "beam", [((x + k) % nx * run + i, x * run + i) for x in range(nx) for i in range(run)]
-        )
-
-    blocks = [part] + [fetch(k) for k in range(1, nx)]
-
-    order = jnp.bitwise_xor(slab, jnp.arange(configs, dtype=jnp.int32))
-    places = positions.reshape(configs, quarter, 2)[order].reshape(probes, 2)
+    own = lax.axis_index(("x", "y", "z"))
+    slab = lax.axis_index(("far", "core"))
+
+    def gather(piece, count, axes):
+        copies = jnp.broadcast_to(piece[None], (count, *piece.shape))
+        return lax.all_to_all(copies, axes, 0, 0, tiled=True).reshape(count * piece.shape[0], K)
+
+    whole = potential.reshape(potential.size // K, K)
+    whole = gather(gather(whole, near, ("y", "z")), nx, "x")
+
+    places = positions.reshape(configs, quarter, 2)
+    places = jnp.concatenate([places[slab], places[slab ^ 1]], axis=0)
     square = (tilts[:, 0] ** 2 + tilts[:, 1] ** 2).astype(F32)
     amount = aperture.astype(F32) * (1.0 / math.sqrt(beams))
     weight = jnp.stack([jnp.cos(DEFOCUS_RATE * square) * amount, -jnp.sin(DEFOCUS_RATE * square) * amount])
-    place = own // run
-    turn = place.reshape(1)
-    tilt = jnp.concatenate([lax.dynamic_index_in_dim(tilts, own, 0, keepdims=False), turn * (G // nx)])
+    tilt = lax.dynamic_index_in_dim(tilts, own, 0, keepdims=False)
     start, coef_high, coef_low = pl.pallas_call(
         prepare_kernel,
         out_shape=(
             jax.ShapeDtypeStruct((2 * G, G), F32),
-            jax.ShapeDtypeStruct((2 * probes, 2 * beams), BF16),
-            jax.ShapeDtypeStruct((2 * probes, 2 * beams), BF16),
+            jax.ShapeDtypeStruct((4 * quarter, 2 * beams), BF16),
+            jax.ShapeDtypeStruct((4 * quarter, 2 * beams), BF16),
         ),
-        in_specs=[SMEM, VMEM, VMEM, VMEM],
-        out_specs=(VMEM, VMEM, VMEM),
+        in_specs=[SMEM] + [VMEM] * 3,
+        out_specs=(VMEM,) * 3,
         compiler_params=PARAMS,
         name="prepare",
     )(tilt, places, tilts.T, weight)
@@ -297,36 +283,32 @@
     image = pl.pallas_call(
         propagate_kernel,
         out_shape=jax.ShapeDtypeStruct((2 * K, K), F32),
-        in_specs=[SMEM] + [VMEM] * (2 + nx),
+        in_specs=[VMEM] * 3,
         out_specs=VMEM,
         compiler_params=PARAMS,
         name="propagate",
-    )(turn, jnp.asarray(tables()), start, *blocks)
-
-    block = lax.all_to_all(image.reshape(K, 2, K), "beam", 0, 0).reshape(2 * beams, K)
-    parts = pl.pallas_call(
-        probe_kernel,
-        out_shape=[jax.ShapeDtypeStruct((quarter, K), F32)] * configs,
+    )(jnp.asarray(tables()), start, whole)
+
+    rows = jnp.broadcast_to(image.reshape(1, K, 2, K), (pairs, K, 2, K)).reshape(pairs * K, 2, K)
+    block = lax.all_to_all(rows, ("far", "x", "y", "z"), 0, 0, tiled=True).reshape(2 * pairs * beams, K)
+    mine, other = pl.pallas_call(
+        functools.partial(probe_kernel, configs),
+        out_shape=[jax.ShapeDtypeStruct((quarter, K), F32)] * cores,
         in_specs=[VMEM] * 3,
-        out_specs=[VMEM] * configs,
+        out_specs=[VMEM] * cores,
         compiler_params=PARAMS,
         name="probe",
     )(block, coef_high, coef_low)
-
-    total = parts[0]
-    for bit in (2, 3, 1):
-        total = total + lax.ppermute(parts[bit], "slab", [(i, i ^ bit) for i in range(configs)])
-    return total
+    return mine + lax.ppermute(other, "core", [(0, 1), (1, 0)])
 
 
 def solution(mesh):
-    def step(*args):
-        return per_device((4, 8, 4), *args)
-
+    fine = jax.sharding.Mesh(mesh.devices.reshape(4, 8, 4, 2, 2), ("x", "y", "z", "far", "core"))
+    beam, slab = ("x", "y", "z"), ("far", "core")
     return jax.shard_map(
-        step,
-        mesh=mesh,
-        in_specs=(P("slab", None, "beam"), P(), P(), P()),
-        out_specs=P("slab", "beam"),
+        per_device,
+        mesh=fine,
+        in_specs=(P(slab, None, beam), P(), P(), P()),
+        out_specs=P(slab, beam),
         check_vma=False,
     )

time: 91.9 us -> 87.5 us (0.952)
  starting transfers between devices: 37.4 us -> 23.8 us
  blocking collectives: 20.8 us -> 29 us
  waiting for transfers between devices: 15.2 us -> 18.8 us
  other arithmetic: 2.98 us -> 1.48 us
    ppermute x6 -> x1, starting transfers between devices: 24 us -> 6.33 us  [per_device(): return mine + lax.ppermute(other, 'core', [(0, 1), (1, 0)])]
    all_to_all x1 -> x2, waiting for transfers between devices: 8.33 us -> 18 us  [gather(): lax.all_to_all(copies, axes, 0, 0, tiled=True)]
    all_to_all x1, blocking collectives: 20.8 us -> 29 us  [per_device(): lax.all_to_all(rows, ('far', 'x', 'y', 'z'), 0, 0, tiled=True)]
    ppermute x6 -> x1, waiting for transfers between devices: 6.85 us -> 0.88 us  [per_device(): return mine + lax.ppermute(other, 'core', [(0, 1), (1, 0)])]
    all_to_all x1 -> x2, starting transfers between devices: 13.5 us -> 17.5 us  [gather(): lax.all_to_all(copies, axes, 0, 0, tiled=True)]
    another operation x3, other arithmetic: 1.51 us -> 0.1 us  [per_device(): jnp.stack([jnp.cos(DEFOCUS_RATE * square) * amount, -jnp.sin(DEFOCUS_RATE...]
    broadcast_in_dim x2 -> x5, local copies, waits for them, and re-layouts: 0.73 us -> 1.77 us  [the longest x4 1.7 us: gather(): copies = jnp.broadcast_to(piece[None], (count, *piece.shape))]
  transfers between devices with their start and end apart: 7 -> 3, of which waited for: 4 -> 3; matrix products, arithmetic and copies ran while one was open for 3% -> 1% of each run, Pallas kernels for 2% -> 2%
where the time goes in v3:
time: 87.5 us; the launch traced here: 87.1 us
  blocking collectives  29 us (33%)
  starting transfers between devices  23.8 us (27%)
  waiting for transfers between devices  18.8 us (21%)
  Pallas kernels  8.95 us (10%)
  local copies, waits for them, and re-layouts  4.93 us (6%)
  other arithmetic  1.48 us (2%)
    all_to_all x1, blocking collectives, per_device(): lax.all_to_all(rows, ('far', 'x', 'y', 'z'), 0, 0, tiled=True)  29 us
    all_to_all x2, waiting for transfers between devices, gather(): lax.all_to_all(copies, axes, 0, 0, tiled=True)  18 us
    all_to_all x2, starting transfers between devices, gather(): lax.all_to_all(copies, axes, 0, 0, tiled=True)  17.5 us
    pallas_call x1, Pallas kernels, per_device(): pl.pallas_call(propagate_kernel, out_shape=jax.ShapeDtypeStruct((2 * K, K...  7.23 us
    ppermute x1, starting transfers between devices, per_device(): return mine + lax.ppermute(other, 'core', [(0, 1), (1, 0)])  6.33 us
    unnamed x6, local copies, waits for them, and re-layouts  2.14 us
  transfers between devices with their start and end apart: 3, of which 3 were waited for; matrix products, arithmetic and copies ran while one was open for 1% of the time, Pallas kernels for 2%

profile of v3, /device:TPU:1, one launch (start us, length us, event | category | flops | bytes accessed | tf_op | source)
XLA Modules:
  0.0 87.1 jit_solution(10959923335428860326)
XLA Ops:
  0.0 0.0 copy-start.1
  0.0 0.0 copy-start.2
  0.0 0.7 reduce.1
  0.8 0.7 broadcast_in_dim.22
  1.5 13.5 %all-to-all-start = ((f32[32,12,128]{2,1,0:T(8,128)}), f32[32,12,128]{2,1,0:T(8,128)S(1)}, u32[]{:S(2)}, u32[]{:S(2)}) async-start(f32[32,12,128]{2,1,0:T(8,128)} %broadcast_in_dim.22), calls=%async_computation | async-start | bytes 524288 | tf_op jit(solution)/shard_map/all_to_all | solution.py:259
  15.0 0.7 dynamic-slice_bitcast_fusion.1
  15.7 10.8 %all-to-all-done = f32[32,12,128]{2,1,0:T(8,128)S(1)} async-done(((f32[32,12,128]{2,1,0:T(8,128)}), f32[32,12,128]{2,1,0:T(8,128)S(1)}, u32[]{:S(2)}, u32[]{:S(2)}) %all-to-all-start) | async-done | bytes 196640 | tf_op jit(solution)/shard_map/all_to_all | solution.py:259
  26.5 0.9 %broadcast_in_dim.24 = f32[4,384,128]{2,1,0:T(8,128)} broadcast(f32[384,128]{1,0:T(8,128)S(1)} %broadcast_in_dim.23), dimensions={1,2} | broadcast | bytes 983040 | tf_op jit(solution)/shard_map/broadcast_in_dim | solution.py:258
  27.4 4.0 %all-to-all-start.1 = ((f32[4,384,128]{2,1,0:T(8,128)}), f32[4,384,128]{2,1,0:T(8,128)S(1)}, u32[]{:S(2)}, u32[]{:S(2)}) async-start(f32[4,384,128]{2,1,0:T(8,128)} %broadcast_in_dim.24), calls=%async_computation.1 | async-start | bytes 1572864 | tf_op jit(solution)/shard_map/all_to_all | solution.py:259
  31.4 0.1 copy.12.places_ref
  31.6 0.0 copy-done.1
  31.6 0.2 dynamic-slice_reduce_fusion.tilt_ref
  31.8 0.0 copy-done.2
  31.9 1.3 %prepare.1 = (f32[512,256]{1,0:T(8,128)S(1)}, bf16[512,256]{1,0:T(8,128)(2,1)S(1)}, bf16[512,256]{1,0:T(8,128)(2,1)S(1)}) custom-call(s32[2]{0:T(128)S(1)} %dynamic-slice_reduce_fusion.tilt_ref, s32[256,2]{1,0:T(8,128)S(1)} %copy.12.places_ref, s32[2,128]{1,0:T(2,128)S(1)} %bitcast.25, f32[2,128]{1,0:T(2,128)S(1)} %pad_maximum_fusion.weight_ref), custom_call_target="tpu_custom_call" | custom-call | tf_op jit(solution)/shard_map/prepare/pallas_call | solution.py:270
  33.2 7.2 %all-to-all-done.1 = f32[4,384,128]{2,1,0:T(8,128)S(1)} async-done(((f32[4,384,128]{2,1,0:T(8,128)}), f32[4,384,128]{2,1,0:T(8,128)S(1)}, u32[]{:S(2)}, u32[]{:S(2)}) %all-to-all-start.1) | async-done | bytes 786464 | tf_op jit(solution)/shard_map/all_to_all | solution.py:259
  40.4 0.0 copy-start
  40.4 2.1 %copy-done = bf16[3904,512]{1,0:T(8,128)(2,1)S(1)} copy-done((bf16[3904,512]{1,0:T(8,128)(2,1)S(1)}, bf16[3904,512]{1,0:T(8,128)(2,1)}, u32[]{:S(2)}) %copy-start) | copy-done | bytes 3997720
  42.6 7.2 %propagate.1 = f32[256,128]{1,0:T(8,128)S(1)} custom-call(bf16[3904,512]{1,0:T(8,128)(2,1)S(1)} %copy-done, f32[512,256]{1,0:T(8,128)S(1)} %get-tuple-element.10.wave_ref, f32[1536,128]{1,0:T(8,128)S(1)} %bitcast.22), custom_call_target="tpu_custom_call" | custom-call | tf_op jit(solution)/shard_map/propagate/pallas_call | solution.py:283
  49.8 0.1 broadcast_in_dim.26
  49.9 29.0 %all_to_all.15 = f32[256,2,128]{2,1,0:T(2,128)S(1)} all-to-all(f32[256,2,128]{2,1,0:T(2,128)S(1)} %bitcast.26), channel_id=1, replica_groups=mesh['x'=4,'y'=8,'z'=4,'far'=2,'core'=2] {'far','x','y','z'}, dimensions={0} | all-to-all | bytes 524288 | tf_op jit(solution)/shard_map/all_to_all | solution.py:293
  78.9 0.4 probe.1
  79.2 6.3 %collective-permute-start = (f32[128,128]{1,0:T(8,128)S(1)}, f32[128,128]{1,0:T(8,128)S(1)}, u32[]{:S(2)}, u32[]{:S(2)}) collective-permute-start(f32[128,128]{1,0:T(8,128)S(1)} %get-tuple-element.14), channel_id=1, source_target_pairs={{0,1},{1,0},{2,3},{3,2},{4,5},{5,4},{6,7},{7,6},{8,9},{9,8},{10,11... | collective-permute-start | bytes 196616 | tf_op jit(solution)/shard_map/ppermute | solution.py:302
  85.6 0.9 %collective-permute-done = f32[128,128]{1,0:T(8,128)S(1)} collective-permute-done((f32[128,128]{1,0:T(8,128)S(1)}, f32[128,128]{1,0:T(8,128)S(1)}, u32[]{:S(2)}, u32[]{:S(2)}) %collective-permute-start) | collective-permute-done | bytes 65568 | tf_op jit(solution)/shard_map/ppermute | solution.py:302
  86.5 0.6 add.33
  (6 shorter events, 0.1 us)
Async XLA Ops:
  0.0 31.6 %copy-start.1 = (s32[128,2]{0,1:T(2,128)S(1)}, s32[128,2]{0,1:T(2,128)}, u32[]{:S(2)}) copy-start(s32[128,2]{0,1:T(2,128)} %param.6) | copy-start | bytes 3076
  0.0 31.8 %copy-start.2 = (s32[128]{0:T(128)S(1)}, s32[128]{0:T(128)}, u32[]{:S(2)}) copy-start(s32[128]{0:T(128)} %param.7) | copy-start | bytes 1540
  1.5 25.0 %all-to-all-start = ((f32[32,12,128]{2,1,0:T(8,128)}), f32[32,12,128]{2,1,0:T(8,128)S(1)}, u32[]{:S(2)}, u32[]{:S(2)}) async-start(f32[32,12,128]{2,1,0:T(8,128)} %broadcast_in_dim.22), calls=%async_computation | async-start | bytes 524288 | tf_op jit(solution)/shard_map/all_to_all | solution.py:259
  27.4 13.0 %all-to-all-start.1 = ((f32[4,384,128]{2,1,0:T(8,128)}), f32[4,384,128]{2,1,0:T(8,128)S(1)}, u32[]{:S(2)}, u32[]{:S(2)}) async-start(f32[4,384,128]{2,1,0:T(8,128)} %broadcast_in_dim.24), calls=%async_computation.1 | async-start | bytes 1572864 | tf_op jit(solution)/shard_map/all_to_all | solution.py:259
  40.4 2.1 %copy-start = (bf16[3904,512]{1,0:T(8,128)(2,1)S(1)}, bf16[3904,512]{1,0:T(8,128)(2,1)}, u32[]{:S(2)}) copy-start(bf16[3904,512]{1,0:T(8,128)(2,1)} %constant.41.clone.table_ref) | copy-start | bytes 11993092
  79.2 7.2 %collective-permute-start = (f32[128,128]{1,0:T(8,128)S(1)}, f32[128,128]{1,0:T(8,128)S(1)}, u32[]{:S(2)}, u32[]{:S(2)}) collective-permute-start(f32[128,128]{1,0:T(8,128)S(1)} %get-tuple-element.14), channel_id=1, source_target_pairs={{0,1},{1,0},{2,3},{3,2},{4,5},{5,4},{6,7},{7,6},{8,9},{9,8},{10,11... | collective-permute-start | bytes 196616 | tf_op jit(solution)/shard_map/ppermute | solution.py:302

commit v4 on v0

v4 whole, which is shorter than its diff:
```python
import functools
import math

import jax
import jax.numpy as jnp
from jax import lax
from jax.experimental import pallas as pl
from jax.experimental.pallas import tpu as pltpu
from jax.sharding import PartitionSpec as P

G = 256
K = 128
SLICES = 3
LIMIT = (G // 3) ** 2
REACH = G // 3
ROWS = 176
PIECE = SLICES * 4

FRESNEL_RATE = 0.00019
DEFOCUS_RATE = 0.01

F32 = jnp.float32
BF16 = jnp.bfloat16


def split(value):
    high = value.astype(BF16)
    return high, (value - high.astype(F32)).astype(BF16)


def sine_of(t):
    s = t * t
    sine = jnp.full_like(t, -2.5052108e-8)
    for term in (2.7557319e-6, -1.9841270e-4, 8.3333333e-3, -1.6666667e-1, 1.0):
        sine = sine * s + term
    return sine * t


def cosine_of(t):
    s = t * t
    cosine = jnp.full_like(t, 2.0876757e-9)
    for term in (-2.7557319e-7, 2.4801587e-5, -1.3888889e-3, 4.1666667e-2, -0.5, 1.0):
        cosine = cosine * s + term
    return cosine


def half_angle(steps, length):
    near = ((steps + length // 2) & (length - 1)) - length // 2
    return near.astype(F32) * (math.pi / length)


def cosine_step(steps, length):
    sine = sine_of(half_angle(steps, length))
    return 1.0 - 2.0 * sine * sine


def circle(steps, length):
    half = half_angle(steps, length)
    sine = sine_of(half)
    return 2.0 * sine * cosine_of(half), 1.0 - 2.0 * sine * sine


def iota(shape, axis):
    return lax.broadcasted_iota(jnp.int32, shape, axis)


def natural(place):
    return place & (G // 2 - 1)


def mixed(place):
    n = 2 * natural(place)
    return jnp.where(n < G // 2, n, n - (G // 2 - 1))


def folded(place, order):
    factor = jnp.where(place == G // 2, G // 2, order(place))
    return factor, jnp.where(place > G // 2, -(G // 4), 0)


def position(place, order):
    n = order(place)
    return jnp.where(place < G // 2, n, jnp.where(place == G // 2, G // 2, -n))


def signed(index, length):
    return jnp.where(index < length // 2, index, index - length)


def forward_table(shape, frequency, order, axis):
    factor, offset = folded(iota(shape, axis), order)
    return cosine_step(frequency(iota(shape, 1 - axis)) * factor + offset, G)


def fresnel(shape, frequency_u, frequency_v):
    u, v = frequency_u(iota(shape, 0)), frequency_v(iota(shape, 1))
    square = u * u + v * v
    angle = jnp.minimum(square, LIMIT).astype(F32) * FRESNEL_RATE
    keep = jnp.where(square <= LIMIT, 1.0 / (G * G), 0.0)
    return cosine_of(angle) * keep, -sine_of(angle) * keep


def copies_kernel(potential_ref, out_ref):
    values = potential_ref[0]
    pick = ((iota((K, K), 0) + iota((K, K), 1)) & (K - 1)) == 0
    mirror = jnp.where(pick, 1.0, 0.0)
    quarters = [values[:, K * i : K * (i + 1)] for i in range(4)]
    for i in (1, 3):
        quarters[i] = jnp.dot(
            quarters[i], mirror, precision=lax.Precision.HIGHEST, preferred_element_type=F32
        )
    piece = jnp.concatenate(quarters, axis=0)
    out_ref[...] = jnp.broadcast_to(piece[None], out_ref.shape)


AHEAD_LEFT = (0, ROWS, G)
AHEAD_RIGHT = (AHEAD_LEFT[0] + AHEAD_LEFT[1], G, G)
BACK_RIGHT = (AHEAD_RIGHT[0] + G, G, G)
BACK_LEFT = (BACK_RIGHT[0] + G, G, G)
CROP_LEFT = (BACK_LEFT[0] + G, K, G)
CROP_RIGHT = (CROP_LEFT[0] + K, G, K)
IMAGE_RIGHT = (CROP_RIGHT[0] + G, K, 2 * K)
IMAGE_LEFT = (IMAGE_RIGHT[0] + K, 2 * K, 2 * K)
TABLE_ROWS = IMAGE_LEFT[0] + IMAGE_LEFT[1]

def terms(ref, where):
    row, rows, columns = where
    return ref[row : row + rows, :columns], ref[row : row + rows, G : G + columns]


def near(index):
    return index - REACH


def whole(index):
    return index


def band(index):
    return signed(index, K)


def plane_wave(tilt_x, tilt_y):
    sine_x, cosine_x = circle(tilt_x * position(iota((G, K), 0), mixed), G)
    sine_y, cosine_y = circle(tilt_y * position(iota((8, G), 1), natural), G)
    sine_x, cosine_x = (jnp.concatenate([value] * (G // K), axis=1) for value in (sine_x, cosine_x))
    sine_y, cosine_y = (jnp.concatenate([value] * (G // 8), axis=0) for value in (sine_y, cosine_y))
    return cosine_x * cosine_y - sine_x * sine_y, sine_x * cosine_y + cosine_x * sine_y


def prepare_kernel(places_ref, tilts_ref, weight_ref, high_ref, low_ref, table_ref):
    probes = places_ref.shape[0]
    beams = tilts_ref.shape[1]
    steps = places_ref[:, 0:1] * tilts_ref[0:1, :] + places_ref[:, 1:2] * tilts_ref[1:2, :]
    sine, cosine = circle(-steps, K)
    weight_re, weight_im = weight_ref[0:1, :], weight_ref[1:2, :]
    real = cosine * weight_re - sine * weight_im
    imag = cosine * weight_im + sine * weight_re
    for row, column, part in (
        (0, 0, real),
        (0, beams, -imag),
        (probes, 0, imag),
        (probes, beams, real),
    ):
        high, low = split(part)
        high_ref[row : row + probes, column : column + beams] = high
        low_ref[row : row + probes, column : column + beams] = low

    m, other = iota((2 * K, 2 * K), 0), iota((2 * K, 2 * K), 1)
    turn = 2 * (m >> 1) * (other & (K - 1)) + (G // 4) * ((other >> 7) - (m & 1))
    left, right = iota((K, 2 * K), 0), iota((K, 2 * K), 1)
    for (row, rows, columns), table in (
        (AHEAD_LEFT, forward_table((ROWS, G), near, mixed, 1)),
        (AHEAD_RIGHT, forward_table((G, G), whole, natural, 0)),
        (BACK_RIGHT, forward_table((G, G), whole, natural, 1)),
        (BACK_LEFT, forward_table((G, G), near, mixed, 0)),
        (CROP_LEFT, forward_table((K, G), band, mixed, 1)),
        (CROP_RIGHT, forward_table((G, K), band, natural, 0)),
        (IMAGE_RIGHT, cosine_step(2 * left * (right & (K - 1)) - (G // 4) * (right >> 7), G)),
        (IMAGE_LEFT, cosine_step(turn, G)),
    ):
        high, low = split(table)
        table_ref[row : row + rows, :columns] = high
        table_ref[row : row + rows, G : G + columns] = low


def from_left(table, field):
    high, low = split(field)
    short = table[0].shape[1] - field.shape[0]
    if short:
        none = jnp.zeros((short, field.shape[1]), BF16)
        high, low = jnp.concatenate([high, none], axis=0), jnp.concatenate([low, none], axis=0)
    return jnp.dot(
        jnp.concatenate([table[0], table[0], table[1]], axis=1),
        jnp.concatenate([high, low, high], axis=0),
        preferred_element_type=F32,
    )


def from_right(field, table):
    high, low = split(field)
    return jnp.dot(
        jnp.concatenate([high, low, high], axis=1),
        jnp.concatenate([table[0], table[0], table[1]], axis=0),
        preferred_element_type=F32,
    )


def halves(value, axis):
    half = value.shape[axis] // 2
    return lax.slice_in_dim(value, 0, half, axis=axis), lax.slice_in_dim(value, half, 2 * half, axis=axis)


def fold(real, imag, axis):
    real_ahead, real_back = halves(real, axis)
    imag_ahead, imag_back = halves(imag, axis)
    alone = iota(real_ahead.shape, axis) == 0
    return (
        jnp.concatenate(
            [
                jnp.where(alone, real_ahead, real_ahead + real_back),
                jnp.where(alone, real_back, imag_ahead - imag_back),
            ],
            axis=axis,
        ),
        jnp.concatenate(
            [
                jnp.where(alone, imag_ahead, imag_ahead + imag_back),
                jnp.where(alone, imag_back, real_back - real_ahead),
            ],
            axis=axis,
        ),
    )


def unfold(real, imag, axis):
    real_even, real_odd = halves(real, axis)
    imag_even, imag_odd = halves(imag, axis)
    alone = iota(real_even.shape, axis) == 0
    return (
        jnp.concatenate(
            [
                jnp.where(alone, real_even, real_even - imag_odd),
                jnp.where(alone, real_odd, real_even + imag_odd),
            ],
            axis=axis,
        ),
        jnp.concatenate(
            [
                jnp.where(alone, imag_even, imag_even + real_odd),
                jnp.where(alone, imag_odd, imag_even - real_odd),
            ],
            axis=axis,
        ),
    )


def spectrum(real, imag, left, right, factor):
    field = from_left(left, jnp.concatenate(fold(real, imag, 0), axis=1))
    field = jnp.concatenate(fold(*halves(field, 1), 1), axis=0)
    real, imag = halves(from_right(field, right), 0)
    return (
        real * factor[0] - imag * factor[1],
        real * factor[1] + imag * factor[0],
    )


def screened(real, imag, potential_ref, layer):
    count = G // 4

    def rows(half, parity, side):
        at = PIECE * count * half + SLICES * (2 * parity + side) + layer
        return potential_ref[pl.ds(at, count, PIECE), :]

    def block(half, parity):
        values = jnp.concatenate([rows(half, parity, side) for side in range(2)], axis=1)
        return pltpu.roll(values, 1, 0) if half and not parity else values

    potential = jnp.concatenate([block(half, parity) for half in range(2) for parity in range(2)], axis=0)
    sine, cosine = sine_of(potential - 1.5), cosine_of(potential - 1.5)
    cos_mid, sin_mid = math.cos(1.5), math.sin(1.5)
    cosine, sine = cosine * cos_mid - sine * sin_mid, sine * cos_mid + cosine * sin_mid
    return real * cosine - imag * sine, real * sine + imag * cosine


def propagate_kernel(tilt_ref, potential_ref, table_ref, out_ref, factor_ref):
    table = functools.partial(terms, table_ref)
    real, imag = fresnel((ROWS, G), near, lambda index: signed(index, G))
    factor_ref[0], factor_ref[1] = real, imag
    real, imag = plane_wave(tilt_ref[0], tilt_ref[1])
    for layer in range(SLICES - 1):
        real, imag = screened(real, imag, potential_ref, layer)
        real, imag = spectrum(real, imag, table(AHEAD_LEFT), table(AHEAD_RIGHT), factor_ref)
        field = from_right(jnp.concatenate([real, imag], axis=0), table(BACK_RIGHT))
        field = jnp.concatenate(unfold(*halves(field, 0), 1), axis=1)
        real, imag = unfold(*halves(from_left(table(BACK_LEFT), field), 1), 0)
    real, imag = screened(real, imag, potential_ref, SLICES - 1)
    real, imag = spectrum(real, imag, table(CROP_LEFT), table(CROP_RIGHT), fresnel((K, K), band, band))
    product = from_right(jnp.concatenate([real, imag], axis=0), table(IMAGE_RIGHT))
    real = product[:K, :K] - product[K:, K:]
    imag = product[:K, K:] + product[K:, :K]
    out_ref[...] = from_left(table(IMAGE_LEFT), jnp.concatenate([real, imag], axis=0))


def probe_kernel(configs, block_ref, high_ref, low_ref, mine_ref, other_ref):
    here = block_ref.shape[0] // (2 * K)
    field = jnp.concatenate(
        [
            jnp.concatenate(
                [block_ref[pl.ds(2 * K * config + part, K, 2), :] for part in range(2)], axis=0
            )
            for config in range(here)
        ],
        axis=1,
    )
    waves = from_left((high_ref[...], low_ref[...]), field)
    probes = waves.shape[0] // 2
    real, imag = waves[:probes], waves[probes:]
    power = real * real + imag * imag
    total = sum(power[:, K * config : K * config + K] for config in range(here)) * (1.0 / configs)
    mine_ref[...] = total[: probes // 2]
    other_ref[...] = total[probes // 2 :]


VMEM = pl.BlockSpec(memory_space=pltpu.VMEM)
SMEM = pl.BlockSpec(memory_space=pltpu.SMEM)
PARAMS = pltpu.CompilerParams(vmem_limit_bytes=24 * 1024 * 1024)


def shape_of(dtype, *shape):
    return jax.ShapeDtypeStruct(shape, dtype)


def prepare(places, tilts, weight):
    probes, beams = places.shape[0], tilts.shape[1]
    out = [
        shape_of(BF16, 2 * probes, 2 * beams),
        shape_of(BF16, 2 * probes, 2 * beams),
        shape_of(BF16, TABLE_ROWS, 2 * G),
    ]
    return pl.pallas_call(
        prepare_kernel,
        out_shape=out,
        in_specs=[VMEM] * 3,
        out_specs=[VMEM] * len(out),
        compiler_params=PARAMS,
        name="prepare",
    )(places, tilts, weight)


def propagate(tilt, potential, table):
    return pl.pallas_call(
        propagate_kernel,
        out_shape=shape_of(F32, 2 * K, K),
        in_specs=[SMEM, VMEM, VMEM],
        out_specs=VMEM,
        scratch_shapes=[pltpu.VMEM((2, ROWS, G), F32)],
        compiler_params=PARAMS,
        name="propagate",
    )(tilt, potential, table)


def probe(block, high, low, configs):
    quarter = high.shape[0] // 4
    return pl.pallas_call(
        functools.partial(probe_kernel, configs),
        out_shape=[shape_of(F32, quarter, K)] * 2,
        in_specs=[VMEM] * 3,
        out_specs=[VMEM] * 2,
        compiler_params=PARAMS,
        name="probe",
    )(block, high, low)


def copies_of(potential, count):
    return pl.pallas_call(
        copies_kernel,
        out_shape=shape_of(F32, count, PIECE, K),
        in_specs=[VMEM],
        out_specs=VMEM,
        compiler_params=PARAMS,
        name="copies",
    )(potential)


def per_device(groups, potential, tilts, aperture, positions):
    near, far = groups
    devices = lax.axis_size("beam")
    pairs, cores = lax.axis_size("pair"), lax.axis_size("core")
    configs = pairs * cores
    beams = tilts.shape[0]
    quarter = positions.shape[0] // configs
    own = lax.axis_index("beam")
    slab = lax.axis_index(("pair", "core"))

    part = lax.all_to_all(copies_of(potential, len(near[0])), "beam", 0, 0, axis_index_groups=near)
    part, tilts, aperture, positions = lax.optimization_barrier((part, tilts, aperture, positions))
    part = part.reshape(len(near[0]) * PIECE, K)
    whole = lax.all_to_all(
        jnp.broadcast_to(part[None], (len(far[0]), *part.shape)), "beam", 0, 0, axis_index_groups=far
    ).reshape(devices * PIECE, K)

    places = positions.reshape(configs, quarter, 2)
    places = jnp.concatenate([places[slab], places[slab ^ 1]], axis=0)
    square = (tilts[:, 0] ** 2 + tilts[:, 1] ** 2).astype(F32)
    amount = aperture.astype(F32) * (1.0 / math.sqrt(beams))
    weight = jnp.stack([jnp.cos(DEFOCUS_RATE * square) * amount, -jnp.sin(DEFOCUS_RATE * square) * amount])
    tilt = lax.dynamic_index_in_dim(tilts, own, 0, keepdims=False)
    coef_high, coef_low, table = prepare(places, tilts.T, weight)
    image = propagate(tilt, whole, table)

    rows = jnp.broadcast_to(image.reshape(1, K, 2, K), (pairs, K, 2, K)).reshape(pairs * K, 2, K)
    block = lax.all_to_all(rows, ("pair", "beam"), 0, 0, tiled=True).reshape(2 * pairs * beams, K)
    mine, other = probe(block, coef_high, coef_low, configs)
    return mine + lax.ppermute(other, "core", [(0, 1), (1, 0)])


def solution(mesh):
    fine = jax.sharding.Mesh(mesh.devices.reshape(-1, 2, 2), ("beam", "pair", "core"))
    nx, run = 4, mesh.devices.shape[0] // 4
    near = [[x * run + i for i in (range(run) if 2 * x < nx else reversed(range(run)))] for x in range(nx)]
    order = [*range(nx // 2), *reversed(range(nx // 2, nx))]
    far = [[x * run + i for x in order] for i in range(run)]
    return jax.shard_map(
        functools.partial(per_device, (near, far)),
        mesh=fine,
        in_specs=(P(("pair", "core"), None, "beam"), P(), P(), P()),
        out_specs=P(("pair", "core"), "beam"),
        check_vma=False,
    )
```

time: 559 us -> 83.6 us (0.15)
  blocking collectives: 317 us -> 28.1 us
  waiting for transfers between devices: 105 us -> 20.9 us
  matrix products: 81 us -> 0 us
  local copies, waits for them, and re-layouts: 29.5 us -> 2.06 us
  starting transfers between devices: 6.34 us -> 22.2 us
  between operations: 14.1 us -> 0.13 us
  Pallas kernels: 0 us -> 9.11 us
    all_gather x1 -> x0, blocking collectives: 317 us -> none  [per_device(): layers = transmit(lax.all_gather(potential[0], 'beam', axis=1, tiled=True))]
    reduce_scatter x1 -> x0, waiting for transfers between devices: 94.7 us -> none  [per_device(): summed = lax.psum_scatter(terms, 'slab', scatter_dimension=0, tiled=True)]
    dot_general x52 -> x0, matrix products: 81 us -> none  [the longest x24 45 us: contract(): jnp.einsum('mx,bxy->bmy', matrix, field, precision=lax.Precision.HIGHEST)]
    all_to_all x0 -> x1, blocking collectives: none -> 28.1 us  [per_device(): lax.all_to_all(rows, ('pair', 'beam'), 0, 0, tiled=True)]
    sin x1 -> x0, local copies, waits for them, and re-layouts: 22 us -> none  [transmit(): return jnp.stack([jnp.cos(piece), jnp.sin(piece)])]
    all_to_all x1 -> x2, starting transfers between devices: 6.3 us -> 17.1 us  [the longest x1 13.6 us: per_device(): lax.all_to_all(copies_of(potential, len(near[0])), 'beam', 0, 0, axis_ind...]
    all_to_all x1 -> x2, waiting for transfers between devices: 10.3 us -> 20 us  [the longest x1 11.5 us: per_device(): lax.all_to_all(copies_of(potential, len(near[0])), 'beam', 0, 0, axis_ind...]
    pallas_call x0 -> x4, Pallas kernels: none -> 9.11 us  [the longest x1 5.5 us: propagate(): pl.pallas_call(propagate_kernel, out_shape=shape_of(F32, 2 * K, K), in_sp...]
  transfers between devices with their start and end apart: 2 -> 3, of which waited for: 2 -> 3; matrix products, arithmetic and copies ran while one was open for 0% -> 1% of each run, Pallas kernels for 0% -> 3%
where the time goes in v4:
time: 83.6 us; the launch traced here: 83.2 us
  blocking collectives  28.1 us (34%)
  starting transfers between devices  22.2 us (27%)
  waiting for transfers between devices  20.9 us (25%)
  Pallas kernels  9.11 us (11%)
  local copies, waits for them, and re-layouts  2.06 us (2%)
    all_to_all x1, blocking collectives, per_device(): lax.all_to_all(rows, ('pair', 'beam'), 0, 0, tiled=True)  28.1 us
    all_to_all x1, starting transfers between devices, per_device(): lax.all_to_all(copies_of(potential, len(near[0])), 'beam', 0, 0, axis_ind...  13.6 us
    all_to_all x1, waiting for transfers between devices, per_device(): lax.all_to_all(copies_of(potential, len(near[0])), 'beam', 0, 0, axis_ind...  11.5 us
    all_to_all x1, waiting for transfers between devices, per_device(): lax.all_to_all(jnp.broadcast_to(part[None], (len(far[0]), *part.shape)),...  8.55 us
    pallas_call x1, Pallas kernels, propagate(): pl.pallas_call(propagate_kernel, out_shape=shape_of(F32, 2 * K, K), in_sp...  5.5 us
    ppermute x1, starting transfers between devices, per_device(): return mine + lax.ppermute(other, 'core', [(0, 1), (1, 0)])  5.1 us
    all_to_all x1, starting transfers between devices, per_device(): lax.all_to_all(jnp.broadcast_to(part[None], (len(far[0]), *part.shape)),...  3.49 us
    pallas_call x1, Pallas kernels, prepare(): pl.pallas_call(prepare_kernel, out_shape=out, in_specs=[VMEM] * 3, out_sp...  2.3 us
  transfers between devices with their start and end apart: 3, of which 3 were waited for; matrix products, arithmetic and copies ran while one was open for 1% of the time, Pallas kernels for 3%

profile of v4, /device:TPU:1, one launch (start us, length us, event | category | flops | bytes accessed | tf_op | source)
XLA Modules:
  0.0 83.2 jit_solution(1315303933090641854)
XLA Ops:
  0.0 0.7 copy.11.potential_ref
  0.7 0.9 %copies.1 = f32[32,12,128]{2,1,0:T(8,128)} custom-call(f32[1,3,512]{2,1,0:T(4,128)S(1)} %copy.11.potential_ref), custom_call_target="tpu_custom_call" | custom-call | tf_op jit(solution)/shard_map/copies/pallas_call | solution.py:376
  1.6 0.0 copy-start.1
  1.6 0.0 copy-start
  1.6 0.0 copy-start.2
  1.6 13.6 %all-to-all-start = ((f32[32,12,128]{2,1,0:T(8,128)}), f32[32,12,128]{2,1,0:T(8,128)S(1)}, u32[]{:S(2)}, u32[]{:S(2)}) async-start(f32[32,12,128]{2,1,0:T(8,128)} %copies.1), calls=%async_computation | async-start | bytes 524288 | tf_op jit(solution)/shard_map/all_to_all | solution.py:396
  15.3 11.5 %all-to-all-done = f32[32,12,128]{2,1,0:T(8,128)S(1)} async-done(((f32[32,12,128]{2,1,0:T(8,128)}), f32[32,12,128]{2,1,0:T(8,128)S(1)}, u32[]{:S(2)}, u32[]{:S(2)}) %all-to-all-start) | async-done | bytes 196640 | tf_op jit(solution)/shard_map/all_to_all | solution.py:396
  26.8 0.9 %broadcast_in_dim.15 = f32[4,384,128]{2,1,0:T(8,128)} broadcast(f32[384,128]{1,0:T(8,128)S(1)} %broadcast_in_dim.14), dimensions={1,2} | broadcast | bytes 983040 | tf_op jit(solution)/shard_map/broadcast_in_dim | solution.py:400
  27.7 3.5 %all-to-all-start.1 = ((f32[4,384,128]{2,1,0:T(8,128)}), f32[4,384,128]{2,1,0:T(8,128)S(1)}, u32[]{:S(2)}, u32[]{:S(2)}) async-start(f32[4,384,128]{2,1,0:T(8,128)} %broadcast_in_dim.15), calls=%async_computation.1 | async-start | bytes 1572864 | tf_op jit(solution)/shard_map/all_to_all | solution.py:399
  31.2 0.0 copy-done.1
  31.2 0.1 copy.14.places_ref
  31.4 0.0 copy-done
  31.4 0.2 dynamic-slice_reduce_fusion.tilt_ref
  31.6 0.0 copy-done.2
  31.7 2.3 %prepare.1 = (bf16[512,256]{1,0:T(8,128)(2,1)S(1)}, bf16[512,256]{1,0:T(8,128)(2,1)S(1)}, bf16[1712,512]{1,0:T(8,128)(2,1)S(1)}) custom-call(s32[256,2]{1,0:T(8,128)S(1)} %copy.14.places_ref, s32[2,128]{1,0:T(2,128)S(1)} %bitcast.25, f32[2,128]{1,0:T(2,128)S(1)} %pad_maximum_fusion.weight_ref), custom_call_target="tpu_custom_call" | custom-call | tf_op jit(solution)/shard_map/prepare/pallas_call | solution.py:341
  34.0 8.6 %all-to-all-done.1 = f32[4,384,128]{2,1,0:T(8,128)S(1)} async-done(((f32[4,384,128]{2,1,0:T(8,128)}), f32[4,384,128]{2,1,0:T(8,128)S(1)}, u32[]{:S(2)}, u32[]{:S(2)}) %all-to-all-start.1) | async-done | bytes 786464 | tf_op jit(solution)/shard_map/all_to_all | solution.py:399
  42.5 5.5 %propagate.1 = f32[256,128]{1,0:T(8,128)S(1)} custom-call(s32[2]{0:T(128)S(1)} %dynamic-slice_reduce_fusion.tilt_ref, f32[1536,128]{1,0:T(8,128)S(1)} %bitcast.22, bf16[1712,512]{1,0:T(8,128)(2,1)S(1)} %get-tuple-element.18.table_ref), custom_call_target="tpu_custom_call" | custom-call | tf_op jit(solution)/shard_map/propagate/pallas_call | solution.py:352
  48.0 0.1 broadcast_in_dim.17
  48.1 28.1 %all_to_all.15 = f32[256,2,128]{2,1,0:T(2,128)S(1)} all-to-all(f32[256,2,128]{2,1,0:T(2,128)S(1)} %bitcast.26), channel_id=1, replica_groups=mesh['beam'=128,'pair'=2,'core'=2] {'pair','beam'}, dimensions={0} | all-to-all | bytes 524288 | tf_op jit(solution)/shard_map/all_to_all | solution.py:413
  76.2 0.4 probe.1
  76.6 5.1 %collective-permute-start = (f32[128,128]{1,0:T(8,128)S(1)}, f32[128,128]{1,0:T(8,128)S(1)}, u32[]{:S(2)}, u32[]{:S(2)}) collective-permute-start(f32[128,128]{1,0:T(8,128)S(1)} %get-tuple-element.22), channel_id=1, source_target_pairs={{0,1},{1,0},{2,3},{3,2},{4,5},{5,4},{6,7},{7,6},{8,9},{9,8},{10,11... | collective-permute-start | bytes 196616 | tf_op jit(solution)/shard_map/ppermute | solution.py:415
  81.7 0.9 %collective-permute-done = f32[128,128]{1,0:T(8,128)S(1)} collective-permute-done((f32[128,128]{1,0:T(8,128)S(1)}, f32[128,128]{1,0:T(8,128)S(1)}, u32[]{:S(2)}, u32[]{:S(2)}) %collective-permute-start) | collective-permute-done | bytes 65568 | tf_op jit(solution)/shard_map/ppermute | solution.py:415
  82.6 0.6 add.25
  (6 shorter events, 0.1 us)
Async XLA Ops:
  1.6 29.6 %copy-start.1 = (s32[512,2]{0,1:T(2,128)S(1)}, s32[512,2]{0,1:T(2,128)}, u32[]{:S(2)}) copy-start(s32[512,2]{0,1:T(2,128)} %param.7) | copy-start | bytes 12292
  1.6 29.7 %copy-start = (s32[128,2]{0,1:T(2,128)S(1)}, s32[128,2]{0,1:T(2,128)}, u32[]{:S(2)}) copy-start(s32[128,2]{0,1:T(2,128)} %param.5) | copy-start | bytes 3076
  1.6 29.9 %copy-start.2 = (s32[128]{0:T(128)S(1)}, s32[128]{0:T(128)}, u32[]{:S(2)}) copy-start(s32[128]{0:T(128)} %param.6) | copy-start | bytes 1540
  1.6 25.1 %all-to-all-start = ((f32[32,12,128]{2,1,0:T(8,128)}), f32[32,12,128]{2,1,0:T(8,128)S(1)}, u32[]{:S(2)}, u32[]{:S(2)}) async-start(f32[32,12,128]{2,1,0:T(8,128)} %copies.1), calls=%async_computation | async-start | bytes 524288 | tf_op jit(solution)/shard_map/all_to_all | solution.py:396
  27.7 14.9 %all-to-all-start.1 = ((f32[4,384,128]{2,1,0:T(8,128)}), f32[4,384,128]{2,1,0:T(8,128)S(1)}, u32[]{:S(2)}, u32[]{:S(2)}) async-start(f32[4,384,128]{2,1,0:T(8,128)} %broadcast_in_dim.15), calls=%async_computation.1 | async-start | bytes 1572864 | tf_op jit(solution)/shard_map/all_to_all | solution.py:399
  76.6 6.0 %collective-permute-start = (f32[128,128]{1,0:T(8,128)S(1)}, f32[128,128]{1,0:T(8,128)S(1)}, u32[]{:S(2)}, u32[]{:S(2)}) collective-permute-start(f32[128,128]{1,0:T(8,128)S(1)} %get-tuple-element.22), channel_id=1, source_target_pairs={{0,1},{1,0},{2,3},{3,2},{4,5},{5,4},{6,7},{7,6},{8,9},{9,8},{10,11... | collective-permute-start | bytes 196616 | tf_op jit(solution)/shard_map/ppermute | solution.py:415

commit v5 on v4

--- a/solution.py
+++ b/solution.py
@@ -30,16 +30,16 @@
 
 def sine_of(t):
     s = t * t
-    sine = jnp.full_like(t, -2.5052108e-8)
-    for term in (2.7557319e-6, -1.9841270e-4, 8.3333333e-3, -1.6666667e-1, 1.0):
+    sine = jnp.full_like(t, 2.60501958e-6)
+    for term in (-1.9808983e-4, 8.33304978e-3, -1.66666579e-1, 0.999999996):
         sine = sine * s + term
     return sine * t
 
 
 def cosine_of(t):
     s = t * t
-    cosine = jnp.full_like(t, 2.0876757e-9)
-    for term in (-2.7557319e-7, 2.4801587e-5, -1.3888889e-3, 4.1666667e-2, -0.5, 1.0):
+    cosine = jnp.full_like(t, 2.31515759e-5)
+    for term in (-1.38535979e-3, 4.16635698e-2, -0.499999047, 0.999999953):
         cosine = cosine * s + term
     return cosine
 
@@ -109,8 +109,11 @@
         quarters[i] = jnp.dot(
             quarters[i], mirror, precision=lax.Precision.HIGHEST, preferred_element_type=F32
         )
-    piece = jnp.concatenate(quarters, axis=0)
-    out_ref[...] = jnp.broadcast_to(piece[None], out_ref.shape)
+    pieces = [
+        jnp.concatenate([quarter[layer : layer + 1] for quarter in quarters], axis=0)[None]
+        for layer in range(SLICES)
+    ]
+    out_ref[...] = jnp.concatenate(pieces * (out_ref.shape[0] // SLICES), axis=0)
 
 
 AHEAD_LEFT = (0, ROWS, G)
@@ -118,8 +121,7 @@
 BACK_RIGHT = (AHEAD_RIGHT[0] + G, G, G)
 BACK_LEFT = (BACK_RIGHT[0] + G, G, G)
 CROP_LEFT = (BACK_LEFT[0] + G, K, G)
-CROP_RIGHT = (CROP_LEFT[0] + K, G, K)
-IMAGE_RIGHT = (CROP_RIGHT[0] + G, K, 2 * K)
+IMAGE_RIGHT = (CROP_LEFT[0] + K, K, 2 * K)
 IMAGE_LEFT = (IMAGE_RIGHT[0] + K, 2 * K, 2 * K)
 TABLE_ROWS = IMAGE_LEFT[0] + IMAGE_LEFT[1]
 
@@ -129,53 +131,40 @@
 
 
 def near(index):
-    return index - REACH
+    return index - ROWS // 2
 
 
 def whole(index):
     return index
 
 
-def band(index):
-    return signed(index, K)
-
-
-def plane_wave(tilt_x, tilt_y):
-    sine_x, cosine_x = circle(tilt_x * position(iota((G, K), 0), mixed), G)
-    sine_y, cosine_y = circle(tilt_y * position(iota((8, G), 1), natural), G)
-    sine_x, cosine_x = (jnp.concatenate([value] * (G // K), axis=1) for value in (sine_x, cosine_x))
-    sine_y, cosine_y = (jnp.concatenate([value] * (G // 8), axis=0) for value in (sine_y, cosine_y))
-    return cosine_x * cosine_y - sine_x * sine_y, sine_x * cosine_y + cosine_x * sine_y
-
-
-def prepare_kernel(places_ref, tilts_ref, weight_ref, high_ref, low_ref, table_ref):
+def centred(index):
+    return index - K // 2
+
+
+def prepare_kernel(
+    tilt_ref, places_ref, tilts_ref, weight_ref, coef_ref, table_ref, factor_ref, across_ref
+):
+    across_ref[0], across_ref[1] = circle(tilt_ref[0] * position(iota((G, K), 0), mixed), G)
+    factor_ref[0], factor_ref[1] = fresnel((ROWS, G), near, lambda index: signed(index, G))
+
     probes = places_ref.shape[0]
     beams = tilts_ref.shape[1]
     steps = places_ref[:, 0:1] * tilts_ref[0:1, :] + places_ref[:, 1:2] * tilts_ref[1:2, :]
     sine, cosine = circle(-steps, K)
     weight_re, weight_im = weight_ref[0:1, :], weight_ref[1:2, :]
-    real = cosine * weight_re - sine * weight_im
-    imag = cosine * weight_im + sine * weight_re
-    for row, column, part in (
-        (0, 0, real),
-        (0, beams, -imag),
-        (probes, 0, imag),
-        (probes, beams, real),
-    ):
-        high, low = split(part)
-        high_ref[row : row + probes, column : column + beams] = high
-        low_ref[row : row + probes, column : column + beams] = low
+    coef_ref[0] = cosine * weight_re - sine * weight_im
+    coef_ref[1] = cosine * weight_im + sine * weight_re
 
     m, other = iota((2 * K, 2 * K), 0), iota((2 * K, 2 * K), 1)
-    turn = 2 * (m >> 1) * (other & (K - 1)) + (G // 4) * ((other >> 7) - (m & 1))
+    turn = 2 * (m >> 1) * centred(other & (K - 1)) + (G // 4) * ((other >> 7) - (m & 1))
     left, right = iota((K, 2 * K), 0), iota((K, 2 * K), 1)
     for (row, rows, columns), table in (
         (AHEAD_LEFT, forward_table((ROWS, G), near, mixed, 1)),
         (AHEAD_RIGHT, forward_table((G, G), whole, natural, 0)),
         (BACK_RIGHT, forward_table((G, G), whole, natural, 1)),
         (BACK_LEFT, forward_table((G, G), near, mixed, 0)),
-        (CROP_LEFT, forward_table((K, G), band, mixed, 1)),
-        (CROP_RIGHT, forward_table((G, K), band, natural, 0)),
+        (CROP_LEFT, forward_table((K, G), centred, mixed, 1)),
         (IMAGE_RIGHT, cosine_step(2 * left * (right & (K - 1)) - (G // 4) * (right >> 7), G)),
         (IMAGE_LEFT, cosine_step(turn, G)),
     ):
@@ -211,45 +200,37 @@
     return lax.slice_in_dim(value, 0, half, axis=axis), lax.slice_in_dim(value, half, 2 * half, axis=axis)
 
 
+def alone(first, others, axis):
+    if axis:
+        return jnp.where(iota(others.shape, 1) == 0, first, others)
+    head = jnp.where(iota((8, others.shape[1]), 0) == 0, first[:8], others[:8])
+    return jnp.concatenate([head, others[8:]], axis=0)
+
+
 def fold(real, imag, axis):
     real_ahead, real_back = halves(real, axis)
     imag_ahead, imag_back = halves(imag, axis)
-    alone = iota(real_ahead.shape, axis) == 0
+    real_odd, imag_odd = real_back - real_ahead, imag_ahead - imag_back
     return (
         jnp.concatenate(
-            [
-                jnp.where(alone, real_ahead, real_ahead + real_back),
-                jnp.where(alone, real_back, imag_ahead - imag_back),
-            ],
+            [alone(real_ahead, real_ahead + real_back, axis), alone(real_back, imag_odd, axis)], axis=axis
+        ),
+        jnp.concatenate(
+            [alone(imag_ahead, imag_ahead + imag_back, axis), alone(imag_back, real_odd, axis)], axis=axis
+        ),
+    )
+
+
+def unfold(real, imag, axis):
+    real_even, real_odd = halves(real, axis)
+    imag_even, imag_odd = halves(imag, axis)
+    return (
+        jnp.concatenate(
+            [alone(real_even, real_even - imag_odd, axis), alone(real_odd, real_even + imag_odd, axis)],
             axis=axis,
         ),
         jnp.concatenate(
-            [
-                jnp.where(alone, imag_ahead, imag_ahead + imag_back),
-                jnp.where(alone, imag_back, real_back - real_ahead),
-            ],
-            axis=axis,
-        ),
-    )
-
-
-def unfold(real, imag, axis):
-    real_even, real_odd = halves(real, axis)
-    imag_even, imag_odd = halves(imag, axis)
-    alone = iota(real_even.shape, axis) == 0
-    return (
-        jnp.concatenate(
-            [
-                jnp.where(alone, real_even, real_even - imag_odd),
-                jnp.where(alone, real_odd, real_even + imag_odd),
-            ],
-            axis=axis,
-        ),
-        jnp.concatenate(
-            [
-                jnp.where(alone, imag_even, imag_even + real_odd),
-                jnp.where(alone, imag_odd, imag_even - real_odd),
-            ],
+            [alone(imag_even, imag_even + real_odd, axis), alone(imag_odd, imag_even - real_odd, axis)],
             axis=axis,
         ),
     )
@@ -269,7 +250,7 @@
     count = G // 4
 
     def rows(half, parity, side):
-        at = PIECE * count * half + SLICES * (2 * parity + side) + layer
+        at = PIECE * count * half + 4 * layer + 2 * parity + side
         return potential_ref[pl.ds(at, count, PIECE), :]
 
     def block(half, parity):
@@ -277,32 +258,43 @@
         return pltpu.roll(values, 1, 0) if half and not parity else values
 
     potential = jnp.concatenate([block(half, parity) for half in range(2) for parity in range(2)], axis=0)
-    sine, cosine = sine_of(potential - 1.5), cosine_of(potential - 1.5)
-    cos_mid, sin_mid = math.cos(1.5), math.sin(1.5)
-    cosine, sine = cosine * cos_mid - sine * sin_mid, sine * cos_mid + cosine * sin_mid
-    return real * cosine - imag * sine, real * sine + imag * cosine
-
-
-def propagate_kernel(tilt_ref, potential_ref, table_ref, out_ref, factor_ref):
+    turned = potential - math.pi / 2
+    sine, cosine = cosine_of(turned), sine_of(turned)
+    return -(real * cosine + imag * sine), real * sine - imag * cosine
+
+
+def plane_wave(across_ref, tilt_y):
+    sine_x, cosine_x = (jnp.concatenate([across_ref[i]] * (G // K), axis=1) for i in range(2))
+    sine_y, cosine_y = circle(tilt_y * position(iota((8, G), 1), natural), G)
+    sine_y, cosine_y = (jnp.concatenate([value] * (G // 8), axis=0) for value in (sine_y, cosine_y))
+    return cosine_x * cosine_y - sine_x * sine_y, sine_x * cosine_y + cosine_x * sine_y
+
+
+def band_of(value):
+    return jnp.where(iota((value.shape[0], K), 1) < K // 2, value[:, :K], value[:, K:])
+
+
+def propagate_kernel(tilt_ref, potential_ref, table_ref, factor_ref, across_ref, out_ref):
     table = functools.partial(terms, table_ref)
-    real, imag = fresnel((ROWS, G), near, lambda index: signed(index, G))
-    factor_ref[0], factor_ref[1] = real, imag
-    real, imag = plane_wave(tilt_ref[0], tilt_ref[1])
+    real, imag = plane_wave(across_ref, tilt_ref[1])
     for layer in range(SLICES - 1):
         real, imag = screened(real, imag, potential_ref, layer)
         real, imag = spectrum(real, imag, table(AHEAD_LEFT), table(AHEAD_RIGHT), factor_ref)
         field = from_right(jnp.concatenate([real, imag], axis=0), table(BACK_RIGHT))
         field = jnp.concatenate(unfold(*halves(field, 0), 1), axis=1)
         real, imag = unfold(*halves(from_left(table(BACK_LEFT), field), 1), 0)
+    crop_right = [band_of(term) for term in table(AHEAD_RIGHT)]
+    first = (ROWS - K) // 2
+    crop_factor = [band_of(factor_ref[i, first : first + K, :]) for i in range(2)]
     real, imag = screened(real, imag, potential_ref, SLICES - 1)
-    real, imag = spectrum(real, imag, table(CROP_LEFT), table(CROP_RIGHT), fresnel((K, K), band, band))
+    real, imag = spectrum(real, imag, table(CROP_LEFT), crop_right, crop_factor)
     product = from_right(jnp.concatenate([real, imag], axis=0), table(IMAGE_RIGHT))
     real = product[:K, :K] - product[K:, K:]
     imag = product[:K, K:] + product[K:, :K]
     out_ref[...] = from_left(table(IMAGE_LEFT), jnp.concatenate([real, imag], axis=0))
 
 
-def probe_kernel(configs, block_ref, high_ref, low_ref, mine_ref, other_ref):
+def probe_kernel(configs, block_ref, coef_ref, mine_ref, other_ref):
     here = block_ref.shape[0] // (2 * K)
     field = jnp.concatenate(
         [
@@ -313,7 +305,11 @@
         ],
         axis=1,
     )
-    waves = from_left((high_ref[...], low_ref[...]), field)
+    real, imag = coef_ref[0], coef_ref[1]
+    table = jnp.concatenate(
+        [jnp.concatenate([real, -imag], axis=1), jnp.concatenate([imag, real], axis=1)], axis=0
+    )
+    waves = from_left(split(table), field)
     probes = waves.shape[0] // 2
     real, imag = waves[:probes], waves[probes:]
     power = real * real + imag * imag
@@ -331,51 +327,50 @@
     return jax.ShapeDtypeStruct(shape, dtype)
 
 
-def prepare(places, tilts, weight):
-    probes, beams = places.shape[0], tilts.shape[1]
+def prepare(tilt, places, tilts, weight):
     out = [
-        shape_of(BF16, 2 * probes, 2 * beams),
-        shape_of(BF16, 2 * probes, 2 * beams),
+        shape_of(F32, 2, places.shape[0], tilts.shape[1]),
         shape_of(BF16, TABLE_ROWS, 2 * G),
+        shape_of(F32, 2, ROWS, G),
+        shape_of(F32, 2, G, K),
     ]
     return pl.pallas_call(
         prepare_kernel,
         out_shape=out,
-        in_specs=[VMEM] * 3,
+        in_specs=[SMEM] + [VMEM] * 3,
         out_specs=[VMEM] * len(out),
         compiler_params=PARAMS,
         name="prepare",
-    )(places, tilts, weight)
-
-
-def propagate(tilt, potential, table):
+    )(tilt, places, tilts, weight)
+
+
+def propagate(*operands):
     return pl.pallas_call(
         propagate_kernel,
         out_shape=shape_of(F32, 2 * K, K),
-        in_specs=[SMEM, VMEM, VMEM],
+        in_specs=[SMEM] + [VMEM] * (len(operands) - 1),
         out_specs=VMEM,
-        scratch_shapes=[pltpu.VMEM((2, ROWS, G), F32)],
         compiler_params=PARAMS,
         name="propagate",
-    )(tilt, potential, table)
-
-
-def probe(block, high, low, configs):
-    quarter = high.shape[0] // 4
+    )(*operands)
+
+
+def probe(block, coef, configs):
+    quarter = coef.shape[1] // 2
     return pl.pallas_call(
         functools.partial(probe_kernel, configs),
         out_shape=[shape_of(F32, quarter, K)] * 2,
-        in_specs=[VMEM] * 3,
+        in_specs=[VMEM] * 2,
         out_specs=[VMEM] * 2,
         compiler_params=PARAMS,
         name="probe",
-    )(block, high, low)
+    )(block, coef)
 
 
 def copies_of(potential, count):
     return pl.pallas_call(
         copies_kernel,
-        out_shape=shape_of(F32, count, PIECE, K),
+        out_shape=shape_of(F32, count * SLICES, 4, K),
         in_specs=[VMEM],
         out_specs=VMEM,
         compiler_params=PARAMS,
@@ -393,7 +388,8 @@
     own = lax.axis_index("beam")
     slab = lax.axis_index(("pair", "core"))
 
-    part = lax.all_to_all(copies_of(potential, len(near[0])), "beam", 0, 0, axis_index_groups=near)
+    copies = copies_of(potential, len(near[0]))
+    part = lax.all_to_all(copies, "beam", 0, 0, axis_index_groups=near, tiled=True)
     part, tilts, aperture, positions = lax.optimization_barrier((part, tilts, aperture, positions))
     part = part.reshape(len(near[0]) * PIECE, K)
     whole = lax.all_to_all(
@@ -406,12 +402,12 @@
     amount = aperture.astype(F32) * (1.0 / math.sqrt(beams))
     weight = jnp.stack([jnp.cos(DEFOCUS_RATE * square) * amount, -jnp.sin(DEFOCUS_RATE * square) * amount])
     tilt = lax.dynamic_index_in_dim(tilts, own, 0, keepdims=False)
-    coef_high, coef_low, table = prepare(places, tilts.T, weight)
-    image = propagate(tilt, whole, table)
+    coef, *tables = prepare(tilt, places, tilts.T, weight)
+    image = propagate(tilt, whole, *tables)
 
     rows = jnp.broadcast_to(image.reshape(1, K, 2, K), (pairs, K, 2, K)).reshape(pairs * K, 2, K)
     block = lax.all_to_all(rows, ("pair", "beam"), 0, 0, tiled=True).reshape(2 * pairs * beams, K)
-    mine, other = probe(block, coef_high, coef_low, configs)
+    mine, other = probe(block, coef, configs)
     return mine + lax.ppermute(other, "core", [(0, 1), (1, 0)])
 
 

time: 83.6 us -> 81.8 us (0.978)
  waiting for transfers between devices: 20.9 us -> 19.5 us
    all_to_all x1, waiting for transfers between devices: 11.5 us -> 10.5 us  [per_device(): lax.all_to_all(copies, 'beam', 0, 0, axis_index_groups=near, tiled=True)]
where the time goes in v5:
time: 81.8 us; the launch traced here: 81.5 us
  blocking collectives  27.9 us (34%)
  starting transfers between devices  22.2 us (27%)
  waiting for transfers between devices  19.5 us (24%)
  Pallas kernels  9.02 us (11%)
  local copies, waits for them, and re-layouts  2.04 us (2%)
    all_to_all x1, blocking collectives, per_device(): lax.all_to_all(rows, ('pair', 'beam'), 0, 0, tiled=True)  27.9 us
    all_to_all x1, starting transfers between devices, per_device(): lax.all_to_all(copies, 'beam', 0, 0, axis_index_groups=near, tiled=True)  13.6 us
    all_to_all x1, waiting for transfers between devices, per_device(): lax.all_to_all(copies, 'beam', 0, 0, axis_index_groups=near, tiled=True)  10.5 us
    all_to_all x1, waiting for transfers between devices, per_device(): lax.all_to_all(jnp.broadcast_to(part[None], (len(far[0]), *part.shape)),...  8.09 us
    ppermute x1, starting transfers between devices, per_device(): return mine + lax.ppermute(other, 'core', [(0, 1), (1, 0)])  5.11 us
    pallas_call x1, Pallas kernels, propagate(): pl.pallas_call(propagate_kernel, out_shape=shape_of(F32, 2 * K, K), in_sp...  4.95 us
    all_to_all x1, starting transfers between devices, per_device(): lax.all_to_all(jnp.broadcast_to(part[None], (len(far[0]), *part.shape)),...  3.49 us
    pallas_call x1, Pallas kernels, prepare(): pl.pallas_call(prepare_kernel, out_shape=out, in_specs=[SMEM] + [VMEM] *...  2.78 us
  transfers between devices with their start and end apart: 3, of which 3 were waited for; matrix products, arithmetic and copies ran while one was open for 1% of the time, Pallas kernels for 3%

profile of v5, /device:TPU:1, one launch (start us, length us, event | category | flops | bytes accessed | tf_op | source)
XLA Modules:
  0.0 81.5 jit_solution(9789830538237959343)
XLA Ops:
  0.0 0.7 copy.8.potential_ref
  0.7 0.9 %copies.1 = f32[96,4,128]{2,1,0:T(4,128)} custom-call(f32[1,3,512]{2,1,0:T(4,128)S(1)} %copy.8.potential_ref), custom_call_target="tpu_custom_call" | custom-call | tf_op jit(solution)/shard_map/copies/pallas_call | solution.py:371
  1.6 0.0 copy-start.1
  1.6 0.0 copy-start
  1.6 0.0 copy-start.2
  1.6 13.6 %all-to-all-start = ((f32[96,4,128]{2,1,0:T(4,128)}), f32[96,4,128]{2,1,0:T(4,128)S(1)}, u32[]{:S(2)}, u32[]{:S(2)}) async-start(f32[96,4,128]{2,1,0:T(4,128)} %copies.1), calls=%async_computation | async-start | bytes 393216 | tf_op jit(solution)/shard_map/all_to_all | solution.py:392
  15.2 10.5 %all-to-all-done = f32[96,4,128]{2,1,0:T(4,128)S(1)} async-done(((f32[96,4,128]{2,1,0:T(4,128)}), f32[96,4,128]{2,1,0:T(4,128)S(1)}, u32[]{:S(2)}, u32[]{:S(2)}) %all-to-all-start) | async-done | bytes 196640 | tf_op jit(solution)/shard_map/all_to_all | solution.py:392
  25.7 0.9 %broadcast_in_dim.15 = f32[4,384,128]{2,1,0:T(8,128)} broadcast(f32[384,128]{1,0:T(8,128)S(1)} %bitcast.28), dimensions={1,2} | broadcast | bytes 983040 | tf_op jit(solution)/shard_map/broadcast_in_dim | solution.py:396
  26.7 3.5 %all-to-all-start.1 = ((f32[4,384,128]{2,1,0:T(8,128)}), f32[4,384,128]{2,1,0:T(8,128)S(1)}, u32[]{:S(2)}, u32[]{:S(2)}) async-start(f32[4,384,128]{2,1,0:T(8,128)} %broadcast_in_dim.15), calls=%async_computation.1 | async-start | bytes 1572864 | tf_op jit(solution)/shard_map/all_to_all | solution.py:395
  30.2 0.0 copy-done.1
  30.2 0.1 copy.11.places_ref
  30.4 0.0 copy-done
  30.4 0.2 dynamic-slice_reduce_fusion.tilt_ref
  30.6 0.0 copy-done.2
  30.7 2.8 %prepare.1 = (f32[2,256,128]{2,1,0:T(8,128)S(1)}, bf16[1456,512]{1,0:T(8,128)(2,1)S(1)}, f32[2,176,256]{2,1,0:T(8,128)S(1)}, f32[2,256,128]{2,1,0:T(8,128)S(1)}) custom-call(s32[2]{0:T(128)S(1)} %dynamic-slice_reduce_fusion.tilt_ref, s32[256,2]{1,0:T(8,128)S(1)} %copy.11.places_ref, s32[2,128]{1,0:T(2,128)S(1)} %bitcast.26, ...), custom_call_target="tpu_custom_call" | custom-call | tf_op jit(solution)/shard_map/prepare/pallas_call | solution.py:337
  33.4 8.1 %all-to-all-done.1 = f32[4,384,128]{2,1,0:T(8,128)S(1)} async-done(((f32[4,384,128]{2,1,0:T(8,128)}), f32[4,384,128]{2,1,0:T(8,128)S(1)}, u32[]{:S(2)}, u32[]{:S(2)}) %all-to-all-start.1) | async-done | bytes 786464 | tf_op jit(solution)/shard_map/all_to_all | solution.py:395
  41.5 5.0 %propagate.1 = f32[256,128]{1,0:T(8,128)S(1)} custom-call(s32[2]{0:T(128)S(1)} %dynamic-slice_reduce_fusion.tilt_ref, f32[1536,128]{1,0:T(8,128)S(1)} %bitcast.23, bf16[1456,512]{1,0:T(8,128)(2,1)S(1)} %get-tuple-element.19.table_ref, f32[2,176,256]{2,1,0:T(8,128)S(1)} %get-tuple-element.20.factor_ref, f32[2,256,128]{2,1,0:T(8,128)S(1)} %get-tuple-element.21.across_ref), custom_call_target="tpu_custom_call" | custom-call | tf_op jit(solution)/shard_map/propagate/pallas_call | solution.py:348
  46.5 0.1 broadcast_in_dim.17
  46.6 27.9 %all_to_all.15 = f32[256,2,128]{2,1,0:T(2,128)S(1)} all-to-all(f32[256,2,128]{2,1,0:T(2,128)S(1)} %bitcast.27), channel_id=1, replica_groups=mesh['beam'=128,'pair'=2,'core'=2] {'pair','beam'}, dimensions={0} | all-to-all | bytes 524288 | tf_op jit(solution)/shard_map/all_to_all | solution.py:409
  74.4 0.4 probe.1
  74.8 5.1 %collective-permute-start = (f32[128,128]{1,0:T(8,128)S(1)}, f32[128,128]{1,0:T(8,128)S(1)}, u32[]{:S(2)}, u32[]{:S(2)}) collective-permute-start(f32[128,128]{1,0:T(8,128)S(1)} %get-tuple-element.24), channel_id=1, source_target_pairs={{0,1},{1,0},{2,3},{3,2},{4,5},{5,4},{6,7},{7,6},{8,9},{9,8},{10,11... | collective-permute-start | bytes 196616 | tf_op jit(solution)/shard_map/ppermute | solution.py:411
  79.9 0.9 %collective-permute-done = f32[128,128]{1,0:T(8,128)S(1)} collective-permute-done((f32[128,128]{1,0:T(8,128)S(1)}, f32[128,128]{1,0:T(8,128)S(1)}, u32[]{:S(2)}, u32[]{:S(2)}) %collective-permute-start) | collective-permute-done | bytes 65568 | tf_op jit(solution)/shard_map/ppermute | solution.py:411
  80.8 0.6 add.25
  (5 shorter events, 0.1 us)
Async XLA Ops:
  1.6 28.6 %copy-start.1 = (s32[512,2]{0,1:T(2,128)S(1)}, s32[512,2]{0,1:T(2,128)}, u32[]{:S(2)}) copy-start(s32[512,2]{0,1:T(2,128)} %param.7) | copy-start | bytes 12292
  1.6 28.7 %copy-start = (s32[128,2]{0,1:T(2,128)S(1)}, s32[128,2]{0,1:T(2,128)}, u32[]{:S(2)}) copy-start(s32[128,2]{0,1:T(2,128)} %param.5) | copy-start | bytes 3076
  1.6 28.9 %copy-start.2 = (s32[128]{0:T(128)S(1)}, s32[128]{0:T(128)}, u32[]{:S(2)}) copy-start(s32[128]{0:T(128)} %param.6) | copy-start | bytes 1540
  1.6 24.1 %all-to-all-start = ((f32[96,4,128]{2,1,0:T(4,128)}), f32[96,4,128]{2,1,0:T(4,128)S(1)}, u32[]{:S(2)}, u32[]{:S(2)}) async-start(f32[96,4,128]{2,1,0:T(4,128)} %copies.1), calls=%async_computation | async-start | bytes 393216 | tf_op jit(solution)/shard_map/all_to_all | solution.py:392
  26.7 14.9 %all-to-all-start.1 = ((f32[4,384,128]{2,1,0:T(8,128)}), f32[4,384,128]{2,1,0:T(8,128)S(1)}, u32[]{:S(2)}, u32[]{:S(2)}) async-start(f32[4,384,128]{2,1,0:T(8,128)} %broadcast_in_dim.15), calls=%async_computation.1 | async-start | bytes 1572864 | tf_op jit(solution)/shard_map/all_to_all | solution.py:395
  74.8 6.0 %collective-permute-start = (f32[128,128]{1,0:T(8,128)S(1)}, f32[128,128]{1,0:T(8,128)S(1)}, u32[]{:S(2)}, u32[]{:S(2)}) collective-permute-start(f32[128,128]{1,0:T(8,128)S(1)} %get-tuple-element.24), channel_id=1, source_target_pairs={{0,1},{1,0},{2,3},{3,2},{4,5},{5,4},{6,7},{7,6},{8,9},{9,8},{10,11... | collective-permute-start | bytes 196616 | tf_op jit(solution)/shard_map/ppermute | solution.py:411

commit v6 on v5

--- a/solution.py
+++ b/solution.py
@@ -14,6 +14,7 @@
 LIMIT = (G // 3) ** 2
 REACH = G // 3
 ROWS = 176
+CUBE, REST = 8, 16
 PIECE = SLICES * 4
 
 FRESNEL_RATE = 0.00019
@@ -65,22 +66,33 @@
 
 
 def natural(place):
-    return place & (G // 2 - 1)
+    return place
 
 
 def mixed(place):
-    n = 2 * natural(place)
-    return jnp.where(n < G // 2, n, n - (G // 2 - 1))
-
-
-def folded(place, order):
-    factor = jnp.where(place == G // 2, G // 2, order(place))
-    return factor, jnp.where(place > G // 2, -(G // 4), 0)
+    n = place >> 6
+    for source, target in ((5, 5), (4, 2), (3, 0), (2, 4), (1, 3), (0, 1)):
+        n = n + (((place >> source) & 1) << (target + 1))
+    return n
 
 
 def position(place, order):
-    n = order(place)
-    return jnp.where(place < G // 2, n, jnp.where(place == G // 2, G // 2, -n))
+    n = order(place & (G // 2 - 1))
+    return jnp.where(place < G // 2, n, G - 1 - n)
+
+
+def folded(order, axis):
+    place = iota((8, G) if axis else (G, K), axis)
+    factor = 2 * order(place & (G // 2 - 1)) + 1
+    return factor, jnp.where(place < G // 2, 0, -(G // 2))
+
+
+def spread(value, shape):
+    for axis in range(2):
+        times = shape[axis] // value.shape[axis]
+        if times > 1:
+            value = jnp.concatenate([value] * times, axis=axis)
+    return value
 
 
 def signed(index, length):
@@ -88,8 +100,8 @@
 
 
 def forward_table(shape, frequency, order, axis):
-    factor, offset = folded(iota(shape, axis), order)
-    return cosine_step(frequency(iota(shape, 1 - axis)) * factor + offset, G)
+    factor, offset = (spread(value, shape) for value in folded(order, axis))
+    return cosine_step(frequency(iota(shape, 1 - axis)) * factor + offset, 2 * G)
 
 
 def fresnel(shape, frequency_u, frequency_v):
@@ -102,7 +114,7 @@
 
 def copies_kernel(potential_ref, out_ref):
     values = potential_ref[0]
-    pick = ((iota((K, K), 0) + iota((K, K), 1)) & (K - 1)) == 0
+    pick = iota((K, K), 0) + iota((K, K), 1) == K - 1
     mirror = jnp.where(pick, 1.0, 0.0)
     quarters = [values[:, K * i : K * (i + 1)] for i in range(4)]
     for i in (1, 3):
@@ -135,7 +147,7 @@
 
 
 def whole(index):
-    return index
+    return signed(index, G)
 
 
 def centred(index):
@@ -146,7 +158,7 @@
     tilt_ref, places_ref, tilts_ref, weight_ref, coef_ref, table_ref, factor_ref, across_ref
 ):
     across_ref[0], across_ref[1] = circle(tilt_ref[0] * position(iota((G, K), 0), mixed), G)
-    factor_ref[0], factor_ref[1] = fresnel((ROWS, G), near, lambda index: signed(index, G))
+    factor_ref[0], factor_ref[1] = fresnel((ROWS, G), near, whole)
 
     probes = places_ref.shape[0]
     beams = tilts_ref.shape[1]
@@ -157,7 +169,7 @@
     coef_ref[1] = cosine * weight_im + sine * weight_re
 
     m, other = iota((2 * K, 2 * K), 0), iota((2 * K, 2 * K), 1)
-    turn = 2 * (m >> 1) * centred(other & (K - 1)) + (G // 4) * ((other >> 7) - (m & 1))
+    turn = (4 * (m >> 1) + 1) * centred(other & (K - 1)) + K * ((other >> 7) - (m & 1))
     left, right = iota((K, 2 * K), 0), iota((K, 2 * K), 1)
     for (row, rows, columns), table in (
         (AHEAD_LEFT, forward_table((ROWS, G), near, mixed, 1)),
@@ -165,8 +177,8 @@
         (BACK_RIGHT, forward_table((G, G), whole, natural, 1)),
         (BACK_LEFT, forward_table((G, G), near, mixed, 0)),
         (CROP_LEFT, forward_table((K, G), centred, mixed, 1)),
-        (IMAGE_RIGHT, cosine_step(2 * left * (right & (K - 1)) - (G // 4) * (right >> 7), G)),
-        (IMAGE_LEFT, cosine_step(turn, G)),
+        (IMAGE_RIGHT, cosine_step(signed(left, K) * (4 * (right & (K - 1)) + 1) - K * (right >> 7), 2 * G)),
+        (IMAGE_LEFT, cosine_step(turn, 2 * G)),
     ):
         high, low = split(table)
         table_ref[row : row + rows, :columns] = high
@@ -200,24 +212,12 @@
     return lax.slice_in_dim(value, 0, half, axis=axis), lax.slice_in_dim(value, half, 2 * half, axis=axis)
 
 
-def alone(first, others, axis):
-    if axis:
-        return jnp.where(iota(others.shape, 1) == 0, first, others)
-    head = jnp.where(iota((8, others.shape[1]), 0) == 0, first[:8], others[:8])
-    return jnp.concatenate([head, others[8:]], axis=0)
-
-
 def fold(real, imag, axis):
     real_ahead, real_back = halves(real, axis)
     imag_ahead, imag_back = halves(imag, axis)
-    real_odd, imag_odd = real_back - real_ahead, imag_ahead - imag_back
     return (
-        jnp.concatenate(
-            [alone(real_ahead, real_ahead + real_back, axis), alone(real_back, imag_odd, axis)], axis=axis
-        ),
-        jnp.concatenate(
-            [alone(imag_ahead, imag_ahead + imag_back, axis), alone(imag_back, real_odd, axis)], axis=axis
-        ),
+        jnp.concatenate([real_ahead + real_back, imag_ahead - imag_back], axis=axis),
+        jnp.concatenate([imag_ahead + imag_back, real_back - real_ahead], axis=axis),
     )
 
 
@@ -225,14 +225,8 @@
     real_even, real_odd = halves(real, axis)
     imag_even, imag_odd = halves(imag, axis)
     return (
-        jnp.concatenate(
-            [alone(real_even, real_even - imag_odd, axis), alone(real_odd, real_even + imag_odd, axis)],
-            axis=axis,
-        ),
-        jnp.concatenate(
-            [alone(imag_even, imag_even + real_odd, axis), alone(imag_odd, imag_even - real_odd, axis)],
-            axis=axis,
-        ),
+        jnp.concatenate([real_even - imag_odd, real_even + imag_odd], axis=axis),
+        jnp.concatenate([imag_even + real_odd, imag_even - real_odd], axis=axis),
     )
 
 
@@ -247,17 +241,23 @@
 
 
 def screened(real, imag, potential_ref, layer):
-    count = G // 4
-
     def rows(half, parity, side):
-        at = PIECE * count * half + 4 * layer + 2 * parity + side
-        return potential_ref[pl.ds(at, count, PIECE), :]
-
-    def block(half, parity):
-        values = jnp.concatenate([rows(half, parity, side) for side in range(2)], axis=1)
-        return pltpu.roll(values, 1, 0) if half and not parity else values
-
-    potential = jnp.concatenate([block(half, parity) for half in range(2) for parity in range(2)], axis=0)
+        places = [
+            (CUBE - 1 - k if half else k) * REST + (REST // 2 if half else 0) for k in range(CUBE)
+        ]
+        own = 4 * layer + 2 * (1 - parity if half else parity) + side
+        return jnp.concatenate(
+            [potential_ref[pl.ds(PIECE * place + own, REST // 2, PIECE), :] for place in places], axis=0
+        )
+
+    potential = jnp.concatenate(
+        [
+            jnp.concatenate([rows(half, parity, side) for side in range(2)], axis=1)
+            for half in range(2)
+            for parity in range(2)
+        ],
+        axis=0,
+    )
     turned = potential - math.pi / 2
     sine, cosine = cosine_of(turned), sine_of(turned)
     return -(real * cosine + imag * sine), real * sine - imag * cosine
@@ -379,7 +379,7 @@
 
 
 def per_device(groups, potential, tilts, aperture, positions):
-    near, far = groups
+    far, near = groups
     devices = lax.axis_size("beam")
     pairs, cores = lax.axis_size("pair"), lax.axis_size("core")
     configs = pairs * cores
@@ -388,12 +388,11 @@
     own = lax.axis_index("beam")
     slab = lax.axis_index(("pair", "core"))
 
-    copies = copies_of(potential, len(near[0]))
-    part = lax.all_to_all(copies, "beam", 0, 0, axis_index_groups=near, tiled=True)
+    part = lax.all_to_all(copies_of(potential, REST), "beam", 0, 0, axis_index_groups=far, tiled=True)
     part, tilts, aperture, positions = lax.optimization_barrier((part, tilts, aperture, positions))
-    part = part.reshape(len(near[0]) * PIECE, K)
+    part = part.reshape(REST * PIECE, K)
     whole = lax.all_to_all(
-        jnp.broadcast_to(part[None], (len(far[0]), *part.shape)), "beam", 0, 0, axis_index_groups=far
+        jnp.broadcast_to(part[None], (CUBE, *part.shape)), "beam", 0, 0, axis_index_groups=near
     ).reshape(devices * PIECE, K)
 
     places = positions.reshape(configs, quarter, 2)
@@ -411,14 +410,30 @@
     return mine + lax.ppermute(other, "core", [(0, 1), (1, 0)])
 
 
+def spread_bits(value, targets):
+    return sum(((value >> source) & 1) << target for source, target in enumerate(reversed(targets)))
+
+
+def exchange_groups():
+    low, high = (5, 2, 0), (4, 3, 1)
+    half = range(REST // 2)
+    far = [
+        [spread_bits(k, low) + spread_bits(j, high) for j in half]
+        + [64 + spread_bits(k, low) + spread_bits(j, high) for j in reversed(half)]
+        for k in range(CUBE)
+    ]
+    near = [
+        [top + spread_bits(k, low) + spread_bits(j, high) for k in range(CUBE)]
+        for top in (0, 64)
+        for j in half
+    ]
+    return far, near
+
+
 def solution(mesh):
     fine = jax.sharding.Mesh(mesh.devices.reshape(-1, 2, 2), ("beam", "pair", "core"))
-    nx, run = 4, mesh.devices.shape[0] // 4
-    near = [[x * run + i for i in (range(run) if 2 * x < nx else reversed(range(run)))] for x in range(nx)]
-    order = [*range(nx // 2), *reversed(range(nx // 2, nx))]
-    far = [[x * run + i for x in order] for i in range(run)]
     return jax.shard_map(
-        functools.partial(per_device, (near, far)),
+        functools.partial(per_device, exchange_groups()),
         mesh=fine,
         in_specs=(P(("pair", "core"), None, "beam"), P(), P(), P()),
         out_specs=P(("pair", "core"), "beam"),

time: 81.8 us -> 81.7 us (level)
  blocking collectives: 27.9 us -> 53.2 us
  starting transfers between devices: 22.2 us -> 9.26 us
  waiting for transfers between devices: 19.5 us -> 7.69 us
    all_to_all x0 -> x1, blocking collectives: none -> 24.5 us  [per_device(): lax.all_to_all(copies_of(potential, REST), 'beam', 0, 0, axis_index_group...]
    all_to_all x2 -> x1, starting transfers between devices: 17.1 us -> 3.63 us  [per_device(): lax.all_to_all(jnp.broadcast_to(part[None], (CUBE, *part.shape)), 'beam',...]
    all_to_all x2 -> x1, waiting for transfers between devices: 18.6 us -> 6.81 us  [per_device(): lax.all_to_all(jnp.broadcast_to(part[None], (CUBE, *part.shape)), 'beam',...]
  transfers between devices with their start and end apart: 3 -> 2, of which waited for: 3 -> 2; matrix products, arithmetic and copies ran while one was open for 1% -> 1% of each run, Pallas kernels for 3% -> 3%
where the time goes in v6:
time: 81.7 us; the launch traced here: 81.4 us
  blocking collectives  53.2 us (65%)
  starting transfers between devices  9.26 us (11%)
  Pallas kernels  8.39 us (10%)
  waiting for transfers between devices  7.69 us (9%)
  local copies, waits for them, and re-layouts  2.06 us (3%)
    all_to_all x1, blocking collectives, per_device(): lax.all_to_all(rows, ('pair', 'beam'), 0, 0, tiled=True)  28.7 us
    all_to_all x1, blocking collectives, per_device(): lax.all_to_all(copies_of(potential, REST), 'beam', 0, 0, axis_index_group...  24.5 us
    all_to_all x1, waiting for transfers between devices, per_device(): lax.all_to_all(jnp.broadcast_to(part[None], (CUBE, *part.shape)), 'beam',...  6.81 us
    ppermute x1, starting transfers between devices, per_device(): return mine + lax.ppermute(other, 'core', [(0, 1), (1, 0)])  5.63 us
    pallas_call x1, Pallas kernels, propagate(): pl.pallas_call(propagate_kernel, out_shape=shape_of(F32, 2 * K, K), in_sp...  4.94 us
    all_to_all x1, starting transfers between devices, per_device(): lax.all_to_all(jnp.broadcast_to(part[None], (CUBE, *part.shape)), 'beam',...  3.63 us
    pallas_call x1, Pallas kernels, prepare(): pl.pallas_call(prepare_kernel, out_shape=out, in_specs=[SMEM] + [VMEM] *...  2.84 us
  transfers between devices with their start and end apart: 2, of which 2 were waited for; matrix products, arithmetic and copies ran while one was open for 1% of the time, Pallas kernels for 3%

profile of v6, /device:TPU:1, one launch (start us, length us, event | category | flops | bytes accessed | tf_op | source)
XLA Modules:
  0.0 81.4 jit_solution(1238414487960033347)
XLA Ops:
  0.0 0.0 copy-start.1
  0.0 0.0 copy-start.2
  0.0 0.0 copy-start
  0.0 0.7 copy.8.potential_ref
  0.7 0.2 copies.1
  1.0 24.5 %all_to_all.15 = f32[48,4,128]{2,1,0:T(4,128)S(1)} all-to-all(f32[48,4,128]{2,1,0:T(4,128)S(1)} %copies.1), channel_id=1, replica_groups={{0,8,32,40,64,72,96,104,360,352,328,320,296,288,264,256},{4,12,36,44,68..., dimensions={0} | all-to-all | bytes 196608 | tf_op jit(solution)/shard_map/all_to_all | solution.py:391
  25.5 0.9 %broadcast_in_dim.15 = f32[8,192,128]{2,1,0:T(8,128)} broadcast(f32[192,128]{1,0:T(8,128)S(1)} %bitcast.28), dimensions={1,2} | broadcast | bytes 884736 | tf_op jit(solution)/shard_map/broadcast_in_dim | solution.py:395
  26.4 3.6 %all-to-all-start.1 = ((f32[8,192,128]{2,1,0:T(8,128)}), f32[8,192,128]{2,1,0:T(8,128)S(1)}, u32[]{:S(2)}, u32[]{:S(2)}) async-start(f32[8,192,128]{2,1,0:T(8,128)} %broadcast_in_dim.15), calls=%async_computation.1 | async-start | bytes 1572864 | tf_op jit(solution)/shard_map/all_to_all | solution.py:394
  30.0 0.0 copy-done.1
  30.1 0.1 copy.11.places_ref
  30.2 0.0 copy-done
  30.2 0.2 dynamic-slice_reduce_fusion.tilt_ref
  30.4 0.0 copy-done.2
  30.5 2.8 %prepare.1 = (f32[2,256,128]{2,1,0:T(8,128)S(1)}, bf16[1456,512]{1,0:T(8,128)(2,1)S(1)}, f32[2,176,256]{2,1,0:T(8,128)S(1)}, f32[2,256,128]{2,1,0:T(8,128)S(1)}) custom-call(s32[2]{0:T(128)S(1)} %dynamic-slice_reduce_fusion.tilt_ref, s32[256,2]{1,0:T(8,128)S(1)} %copy.11.places_ref, s32[2,128]{1,0:T(2,128)S(1)} %bitcast.26, ...), custom_call_target="tpu_custom_call" | custom-call | tf_op jit(solution)/shard_map/prepare/pallas_call | solution.py:337
  33.4 6.8 %all-to-all-done.1 = f32[8,192,128]{2,1,0:T(8,128)S(1)} async-done(((f32[8,192,128]{2,1,0:T(8,128)}), f32[8,192,128]{2,1,0:T(8,128)S(1)}, u32[]{:S(2)}, u32[]{:S(2)}) %all-to-all-start.1) | async-done | bytes 786464 | tf_op jit(solution)/shard_map/all_to_all | solution.py:394
  40.2 4.9 %propagate.1 = f32[256,128]{1,0:T(8,128)S(1)} custom-call(s32[2]{0:T(128)S(1)} %dynamic-slice_reduce_fusion.tilt_ref, f32[1536,128]{1,0:T(8,128)S(1)} %bitcast.23, bf16[1456,512]{1,0:T(8,128)(2,1)S(1)} %get-tuple-element.19.table_ref, f32[2,176,256]{2,1,0:T(8,128)S(1)} %get-tuple-element.20.factor_ref, f32[2,256,128]{2,1,0:T(8,128)S(1)} %get-tuple-element.21.across_ref), custom_call_target="tpu_custom_call" | custom-call | tf_op jit(solution)/shard_map/propagate/pallas_call | solution.py:348
  45.1 0.1 broadcast_in_dim.17
  45.2 28.7 %all_to_all.16 = f32[256,2,128]{2,1,0:T(2,128)S(1)} all-to-all(f32[256,2,128]{2,1,0:T(2,128)S(1)} %bitcast.27), channel_id=1, replica_groups=mesh['beam'=128,'pair'=2,'core'=2] {'pair','beam'}, dimensions={0} | all-to-all | bytes 524288 | tf_op jit(solution)/shard_map/all_to_all | solution.py:408
  73.9 0.4 probe.1
  74.2 5.6 %collective-permute-start = (f32[128,128]{1,0:T(8,128)S(1)}, f32[128,128]{1,0:T(8,128)S(1)}, u32[]{:S(2)}, u32[]{:S(2)}) collective-permute-start(f32[128,128]{1,0:T(8,128)S(1)} %get-tuple-element.24), channel_id=1, source_target_pairs={{0,1},{1,0},{2,3},{3,2},{4,5},{5,4},{6,7},{7,6},{8,9},{9,8},{10,11... | collective-permute-start | bytes 196616 | tf_op jit(solution)/shard_map/ppermute | solution.py:410
  79.9 0.9 %collective-permute-done = f32[128,128]{1,0:T(8,128)S(1)} collective-permute-done((f32[128,128]{1,0:T(8,128)S(1)}, f32[128,128]{1,0:T(8,128)S(1)}, u32[]{:S(2)}, u32[]{:S(2)}) %collective-permute-start) | collective-permute-done | bytes 65568 | tf_op jit(solution)/shard_map/ppermute | solution.py:410
  80.8 0.6 add.25
  (5 shorter events, 0.1 us)
Async XLA Ops:
  0.0 30.0 %copy-start.1 = (s32[512,2]{0,1:T(2,128)S(1)}, s32[512,2]{0,1:T(2,128)}, u32[]{:S(2)}) copy-start(s32[512,2]{0,1:T(2,128)} %param.7) | copy-start | bytes 12292
  0.0 30.4 %copy-start.2 = (s32[128]{0:T(128)S(1)}, s32[128]{0:T(128)}, u32[]{:S(2)}) copy-start(s32[128]{0:T(128)} %param.6) | copy-start | bytes 1540
  0.0 30.2 %copy-start = (s32[128,2]{0,1:T(2,128)S(1)}, s32[128,2]{0,1:T(2,128)}, u32[]{:S(2)}) copy-start(s32[128,2]{0,1:T(2,128)} %param.5) | copy-start | bytes 3076
  26.4 13.8 %all-to-all-start.1 = ((f32[8,192,128]{2,1,0:T(8,128)}), f32[8,192,128]{2,1,0:T(8,128)S(1)}, u32[]{:S(2)}, u32[]{:S(2)}) async-start(f32[8,192,128]{2,1,0:T(8,128)} %broadcast_in_dim.15), calls=%async_computation.1 | async-start | bytes 1572864 | tf_op jit(solution)/shard_map/all_to_all | solution.py:394
  74.2 6.5 %collective-permute-start = (f32[128,128]{1,0:T(8,128)S(1)}, f32[128,128]{1,0:T(8,128)S(1)}, u32[]{:S(2)}, u32[]{:S(2)}) collective-permute-start(f32[128,128]{1,0:T(8,128)S(1)} %get-tuple-element.24), channel_id=1, source_target_pairs={{0,1},{1,0},{2,3},{3,2},{4,5},{5,4},{6,7},{7,6},{8,9},{9,8},{10,11... | collective-permute-start | bytes 196616 | tf_op jit(solution)/shard_map/ppermute | solution.py:410

commit v7 on v6

--- a/solution.py
+++ b/solution.py
@@ -379,7 +379,6 @@
 
 
 def per_device(groups, potential, tilts, aperture, positions):
-    far, near = groups
     devices = lax.axis_size("beam")
     pairs, cores = lax.axis_size("pair"), lax.axis_size("core")
     configs = pairs * cores
@@ -388,12 +387,10 @@
     own = lax.axis_index("beam")
     slab = lax.axis_index(("pair", "core"))
 
-    part = lax.all_to_all(copies_of(potential, REST), "beam", 0, 0, axis_index_groups=far, tiled=True)
-    part, tilts, aperture, positions = lax.optimization_barrier((part, tilts, aperture, positions))
-    part = part.reshape(REST * PIECE, K)
-    whole = lax.all_to_all(
-        jnp.broadcast_to(part[None], (CUBE, *part.shape)), "beam", 0, 0, axis_index_groups=near
-    ).reshape(devices * PIECE, K)
+    pieces = lax.all_to_all(
+        copies_of(potential, devices), "beam", 0, 0, axis_index_groups=groups, tiled=True
+    )
+    whole = pieces.reshape(devices * PIECE, K)
 
     places = positions.reshape(configs, quarter, 2)
     places = jnp.concatenate([places[slab], places[slab ^ 1]], axis=0)
@@ -422,12 +419,7 @@
         + [64 + spread_bits(k, low) + spread_bits(j, high) for j in reversed(half)]
         for k in range(CUBE)
     ]
-    near = [
-        [top + spread_bits(k, low) + spread_bits(j, high) for k in range(CUBE)]
-        for top in (0, 64)
-        for j in half
-    ]
-    return far, near
+    return [sum(far, [])]
 
 
 def solution(mesh):

time: 81.7 us -> 84.3 us (1.032)
  blocking collectives: 53.2 us -> 28.6 us
  starting transfers between devices: 9.26 us -> 23.1 us
  waiting for transfers between devices: 7.69 us -> 21 us
  Pallas kernels: 8.39 us -> 9.36 us
  local copies, waits for them, and re-layouts: 2.06 us -> 1.14 us
    all_to_all x1 -> x0, blocking collectives: 24.5 us -> none  [per_device(): lax.all_to_all(copies_of(potential, REST), 'beam', 0, 0, axis_index_group...]
    all_to_all x1, starting transfers between devices: 3.63 us -> 17.8 us  [per_device(): lax.all_to_all(copies_of(potential, devices), 'beam', 0, 0, axis_index_gr...]
    all_to_all x1, waiting for transfers between devices: 6.81 us -> 20.1 us  [per_device(): lax.all_to_all(copies_of(potential, devices), 'beam', 0, 0, axis_index_gr...]
    pallas_call x1, Pallas kernels: 0.23 us -> 1.2 us  [copies_of(): pl.pallas_call(copies_kernel, out_shape=shape_of(F32, count * SLICES, 4,...]
    broadcast_in_dim x1 -> x0, local copies, waits for them, and re-layouts: 0.93 us -> none  [per_device(): jnp.broadcast_to(part[None], (CUBE, *part.shape))]
where the time goes in v7:
time: 84.3 us; the launch traced here: 84 us
  blocking collectives  28.6 us (34%)
  starting transfers between devices  23.1 us (27%)
  waiting for transfers between devices  21 us (25%)
  Pallas kernels  9.36 us (11%)
  local copies, waits for them, and re-layouts  1.14 us (1%)
    all_to_all x1, blocking collectives, per_device(): lax.all_to_all(rows, ('pair', 'beam'), 0, 0, tiled=True)  28.6 us
    all_to_all x1, waiting for transfers between devices, per_device(): lax.all_to_all(copies_of(potential, devices), 'beam', 0, 0, axis_index_gr...  20.1 us
    all_to_all x1, starting transfers between devices, per_device(): lax.all_to_all(copies_of(potential, devices), 'beam', 0, 0, axis_index_gr...  17.8 us
    ppermute x1, starting transfers between devices, per_device(): return mine + lax.ppermute(other, 'core', [(0, 1), (1, 0)])  5.35 us
    pallas_call x1, Pallas kernels, propagate(): pl.pallas_call(propagate_kernel, out_shape=shape_of(F32, 2 * K, K), in_sp...  4.94 us
    pallas_call x1, Pallas kernels, prepare(): pl.pallas_call(prepare_kernel, out_shape=out, in_specs=[SMEM] + [VMEM] *...  2.84 us
  transfers between devices with their start and end apart: 2, of which 2 were waited for; matrix products, arithmetic and copies ran while one was open for 1% of the time, Pallas kernels for 3%

profile of v7, /device:TPU:1, one launch (start us, length us, event | category | flops | bytes accessed | tf_op | source)
XLA Modules:
  0.0 84.0 jit_solution(7620254204182922154)
XLA Ops:
  0.0 0.0 copy-start.1
  0.0 0.0 copy-start
  0.0 0.0 copy-start.2
  0.0 0.7 copy.8.potential_ref
  0.7 1.2 %copies.1 = f32[384,4,128]{2,1,0:T(4,128)} custom-call(f32[1,3,512]{2,1,0:T(4,128)S(1)} %copy.8.potential_ref), custom_call_target="tpu_custom_call" | custom-call | tf_op jit(solution)/shard_map/copies/pallas_call | solution.py:371
  1.9 17.8 %all-to-all-start = ((f32[384,4,128]{2,1,0:T(4,128)}), f32[384,4,128]{2,1,0:T(4,128)S(1)}, u32[]{:S(2)}, u32[]{:S(2)}) async-start(f32[384,4,128]{2,1,0:T(4,128)} %copies.1), calls=%async_computation | async-start | bytes 1572864 | tf_op jit(solution)/shard_map/all_to_all | solution.py:390
  19.7 0.0 copy-done.1
  19.8 0.1 copy.11.places_ref
  19.9 0.0 copy-done
  19.9 0.2 dynamic-slice_reduce_fusion.tilt_ref
  20.1 0.0 copy-done.2
  20.2 2.8 %prepare.1 = (f32[2,256,128]{2,1,0:T(8,128)S(1)}, bf16[1456,512]{1,0:T(8,128)(2,1)S(1)}, f32[2,176,256]{2,1,0:T(8,128)S(1)}, f32[2,256,128]{2,1,0:T(8,128)S(1)}) custom-call(s32[2]{0:T(128)S(1)} %dynamic-slice_reduce_fusion.tilt_ref, s32[256,2]{1,0:T(8,128)S(1)} %copy.11.places_ref, s32[2,128]{1,0:T(2,128)S(1)} %bitcast.25, ...), custom_call_target="tpu_custom_call" | custom-call | tf_op jit(solution)/shard_map/prepare/pallas_call | solution.py:337
  23.1 20.1 %all-to-all-done = f32[384,4,128]{2,1,0:T(4,128)S(1)} async-done(((f32[384,4,128]{2,1,0:T(4,128)}), f32[384,4,128]{2,1,0:T(4,128)S(1)}, u32[]{:S(2)}, u32[]{:S(2)}) %all-to-all-start) | async-done | bytes 786464 | tf_op jit(solution)/shard_map/all_to_all | solution.py:390
  43.2 4.9 %propagate.1 = f32[256,128]{1,0:T(8,128)S(1)} custom-call(s32[2]{0:T(128)S(1)} %dynamic-slice_reduce_fusion.tilt_ref, f32[1536,128]{1,0:T(8,128)S(1)} %bitcast.22, bf16[1456,512]{1,0:T(8,128)(2,1)S(1)} %get-tuple-element.11.table_ref, f32[2,176,256]{2,1,0:T(8,128)S(1)} %get-tuple-element.12.factor_ref, f32[2,256,128]{2,1,0:T(8,128)S(1)} %get-tuple-element.13.across_ref), custom_call_target="tpu_custom_call" | custom-call | tf_op jit(solution)/shard_map/propagate/pallas_call | solution.py:348
  48.1 0.1 broadcast_in_dim.8
  48.2 28.6 %all_to_all.10 = f32[256,2,128]{2,1,0:T(2,128)S(1)} all-to-all(f32[256,2,128]{2,1,0:T(2,128)S(1)} %bitcast.26), channel_id=1, replica_groups=mesh['beam'=128,'pair'=2,'core'=2] {'pair','beam'}, dimensions={0} | all-to-all | bytes 524288 | tf_op jit(solution)/shard_map/all_to_all | solution.py:405
  76.8 0.4 probe.1
  77.2 5.3 %collective-permute-start = (f32[128,128]{1,0:T(8,128)S(1)}, f32[128,128]{1,0:T(8,128)S(1)}, u32[]{:S(2)}, u32[]{:S(2)}) collective-permute-start(f32[128,128]{1,0:T(8,128)S(1)} %get-tuple-element.16), channel_id=1, source_target_pairs={{0,1},{1,0},{2,3},{3,2},{4,5},{5,4},{6,7},{7,6},{8,9},{9,8},{10,11... | collective-permute-start | bytes 196616 | tf_op jit(solution)/shard_map/ppermute | solution.py:407
  82.5 0.9 %collective-permute-done = f32[128,128]{1,0:T(8,128)S(1)} collective-permute-done((f32[128,128]{1,0:T(8,128)S(1)}, f32[128,128]{1,0:T(8,128)S(1)}, u32[]{:S(2)}, u32[]{:S(2)}) %collective-permute-start) | collective-permute-done | bytes 65568 | tf_op jit(solution)/shard_map/ppermute | solution.py:407
  83.4 0.6 add.25
  (5 shorter events, 0.1 us)
Async XLA Ops:
  0.0 19.7 %copy-start.1 = (s32[512,2]{0,1:T(2,128)S(1)}, s32[512,2]{0,1:T(2,128)}, u32[]{:S(2)}) copy-start(s32[512,2]{0,1:T(2,128)} %param.7) | copy-start | bytes 12292
  0.0 19.9 %copy-start = (s32[128,2]{0,1:T(2,128)S(1)}, s32[128,2]{0,1:T(2,128)}, u32[]{:S(2)}) copy-start(s32[128,2]{0,1:T(2,128)} %param.5) | copy-start | bytes 3076
  0.0 20.1 %copy-start.2 = (s32[128]{0:T(128)S(1)}, s32[128]{0:T(128)}, u32[]{:S(2)}) copy-start(s32[128]{0:T(128)} %param.6) | copy-start | bytes 1540
  1.9 41.2 %all-to-all-start = ((f32[384,4,128]{2,1,0:T(4,128)}), f32[384,4,128]{2,1,0:T(4,128)S(1)}, u32[]{:S(2)}, u32[]{:S(2)}) async-start(f32[384,4,128]{2,1,0:T(4,128)} %copies.1), calls=%async_computation | async-start | bytes 1572864 | tf_op jit(solution)/shard_map/all_to_all | solution.py:390
  77.2 6.2 %collective-permute-start = (f32[128,128]{1,0:T(8,128)S(1)}, f32[128,128]{1,0:T(8,128)S(1)}, u32[]{:S(2)}, u32[]{:S(2)}) collective-permute-start(f32[128,128]{1,0:T(8,128)S(1)} %get-tuple-element.16), channel_id=1, source_target_pairs={{0,1},{1,0},{2,3},{3,2},{4,5},{5,4},{6,7},{7,6},{8,9},{9,8},{10,11... | collective-permute-start | bytes 196616 | tf_op jit(solution)/shard_map/ppermute | solution.py:407

commit v8 on v6

--- a/solution.py
+++ b/solution.py
@@ -389,11 +389,6 @@
     slab = lax.axis_index(("pair", "core"))
 
     part = lax.all_to_all(copies_of(potential, REST), "beam", 0, 0, axis_index_groups=far, tiled=True)
-    part, tilts, aperture, positions = lax.optimization_barrier((part, tilts, aperture, positions))
-    part = part.reshape(REST * PIECE, K)
-    whole = lax.all_to_all(
-        jnp.broadcast_to(part[None], (CUBE, *part.shape)), "beam", 0, 0, axis_index_groups=near
-    ).reshape(devices * PIECE, K)
 
     places = positions.reshape(configs, quarter, 2)
     places = jnp.concatenate([places[slab], places[slab ^ 1]], axis=0)
@@ -402,6 +397,11 @@
     weight = jnp.stack([jnp.cos(DEFOCUS_RATE * square) * amount, -jnp.sin(DEFOCUS_RATE * square) * amount])
     tilt = lax.dynamic_index_in_dim(tilts, own, 0, keepdims=False)
     coef, *tables = prepare(tilt, places, tilts.T, weight)
+    part, coef, *tables = lax.optimization_barrier((part, coef, *tables))
+    part = part.reshape(REST * PIECE, K)
+    whole = lax.all_to_all(
+        jnp.broadcast_to(part[None], (CUBE, *part.shape)), "beam", 0, 0, axis_index_groups=near
+    ).reshape(devices * PIECE, K)
     image = propagate(tilt, whole, *tables)
 
     rows = jnp.broadcast_to(image.reshape(1, K, 2, K), (pairs, K, 2, K)).reshape(pairs * K, 2, K)

time: 81.7 us -> 83.2 us (1.018)
  starting transfers between devices: 9.26 us -> 19.8 us
  blocking collectives: 53.2 us -> 43.6 us
  waiting for transfers between devices: 7.69 us -> 4.98 us
  other arithmetic: 0.74 us -> 2.15 us
  local copies, waits for them, and re-layouts: 2.06 us -> 3.19 us
    all_to_all x1, blocking collectives: 24.5 us -> 13.7 us  [per_device(): lax.all_to_all(jnp.broadcast_to(part[None], (CUBE, *part.shape)), 'beam',...]
    all_to_all x1, starting transfers between devices: 3.63 us -> 13.8 us  [per_device(): lax.all_to_all(copies_of(potential, REST), 'beam', 0, 0, axis_index_group...]
    all_to_all x1, waiting for transfers between devices: 6.81 us -> 4.1 us  [per_device(): lax.all_to_all(copies_of(potential, REST), 'beam', 0, 0, axis_index_group...]
    another operation x3, other arithmetic: 0.1 us -> 1.51 us  [per_device(): jnp.stack([jnp.cos(DEFOCUS_RATE * square) * amount, -jnp.sin(DEFOCUS_RATE...]
    all_to_all x1, blocking collectives: 28.7 us -> 29.9 us  [per_device(): lax.all_to_all(rows, ('pair', 'beam'), 0, 0, tiled=True)]
    broadcast_in_dim x1, local copies, waits for them, and re-layouts: 0.93 us -> 0.05 us  [per_device(): jnp.broadcast_to(part[None], (CUBE, *part.shape))]
  transfers between devices with their start and end apart: 2 -> 2, of which waited for: 2 -> 2; matrix products, arithmetic and copies ran while one was open for 1% -> 4% of each run, Pallas kernels for 3% -> 3%
where the time goes in v8:
time: 83.2 us; the launch traced here: 82.8 us
  blocking collectives  43.6 us (52%)
  starting transfers between devices  19.8 us (24%)
  Pallas kernels  9.02 us (11%)
  waiting for transfers between devices  4.98 us (6%)
  local copies, waits for them, and re-layouts  3.19 us (4%)
  other arithmetic  2.15 us (3%)
    all_to_all x1, blocking collectives, per_device(): lax.all_to_all(rows, ('pair', 'beam'), 0, 0, tiled=True)  29.9 us
    all_to_all x1, starting transfers between devices, per_device(): lax.all_to_all(copies_of(potential, REST), 'beam', 0, 0, axis_index_group...  13.8 us
    all_to_all x1, blocking collectives, per_device(): lax.all_to_all(jnp.broadcast_to(part[None], (CUBE, *part.shape)), 'beam',...  13.7 us
    ppermute x1, starting transfers between devices, per_device(): return mine + lax.ppermute(other, 'core', [(0, 1), (1, 0)])  5.95 us
    pallas_call x1, Pallas kernels, propagate(): pl.pallas_call(propagate_kernel, out_shape=shape_of(F32, 2 * K, K), in_sp...  4.94 us
    all_to_all x1, waiting for transfers between devices, per_device(): lax.all_to_all(copies_of(potential, REST), 'beam', 0, 0, axis_index_group...  4.1 us
    pallas_call x1, Pallas kernels, prepare(): pl.pallas_call(prepare_kernel, out_shape=out, in_specs=[SMEM] + [VMEM] *...  2.84 us
  transfers between devices with their start and end apart: 2, of which 2 were waited for; matrix products, arithmetic and copies ran while one was open for 4% of the time, Pallas kernels for 3%

profile of v8, /device:TPU:1, one launch (start us, length us, event | category | flops | bytes accessed | tf_op | source)
XLA Modules:
  0.0 82.8 jit_solution(7529539114761200224)
XLA Ops:
  0.0 0.7 copy.8.potential_ref
  0.7 0.9 %copies.1 = f32[48,4,128]{2,1,0:T(4,128)} custom-call(f32[1,3,512]{2,1,0:T(4,128)S(1)} %copy.8.potential_ref), custom_call_target="tpu_custom_call" | custom-call | tf_op jit(solution)/shard_map/copies/pallas_call | solution.py:371
  1.6 13.8 %all-to-all-start = ((f32[48,4,128]{2,1,0:T(4,128)}), f32[48,4,128]{2,1,0:T(4,128)S(1)}, u32[]{:S(2)}, u32[]{:S(2)}) async-start(f32[48,4,128]{2,1,0:T(4,128)} %copies.1), calls=%async_computation | async-start | bytes 196608 | tf_op jit(solution)/shard_map/all_to_all | solution.py:391
  15.4 0.9 %dynamic-slice_reduce_fusion.tilt_ref = s32[2]{0:T(128)S(1)} fusion(s32[128,2]{0,1:T(2,128)} %param.5, s32[]{:T(128)S(6)} %select_n.10), kind=kLoop, calls=%fused_computation.4 | loop fusion | bytes 20 | tf_op jit(solution)/shard_map/jit(dynamic_index_in_dim)/dynamic_slice | solution.py:398
  16.3 0.8 fusion.1
  17.1 0.7 fusion
  17.8 0.7 dynamic-slice_bitcast_fusion.1
  18.5 0.1 copy.11.places_ref
  18.7 0.0 copy-start
  18.7 0.7 copy-done
  19.3 2.8 %prepare.1 = (f32[2,256,128]{2,1,0:T(8,128)S(1)}, bf16[1456,512]{1,0:T(8,128)(2,1)S(1)}, f32[2,176,256]{2,1,0:T(8,128)S(1)}, f32[2,256,128]{2,1,0:T(8,128)S(1)}) custom-call(s32[2]{0:T(128)S(1)} %dynamic-slice_reduce_fusion.tilt_ref, s32[256,2]{1,0:T(8,128)S(1)} %copy.11.places_ref, s32[2,128]{1,0:T(2,128)S(1)} %bitcast.26, ...), custom_call_target="tpu_custom_call" | custom-call | tf_op jit(solution)/shard_map/prepare/pallas_call | solution.py:337
  22.2 4.1 %all-to-all-done = f32[48,4,128]{2,1,0:T(4,128)S(1)} async-done(((f32[48,4,128]{2,1,0:T(4,128)}), f32[48,4,128]{2,1,0:T(4,128)S(1)}, u32[]{:S(2)}, u32[]{:S(2)}) %all-to-all-start) | async-done | bytes 98336 | tf_op jit(solution)/shard_map/all_to_all | solution.py:391
  26.3 0.1 broadcast_in_dim.15
  26.3 13.7 %all_to_all.15 = f32[8,192,128]{2,1,0:T(8,128)S(1)} all-to-all(f32[8,192,128]{2,1,0:T(8,128)S(1)} %broadcast_in_dim.15), channel_id=1, replica_groups={{0,4,16,20,128,132,144,148},{8,12,24,28,136,140,152,156},{32,36,48,52,1..., dimensions={0} | all-to-all | bytes 1572864 | tf_op jit(solution)/shard_map/all_to_all | solution.py:402
  40.0 4.9 %propagate.1 = f32[256,128]{1,0:T(8,128)S(1)} custom-call(s32[2]{0:T(128)S(1)} %dynamic-slice_reduce_fusion.tilt_ref, f32[1536,128]{1,0:T(8,128)S(1)} %bitcast.23, bf16[1456,512]{1,0:T(8,128)(2,1)S(1)} %get-tuple-element.21.table_ref, f32[2,176,256]{2,1,0:T(8,128)S(1)} %get-tuple-element.22.factor_ref, f32[2,256,128]{2,1,0:T(8,128)S(1)} %get-tuple-element.23.across_ref), custom_call_target="tpu_custom_call" | custom-call | tf_op jit(solution)/shard_map/propagate/pallas_call | solution.py:348
  45.0 0.1 broadcast_in_dim.17
  45.1 29.9 %all_to_all.16 = f32[256,2,128]{2,1,0:T(2,128)S(1)} all-to-all(f32[256,2,128]{2,1,0:T(2,128)S(1)} %bitcast.27), channel_id=1, replica_groups=mesh['beam'=128,'pair'=2,'core'=2] {'pair','beam'}, dimensions={0} | all-to-all | bytes 524288 | tf_op jit(solution)/shard_map/all_to_all | solution.py:408
  75.0 0.4 probe.1
  75.3 6.0 %collective-permute-start = (f32[128,128]{1,0:T(8,128)S(1)}, f32[128,128]{1,0:T(8,128)S(1)}, u32[]{:S(2)}, u32[]{:S(2)}) collective-permute-start(f32[128,128]{1,0:T(8,128)S(1)} %get-tuple-element.26), channel_id=1, source_target_pairs={{0,1},{1,0},{2,3},{3,2},{4,5},{5,4},{6,7},{7,6},{8,9},{9,8},{10,11... | collective-permute-start | bytes 196616 | tf_op jit(solution)/shard_map/ppermute | solution.py:410
  81.3 0.9 %collective-permute-done = f32[128,128]{1,0:T(8,128)S(1)} collective-permute-done((f32[128,128]{1,0:T(8,128)S(1)}, f32[128,128]{1,0:T(8,128)S(1)}, u32[]{:S(2)}, u32[]{:S(2)}) %collective-permute-start) | collective-permute-done | bytes 65568 | tf_op jit(solution)/shard_map/ppermute | solution.py:410
  82.2 0.6 add.25
  (2 shorter events, 0.0 us)
Async XLA Ops:
  1.6 24.7 %all-to-all-start = ((f32[48,4,128]{2,1,0:T(4,128)}), f32[48,4,128]{2,1,0:T(4,128)S(1)}, u32[]{:S(2)}, u32[]{:S(2)}) async-start(f32[48,4,128]{2,1,0:T(4,128)} %copies.1), calls=%async_computation | async-start | bytes 196608 | tf_op jit(solution)/shard_map/all_to_all | solution.py:391
  18.7 0.7 copy-start
  75.3 6.8 %collective-permute-start = (f32[128,128]{1,0:T(8,128)S(1)}, f32[128,128]{1,0:T(8,128)S(1)}, u32[]{:S(2)}, u32[]{:S(2)}) collective-permute-start(f32[128,128]{1,0:T(8,128)S(1)} %get-tuple-element.26), channel_id=1, source_target_pairs={{0,1},{1,0},{2,3},{3,2},{4,5},{5,4},{6,7},{7,6},{8,9},{9,8},{10,11... | collective-permute-start | bytes 196616 | tf_op jit(solution)/shard_map/ppermute | solution.py:410

commit v9 on v8

--- a/solution.py
+++ b/solution.py
@@ -155,18 +155,31 @@
 
 
 def prepare_kernel(
-    tilt_ref, places_ref, tilts_ref, weight_ref, coef_ref, table_ref, factor_ref, across_ref
+    own_ref, slab_ref, tilt_ref, tilts_ref, aperture_ref, positions_ref, coef_ref, table_ref, factor_ref, across_ref
 ):
-    across_ref[0], across_ref[1] = circle(tilt_ref[0] * position(iota((G, K), 0), mixed), G)
+    own = own_ref[0]
+    across_ref[0], across_ref[1] = circle(tilt_ref[0, own] * position(iota((G, K), 0), mixed), G)
     factor_ref[0], factor_ref[1] = fresnel((ROWS, G), near, whole)
 
-    probes = places_ref.shape[0]
-    beams = tilts_ref.shape[1]
-    steps = places_ref[:, 0:1] * tilts_ref[0:1, :] + places_ref[:, 1:2] * tilts_ref[1:2, :]
-    sine, cosine = circle(-steps, K)
-    weight_re, weight_im = weight_ref[0:1, :], weight_ref[1:2, :]
-    coef_ref[0] = cosine * weight_re - sine * weight_im
-    coef_ref[1] = cosine * weight_im + sine * weight_re
+    tilts = tilts_ref[...]
+    beams = tilts.shape[1]
+    square = jnp.sum((tilts * tilts).astype(F32), axis=0, keepdims=True)
+    angle = -DEFOCUS_RATE * jnp.broadcast_to(square, (8, beams))
+    turns = jnp.floor(angle * (0.5 / math.pi) + 0.5)
+    half = 0.5 * ((angle - turns * 6.28125) - turns * (2.0 * math.pi - 6.28125))
+    sine, cosine = sine_of(half), cosine_of(half)
+    amount = jnp.broadcast_to(aperture_ref[...].astype(F32) * (1.0 / math.sqrt(beams)), (8, beams))
+    weight_re = spread(amount * (1.0 - 2.0 * sine * sine), (K, beams))
+    weight_im = spread(amount * (2.0 * sine * cosine), (K, beams))
+    none = jnp.zeros((6, K), F32)
+    steep = jnp.concatenate([tilts.astype(F32), none], axis=0).astype(BF16)
+    for core in range(2):
+        at = pl.multiple_of((slab_ref[0] ^ core) * K, K)
+        places = jnp.concatenate([positions_ref[:, pl.ds(at, K)].astype(F32), none], axis=0)
+        steps = jnp.dot(places.T.astype(BF16), steep, preferred_element_type=F32)
+        sine, cosine = circle(-steps.astype(jnp.int32), K)
+        coef_ref[0, K * core : K * (core + 1), :] = cosine * weight_re - sine * weight_im
+        coef_ref[1, K * core : K * (core + 1), :] = cosine * weight_im + sine * weight_re
 
     m, other = iota((2 * K, 2 * K), 0), iota((2 * K, 2 * K), 1)
     turn = (4 * (m >> 1) + 1) * centred(other & (K - 1)) + K * ((other >> 7) - (m & 1))
@@ -274,9 +287,9 @@
     return jnp.where(iota((value.shape[0], K), 1) < K // 2, value[:, :K], value[:, K:])
 
 
-def propagate_kernel(tilt_ref, potential_ref, table_ref, factor_ref, across_ref, out_ref):
+def propagate_kernel(own_ref, tilt_ref, potential_ref, table_ref, factor_ref, across_ref, out_ref):
     table = functools.partial(terms, table_ref)
-    real, imag = plane_wave(across_ref, tilt_ref[1])
+    real, imag = plane_wave(across_ref, tilt_ref[1, own_ref[0]])
     for layer in range(SLICES - 1):
         real, imag = screened(real, imag, potential_ref, layer)
         real, imag = spectrum(real, imag, table(AHEAD_LEFT), table(AHEAD_RIGHT), factor_ref)
@@ -327,9 +340,10 @@
     return jax.ShapeDtypeStruct(shape, dtype)
 
 
-def prepare(tilt, places, tilts, weight):
+def prepare(own, slab, tilts, aperture, positions):
+    beams = tilts.shape[1]
     out = [
-        shape_of(F32, 2, places.shape[0], tilts.shape[1]),
+        shape_of(F32, 2, 2 * K, beams),
         shape_of(BF16, TABLE_ROWS, 2 * G),
         shape_of(F32, 2, ROWS, G),
         shape_of(F32, 2, G, K),
@@ -337,18 +351,18 @@
     return pl.pallas_call(
         prepare_kernel,
         out_shape=out,
-        in_specs=[SMEM] + [VMEM] * 3,
+        in_specs=[SMEM] * 3 + [VMEM] * 3,
         out_specs=[VMEM] * len(out),
         compiler_params=PARAMS,
         name="prepare",
-    )(tilt, places, tilts, weight)
+    )(own, slab, tilts, tilts, aperture, positions)
 
 
 def propagate(*operands):
     return pl.pallas_call(
         propagate_kernel,
         out_shape=shape_of(F32, 2 * K, K),
-        in_specs=[SMEM] + [VMEM] * (len(operands) - 1),
+        in_specs=[SMEM] * 2 + [VMEM] * (len(operands) - 2),
         out_specs=VMEM,
         compiler_params=PARAMS,
         name="propagate",
@@ -384,25 +398,19 @@
     pairs, cores = lax.axis_size("pair"), lax.axis_size("core")
     configs = pairs * cores
     beams = tilts.shape[0]
-    quarter = positions.shape[0] // configs
-    own = lax.axis_index("beam")
-    slab = lax.axis_index(("pair", "core"))
 
     part = lax.all_to_all(copies_of(potential, REST), "beam", 0, 0, axis_index_groups=far, tiled=True)
 
-    places = positions.reshape(configs, quarter, 2)
-    places = jnp.concatenate([places[slab], places[slab ^ 1]], axis=0)
-    square = (tilts[:, 0] ** 2 + tilts[:, 1] ** 2).astype(F32)
-    amount = aperture.astype(F32) * (1.0 / math.sqrt(beams))
-    weight = jnp.stack([jnp.cos(DEFOCUS_RATE * square) * amount, -jnp.sin(DEFOCUS_RATE * square) * amount])
-    tilt = lax.dynamic_index_in_dim(tilts, own, 0, keepdims=False)
-    coef, *tables = prepare(tilt, places, tilts.T, weight)
+    own = lax.axis_index("beam").reshape(1)
+    slab = lax.axis_index(("pair", "core")).reshape(1)
+    tilts = tilts.T
+    coef, *tables = prepare(own, slab, tilts, aperture.reshape(1, beams), positions.T)
     part, coef, *tables = lax.optimization_barrier((part, coef, *tables))
     part = part.reshape(REST * PIECE, K)
     whole = lax.all_to_all(
         jnp.broadcast_to(part[None], (CUBE, *part.shape)), "beam", 0, 0, axis_index_groups=near
     ).reshape(devices * PIECE, K)
-    image = propagate(tilt, whole, *tables)
+    image = propagate(own, tilts, whole, *tables)
 
     rows = jnp.broadcast_to(image.reshape(1, K, 2, K), (pairs, K, 2, K)).reshape(pairs * K, 2, K)
     block = lax.all_to_all(rows, ("pair", "beam"), 0, 0, tiled=True).reshape(2 * pairs * beams, K)

time: 83.2 us -> 81.3 us (0.977)
  blocking collectives: 43.6 us -> 41.6 us
  waiting for transfers between devices: 4.98 us -> 6.94 us
  other arithmetic: 2.15 us -> 0.64 us
    all_to_all x1, waiting for transfers between devices: 4.1 us -> 6.06 us  [per_device(): lax.all_to_all(copies_of(potential, REST), 'beam', 0, 0, axis_index_group...]
    all_to_all x1, blocking collectives: 29.9 us -> 27.9 us  [per_device(): lax.all_to_all(rows, ('pair', 'beam'), 0, 0, tiled=True)]
    another operation x3 -> x0, other arithmetic: 1.51 us -> none  [per_device(): jnp.stack([jnp.cos(DEFOCUS_RATE * square) * amount, -jnp.sin(DEFOCUS_RATE...]
    unnamed x3 -> x9, local copies, waits for them, and re-layouts: 1.37 us -> 2.73 us
    dynamic_slice x1 -> x0, local copies, waits for them, and re-layouts: 0.87 us -> none  [per_device(): tilt = lax.dynamic_index_in_dim(tilts, own, 0, keepdims=False)]
  transfers between devices with their start and end apart: 2 -> 2, of which waited for: 2 -> 2; matrix products, arithmetic and copies ran while one was open for 4% -> 0% of each run, Pallas kernels for 3% -> 3%
where the time goes in v9:
time: 81.3 us; the launch traced here: 80.9 us
  blocking collectives  41.6 us (51%)
  starting transfers between devices  19.8 us (24%)
  Pallas kernels  8.98 us (11%)
  waiting for transfers between devices  6.94 us (9%)
  local copies, waits for them, and re-layouts  2.85 us (4%)
    all_to_all x1, blocking collectives, per_device(): lax.all_to_all(rows, ('pair', 'beam'), 0, 0, tiled=True)  27.9 us
    all_to_all x1, starting transfers between devices, per_device(): lax.all_to_all(copies_of(potential, REST), 'beam', 0, 0, axis_index_group...  13.8 us
    all_to_all x1, blocking collectives, per_device(): lax.all_to_all(jnp.broadcast_to(part[None], (CUBE, *part.shape)), 'beam',...  13.7 us
    all_to_all x1, waiting for transfers between devices, per_device(): lax.all_to_all(copies_of(potential, REST), 'beam', 0, 0, axis_index_group...  6.06 us
    ppermute x1, starting transfers between devices, per_device(): return mine + lax.ppermute(other, 'core', [(0, 1), (1, 0)])  5.95 us
    pallas_call x1, Pallas kernels, propagate(): pl.pallas_call(propagate_kernel, out_shape=shape_of(F32, 2 * K, K), in_sp...  4.96 us
    pallas_call x1, Pallas kernels, prepare(): pl.pallas_call(prepare_kernel, out_shape=out, in_specs=[SMEM] * 3 + [VMEM...  2.78 us
    unnamed x9, local copies, waits for them, and re-layouts  2.73 us
  transfers between devices with their start and end apart: 2, of which 2 were waited for; matrix products, arithmetic and copies ran while one was open for 0% of the time, Pallas kernels for 3%

profile of v9, /device:TPU:1, one launch (start us, length us, event | category | flops | bytes accessed | tf_op | source)
XLA Modules:
  0.0 80.9 jit_solution(11340450050759320788)
XLA Ops:
  0.0 0.0 copy-start.1
  0.0 0.7 copy.5.potential_ref
  0.7 0.9 %copies.1 = f32[48,4,128]{2,1,0:T(4,128)} custom-call(f32[1,3,512]{2,1,0:T(4,128)S(1)} %copy.5.potential_ref), custom_call_target="tpu_custom_call" | custom-call | tf_op jit(solution)/shard_map/copies/pallas_call | solution.py:385
  1.6 13.8 %all-to-all-start = ((f32[48,4,128]{2,1,0:T(4,128)}), f32[48,4,128]{2,1,0:T(4,128)S(1)}, u32[]{:S(2)}, u32[]{:S(2)}) async-start(f32[48,4,128]{2,1,0:T(4,128)} %copies.1), calls=%async_computation | async-start | bytes 196608 | tf_op jit(solution)/shard_map/all_to_all | solution.py:402
  15.4 0.0 copy-start
  15.4 0.7 copy-done
  16.1 0.0 copy-start.2
  16.1 0.7 copy-done.2
  16.8 0.0 copy-start.3
  16.8 0.7 copy-done.3
  17.4 2.8 %prepare.1 = (f32[2,256,128]{2,1,0:T(8,128)S(1)}, bf16[1456,512]{1,0:T(8,128)(2,1)S(1)}, f32[2,176,256]{2,1,0:T(8,128)S(1)}, f32[2,256,128]{2,1,0:T(8,128)S(1)}) custom-call(s32[1]{0:T(128)} %bitcast.own_ref, s32[1]{0:T(128)} %bitcast.2.slab_ref, s32[2,128]{1,0:T(2,128)S(1)} %bitcast.13, s32[2,128]{1,0:T(2,128)S(1)} %bitcast.14, s32[1,128]{1,0:T(1,128)S(1)} %bitcast.17, ...), custom_call_target="tpu_custom_call" | custom-call | tf_op jit(solution)/shard_map/prepare/pallas_call | solution.py:351
  20.2 6.1 %all-to-all-done = f32[48,4,128]{2,1,0:T(4,128)S(1)} async-done(((f32[48,4,128]{2,1,0:T(4,128)}), f32[48,4,128]{2,1,0:T(4,128)S(1)}, u32[]{:S(2)}, u32[]{:S(2)}) %all-to-all-start) | async-done | bytes 98336 | tf_op jit(solution)/shard_map/all_to_all | solution.py:402
  26.3 0.1 broadcast_in_dim.15
  26.4 13.7 %all_to_all.15 = f32[8,192,128]{2,1,0:T(8,128)S(1)} all-to-all(f32[8,192,128]{2,1,0:T(8,128)S(1)} %broadcast_in_dim.15), channel_id=1, replica_groups={{0,4,16,20,128,132,144,148},{8,12,24,28,136,140,152,156},{32,36,48,52,1..., dimensions={0} | all-to-all | bytes 1572864 | tf_op jit(solution)/shard_map/all_to_all | solution.py:410
  40.1 0.0 copy-done.1
  40.1 5.0 %propagate.1 = f32[256,128]{1,0:T(8,128)S(1)} custom-call(s32[1]{0:T(128)} %bitcast.own_ref, s32[2,128]{1,0:T(2,128)S(1)} %bitcast.15, f32[1536,128]{1,0:T(8,128)S(1)} %bitcast.10, bf16[1456,512]{1,0:T(8,128)(2,1)S(1)} %get-tuple-element.21.table_ref, f32[2,176,256]{2,1,0:T(8,128)S(1)} %get-tuple-element.22.factor_ref, ...), custom_call_target="tpu_custom_call" | custom-call | tf_op jit(solution)/shard_map/propagate/pallas_call | solution.py:362
  45.0 0.1 broadcast_in_dim.17
  45.1 27.9 %all_to_all.16 = f32[256,2,128]{2,1,0:T(2,128)S(1)} all-to-all(f32[256,2,128]{2,1,0:T(2,128)S(1)} %bitcast.18), channel_id=1, replica_groups=mesh['beam'=128,'pair'=2,'core'=2] {'pair','beam'}, dimensions={0} | all-to-all | bytes 524288 | tf_op jit(solution)/shard_map/all_to_all | solution.py:416
  73.0 0.4 probe.1
  73.4 6.0 %collective-permute-start = (f32[128,128]{1,0:T(8,128)S(1)}, f32[128,128]{1,0:T(8,128)S(1)}, u32[]{:S(2)}, u32[]{:S(2)}) collective-permute-start(f32[128,128]{1,0:T(8,128)S(1)} %get-tuple-element.26), channel_id=1, source_target_pairs={{0,1},{1,0},{2,3},{3,2},{4,5},{5,4},{6,7},{7,6},{8,9},{9,8},{10,11... | collective-permute-start | bytes 196616 | tf_op jit(solution)/shard_map/ppermute | solution.py:418
  79.4 0.9 %collective-permute-done = f32[128,128]{1,0:T(8,128)S(1)} collective-permute-done((f32[128,128]{1,0:T(8,128)S(1)}, f32[128,128]{1,0:T(8,128)S(1)}, u32[]{:S(2)}, u32[]{:S(2)}) %collective-permute-start) | collective-permute-done | bytes 65568 | tf_op jit(solution)/shard_map/ppermute | solution.py:418
  80.3 0.6 add.7
Async XLA Ops:
  0.0 40.1 %copy-start.1 = (s32[128,2]{0,1:T(2,128)S(1)}, s32[128,2]{0,1:T(2,128)}, u32[]{:S(2)}) copy-start(s32[128,2]{0,1:T(2,128)} %param.5) | copy-start | bytes 3076
  1.6 24.7 %all-to-all-start = ((f32[48,4,128]{2,1,0:T(4,128)}), f32[48,4,128]{2,1,0:T(4,128)S(1)}, u32[]{:S(2)}, u32[]{:S(2)}) async-start(f32[48,4,128]{2,1,0:T(4,128)} %copies.1), calls=%async_computation | async-start | bytes 196608 | tf_op jit(solution)/shard_map/all_to_all | solution.py:402
  15.4 0.7 copy-start
  16.1 0.7 copy-start.2
  16.8 0.7 copy-start.3
  73.4 6.8 %collective-permute-start = (f32[128,128]{1,0:T(8,128)S(1)}, f32[128,128]{1,0:T(8,128)S(1)}, u32[]{:S(2)}, u32[]{:S(2)}) collective-permute-start(f32[128,128]{1,0:T(8,128)S(1)} %get-tuple-element.26), channel_id=1, source_target_pairs={{0,1},{1,0},{2,3},{3,2},{4,5},{5,4},{6,7},{7,6},{8,9},{9,8},{10,11... | collective-permute-start | bytes 196616 | tf_op jit(solution)/shard_map/ppermute | solution.py:418

commit v10 on v9

--- a/solution.py
+++ b/solution.py
@@ -14,7 +14,7 @@
 LIMIT = (G // 3) ** 2
 REACH = G // 3
 ROWS = 176
-CUBE, REST = 8, 16
+NEAR, FAR = 32, 4
 PIECE = SLICES * 4
 
 FRESNEL_RATE = 0.00019
@@ -70,10 +70,7 @@
 
 
 def mixed(place):
-    n = place >> 6
-    for source, target in ((5, 5), (4, 2), (3, 0), (2, 4), (1, 3), (0, 1)):
-        n = n + (((place >> source) & 1) << (target + 1))
-    return n
+    return 2 * (place & (G // 4 - 1)) + (place >> 6)
 
 
 def position(place, order):
@@ -212,12 +209,13 @@
 
 
 def from_right(field, table):
-    high, low = split(field)
-    return jnp.dot(
-        jnp.concatenate([high, low, high], axis=1),
-        jnp.concatenate([table[0], table[0], table[1]], axis=0),
-        preferred_element_type=F32,
-    )
+    table = jnp.concatenate([table[0], table[0], table[1]], axis=0)
+
+    def product(rows):
+        high, low = split(rows)
+        return jnp.dot(jnp.concatenate([high, low, high], axis=1), table, preferred_element_type=F32)
+
+    return jnp.concatenate([product(rows) for rows in halves(field, 0)], axis=0)
 
 
 def halves(value, axis):
@@ -254,14 +252,11 @@
 
 
 def screened(real, imag, potential_ref, layer):
+    count = G // 4
+
     def rows(half, parity, side):
-        places = [
-            (CUBE - 1 - k if half else k) * REST + (REST // 2 if half else 0) for k in range(CUBE)
-        ]
         own = 4 * layer + 2 * (1 - parity if half else parity) + side
-        return jnp.concatenate(
-            [potential_ref[pl.ds(PIECE * place + own, REST // 2, PIECE), :] for place in places], axis=0
-        )
+        return potential_ref[pl.ds(PIECE * count * half + own, count, PIECE), :]
 
     potential = jnp.concatenate(
         [
@@ -393,22 +388,22 @@
 
 
 def per_device(groups, potential, tilts, aperture, positions):
-    far, near = groups
+    near, far = groups
     devices = lax.axis_size("beam")
     pairs, cores = lax.axis_size("pair"), lax.axis_size("core")
     configs = pairs * cores
     beams = tilts.shape[0]
 
-    part = lax.all_to_all(copies_of(potential, REST), "beam", 0, 0, axis_index_groups=far, tiled=True)
+    part = lax.all_to_all(copies_of(potential, NEAR), "beam", 0, 0, axis_index_groups=near, tiled=True)
 
     own = lax.axis_index("beam").reshape(1)
     slab = lax.axis_index(("pair", "core")).reshape(1)
     tilts = tilts.T
     coef, *tables = prepare(own, slab, tilts, aperture.reshape(1, beams), positions.T)
     part, coef, *tables = lax.optimization_barrier((part, coef, *tables))
-    part = part.reshape(REST * PIECE, K)
+    part = part.reshape(NEAR * PIECE, K)
     whole = lax.all_to_all(
-        jnp.broadcast_to(part[None], (CUBE, *part.shape)), "beam", 0, 0, axis_index_groups=near
+        jnp.broadcast_to(part[None], (FAR, *part.shape)), "beam", 0, 0, axis_index_groups=far
     ).reshape(devices * PIECE, K)
     image = propagate(own, tilts, whole, *tables)
 
@@ -418,24 +413,12 @@
     return mine + lax.ppermute(other, "core", [(0, 1), (1, 0)])
 
 
-def spread_bits(value, targets):
-    return sum(((value >> source) & 1) << target for source, target in enumerate(reversed(targets)))
-
-
 def exchange_groups():
-    low, high = (5, 2, 0), (4, 3, 1)
-    half = range(REST // 2)
-    far = [
-        [spread_bits(k, low) + spread_bits(j, high) for j in half]
-        + [64 + spread_bits(k, low) + spread_bits(j, high) for j in reversed(half)]
-        for k in range(CUBE)
-    ]
-    near = [
-        [top + spread_bits(k, low) + spread_bits(j, high) for k in range(CUBE)]
-        for top in (0, 64)
-        for j in half
-    ]
-    return far, near
+    run, turned = range(NEAR), range(NEAR - 1, -1, -1)
+    near = [[NEAR * x + i for i in (run if 2 * x < FAR else turned)] for x in range(FAR)]
+    order = [*range(FAR // 2), *range(FAR - 1, FAR // 2 - 1, -1)]
+    far = [[NEAR * x + i for x in order] for i in run]
+    return near, far
 
 
 def solution(mesh):

time: 81.3 us -> 78.8 us (0.969)
  blocking collectives: 41.6 us -> 40 us
    all_to_all x1, blocking collectives: 13.7 us -> 11.4 us  [per_device(): lax.all_to_all(jnp.broadcast_to(part[None], (FAR, *part.shape)), 'beam',...]
where the time goes in v10:
time: 78.8 us; the launch traced here: 78.4 us
  blocking collectives  40 us (51%)
  starting transfers between devices  19.8 us (25%)
  Pallas kernels  8.43 us (11%)
  waiting for transfers between devices  6.65 us (8%)
  local copies, waits for them, and re-layouts  2.83 us (4%)
    all_to_all x1, blocking collectives, per_device(): lax.all_to_all(rows, ('pair', 'beam'), 0, 0, tiled=True)  28.5 us
    all_to_all x1, starting transfers between devices, per_device(): lax.all_to_all(copies_of(potential, NEAR), 'beam', 0, 0, axis_index_group...  13.6 us
    all_to_all x1, blocking collectives, per_device(): lax.all_to_all(jnp.broadcast_to(part[None], (FAR, *part.shape)), 'beam',...  11.4 us
    ppermute x1, starting transfers between devices, per_device(): return mine + lax.ppermute(other, 'core', [(0, 1), (1, 0)])  6.23 us
    all_to_all x1, waiting for transfers between devices, per_device(): lax.all_to_all(copies_of(potential, NEAR), 'beam', 0, 0, axis_index_group...  5.77 us
    pallas_call x1, Pallas kernels, propagate(): pl.pallas_call(propagate_kernel, out_shape=shape_of(F32, 2 * K, K), in_sp...  4.44 us
    unnamed x9, local copies, waits for them, and re-layouts  2.71 us
    pallas_call x1, Pallas kernels, prepare(): pl.pallas_call(prepare_kernel, out_shape=out, in_specs=[SMEM] * 3 + [VMEM...  2.7 us
  transfers between devices with their start and end apart: 2, of which 2 were waited for; matrix products, arithmetic and copies ran while one was open for 0% of the time, Pallas kernels for 3%

profile of v10, /device:TPU:1, one launch (start us, length us, event | category | flops | bytes accessed | tf_op | source)
XLA Modules:
  0.0 78.4 jit_solution(17519138797600145752)
XLA Ops:
  0.0 0.7 copy.5.potential_ref
  0.7 0.9 %copies.1 = f32[96,4,128]{2,1,0:T(4,128)} custom-call(f32[1,3,512]{2,1,0:T(4,128)S(1)} %copy.5.potential_ref), custom_call_target="tpu_custom_call" | custom-call | tf_op jit(solution)/shard_map/copies/pallas_call | solution.py:380
  1.6 0.0 copy-start.1
  1.6 13.6 %all-to-all-start = ((f32[96,4,128]{2,1,0:T(4,128)}), f32[96,4,128]{2,1,0:T(4,128)S(1)}, u32[]{:S(2)}, u32[]{:S(2)}) async-start(f32[96,4,128]{2,1,0:T(4,128)} %copies.1), calls=%async_computation | async-start | bytes 393216 | tf_op jit(solution)/shard_map/all_to_all | solution.py:397
  15.2 0.0 copy-start
  15.2 0.7 copy-done
  15.9 0.0 copy-start.2
  15.9 0.7 copy-done.2
  16.6 0.0 copy-start.3
  16.6 0.7 copy-done.3
  17.2 2.7 %prepare.1 = (f32[2,256,128]{2,1,0:T(8,128)S(1)}, bf16[1456,512]{1,0:T(8,128)(2,1)S(1)}, f32[2,176,256]{2,1,0:T(8,128)S(1)}, f32[2,256,128]{2,1,0:T(8,128)S(1)}) custom-call(s32[1]{0:T(128)} %bitcast.own_ref, s32[1]{0:T(128)} %bitcast.2.slab_ref, s32[2,128]{1,0:T(2,128)S(1)} %bitcast.13, s32[2,128]{1,0:T(2,128)S(1)} %bitcast.14, s32[1,128]{1,0:T(1,128)S(1)} %bitcast.17, ...), custom_call_target="tpu_custom_call" | custom-call | tf_op jit(solution)/shard_map/prepare/pallas_call | solution.py:346
  20.0 5.8 %all-to-all-done = f32[96,4,128]{2,1,0:T(4,128)S(1)} async-done(((f32[96,4,128]{2,1,0:T(4,128)}), f32[96,4,128]{2,1,0:T(4,128)S(1)}, u32[]{:S(2)}, u32[]{:S(2)}) %all-to-all-start) | async-done | bytes 196640 | tf_op jit(solution)/shard_map/all_to_all | solution.py:397
  25.7 0.1 broadcast_in_dim.15
  25.8 11.4 %all_to_all.15 = f32[4,384,128]{2,1,0:T(8,128)S(1)} all-to-all(f32[4,384,128]{2,1,0:T(8,128)S(1)} %broadcast_in_dim.15), channel_id=1, replica_groups={{0,128,384,256},{4,132,388,260},{8,136,392,264},{12,140,396,268},{16,14..., dimensions={0} | all-to-all | bytes 1572864 | tf_op jit(solution)/shard_map/all_to_all | solution.py:405
  37.2 0.0 copy-done.1
  37.2 4.4 %propagate.1 = f32[256,128]{1,0:T(8,128)S(1)} custom-call(s32[1]{0:T(128)} %bitcast.own_ref, s32[2,128]{1,0:T(2,128)S(1)} %bitcast.15, f32[1536,128]{1,0:T(8,128)S(1)} %bitcast.10, bf16[1456,512]{1,0:T(8,128)(2,1)S(1)} %get-tuple-element.21.table_ref, f32[2,176,256]{2,1,0:T(8,128)S(1)} %get-tuple-element.22.factor_ref, ...), custom_call_target="tpu_custom_call" | custom-call | tf_op jit(solution)/shard_map/propagate/pallas_call | solution.py:357
  41.7 0.1 broadcast_in_dim.17
  41.7 28.5 %all_to_all.16 = f32[256,2,128]{2,1,0:T(2,128)S(1)} all-to-all(f32[256,2,128]{2,1,0:T(2,128)S(1)} %bitcast.18), channel_id=1, replica_groups=mesh['beam'=128,'pair'=2,'core'=2] {'pair','beam'}, dimensions={0} | all-to-all | bytes 524288 | tf_op jit(solution)/shard_map/all_to_all | solution.py:411
  70.3 0.4 probe.1
  70.7 6.2 %collective-permute-start = (f32[128,128]{1,0:T(8,128)S(1)}, f32[128,128]{1,0:T(8,128)S(1)}, u32[]{:S(2)}, u32[]{:S(2)}) collective-permute-start(f32[128,128]{1,0:T(8,128)S(1)} %get-tuple-element.26), channel_id=1, source_target_pairs={{0,1},{1,0},{2,3},{3,2},{4,5},{5,4},{6,7},{7,6},{8,9},{9,8},{10,11... | collective-permute-start | bytes 196616 | tf_op jit(solution)/shard_map/ppermute | solution.py:413
  76.9 0.9 %collective-permute-done = f32[128,128]{1,0:T(8,128)S(1)} collective-permute-done((f32[128,128]{1,0:T(8,128)S(1)}, f32[128,128]{1,0:T(8,128)S(1)}, u32[]{:S(2)}, u32[]{:S(2)}) %collective-permute-start) | collective-permute-done | bytes 65568 | tf_op jit(solution)/shard_map/ppermute | solution.py:413
  77.8 0.6 add.7
Async XLA Ops:
  1.6 35.6 %copy-start.1 = (s32[128,2]{0,1:T(2,128)S(1)}, s32[128,2]{0,1:T(2,128)}, u32[]{:S(2)}) copy-start(s32[128,2]{0,1:T(2,128)} %param.5) | copy-start | bytes 3076
  1.6 24.1 %all-to-all-start = ((f32[96,4,128]{2,1,0:T(4,128)}), f32[96,4,128]{2,1,0:T(4,128)S(1)}, u32[]{:S(2)}, u32[]{:S(2)}) async-start(f32[96,4,128]{2,1,0:T(4,128)} %copies.1), calls=%async_computation | async-start | bytes 393216 | tf_op jit(solution)/shard_map/all_to_all | solution.py:397
  15.2 0.7 copy-start
  15.9 0.7 copy-start.2
  16.6 0.7 copy-start.3
  70.7 7.1 %collective-permute-start = (f32[128,128]{1,0:T(8,128)S(1)}, f32[128,128]{1,0:T(8,128)S(1)}, u32[]{:S(2)}, u32[]{:S(2)}) collective-permute-start(f32[128,128]{1,0:T(8,128)S(1)} %get-tuple-element.26), channel_id=1, source_target_pairs={{0,1},{1,0},{2,3},{3,2},{4,5},{5,4},{6,7},{7,6},{8,9},{9,8},{10,11... | collective-permute-start | bytes 196616 | tf_op jit(solution)/shard_map/ppermute | solution.py:413

commit v11 on v10

--- a/solution.py
+++ b/solution.py
@@ -307,7 +307,7 @@
     field = jnp.concatenate(
         [
             jnp.concatenate(
-                [block_ref[pl.ds(2 * K * config + part, K, 2), :] for part in range(2)], axis=0
+                [block_ref[pl.ds(2 * config + part, K, 2 * here), :] for part in range(2)], axis=0
             )
             for config in range(here)
         ],
@@ -407,8 +407,8 @@
     ).reshape(devices * PIECE, K)
     image = propagate(own, tilts, whole, *tables)
 
-    rows = jnp.broadcast_to(image.reshape(1, K, 2, K), (pairs, K, 2, K)).reshape(pairs * K, 2, K)
-    block = lax.all_to_all(rows, ("pair", "beam"), 0, 0, tiled=True).reshape(2 * pairs * beams, K)
+    rows = jnp.broadcast_to(image.reshape(K, 1, 2, K), (K, pairs, 2, K)).reshape(pairs * K, 2, K)
+    block = lax.all_to_all(rows, ("beam", "pair"), 0, 0, tiled=True).reshape(2 * pairs * beams, K)
     mine, other = probe(block, coef, configs)
     return mine + lax.ppermute(other, "core", [(0, 1), (1, 0)])
 

time: 78.8 us -> 77.4 us (0.982)
  blocking collectives: 40 us -> 38.5 us
    all_to_all x1, blocking collectives: 28.5 us -> 27.1 us  [per_device(): lax.all_to_all(rows, ('beam', 'pair'), 0, 0, tiled=True)]
  transfers between devices with their start and end apart: 2 -> 2, of which waited for: 2 -> 2; matrix products, arithmetic and copies ran while one was open for 0% -> 0% of each run, Pallas kernels for 3% -> 4%
where the time goes in v11:
time: 77.4 us; the launch traced here: 77 us
  blocking collectives  38.5 us (50%)
  starting transfers between devices  19.9 us (26%)
  Pallas kernels  8.43 us (11%)
  waiting for transfers between devices  6.65 us (9%)
  local copies, waits for them, and re-layouts  2.83 us (4%)
    all_to_all x1, blocking collectives, per_device(): lax.all_to_all(rows, ('beam', 'pair'), 0, 0, tiled=True)  27.1 us
    all_to_all x1, starting transfers between devices, per_device(): lax.all_to_all(copies_of(potential, NEAR), 'beam', 0, 0, axis_index_group...  13.6 us
    all_to_all x1, blocking collectives, per_device(): lax.all_to_all(jnp.broadcast_to(part[None], (FAR, *part.shape)), 'beam',...  11.4 us
    ppermute x1, starting transfers between devices, per_device(): return mine + lax.ppermute(other, 'core', [(0, 1), (1, 0)])  6.31 us
    all_to_all x1, waiting for transfers between devices, per_device(): lax.all_to_all(copies_of(potential, NEAR), 'beam', 0, 0, axis_index_group...  5.77 us
    pallas_call x1, Pallas kernels, propagate(): pl.pallas_call(propagate_kernel, out_shape=shape_of(F32, 2 * K, K), in_sp...  4.44 us
    unnamed x9, local copies, waits for them, and re-layouts  2.71 us
    pallas_call x1, Pallas kernels, prepare(): pl.pallas_call(prepare_kernel, out_shape=out, in_specs=[SMEM] * 3 + [VMEM...  2.7 us
  transfers between devices with their start and end apart: 2, of which 2 were waited for; matrix products, arithmetic and copies ran while one was open for 0% of the time, Pallas kernels for 4%

profile of v11, /device:TPU:1, one launch (start us, length us, event | category | flops | bytes accessed | tf_op | source)
XLA Modules:
  0.0 77.0 jit_solution(1733393969763316078)
XLA Ops:
  0.0 0.7 copy.5.potential_ref
  0.7 0.9 %copies.1 = f32[96,4,128]{2,1,0:T(4,128)} custom-call(f32[1,3,512]{2,1,0:T(4,128)S(1)} %copy.5.potential_ref), custom_call_target="tpu_custom_call" | custom-call | tf_op jit(solution)/shard_map/copies/pallas_call | solution.py:380
  1.6 0.0 copy-start.1
  1.6 13.6 %all-to-all-start = ((f32[96,4,128]{2,1,0:T(4,128)}), f32[96,4,128]{2,1,0:T(4,128)S(1)}, u32[]{:S(2)}, u32[]{:S(2)}) async-start(f32[96,4,128]{2,1,0:T(4,128)} %copies.1), calls=%async_computation | async-start | bytes 393216 | tf_op jit(solution)/shard_map/all_to_all | solution.py:397
  15.2 0.0 copy-start
  15.2 0.7 copy-done
  15.9 0.0 copy-start.2
  15.9 0.7 copy-done.2
  16.6 0.0 copy-start.3
  16.6 0.7 copy-done.3
  17.2 2.7 %prepare.1 = (f32[2,256,128]{2,1,0:T(8,128)S(1)}, bf16[1456,512]{1,0:T(8,128)(2,1)S(1)}, f32[2,176,256]{2,1,0:T(8,128)S(1)}, f32[2,256,128]{2,1,0:T(8,128)S(1)}) custom-call(s32[1]{0:T(128)} %bitcast.own_ref, s32[1]{0:T(128)} %bitcast.2.slab_ref, s32[2,128]{1,0:T(2,128)S(1)} %bitcast.13, s32[2,128]{1,0:T(2,128)S(1)} %bitcast.14, s32[1,128]{1,0:T(1,128)S(1)} %bitcast.17, ...), custom_call_target="tpu_custom_call" | custom-call | tf_op jit(solution)/shard_map/prepare/pallas_call | solution.py:346
  20.0 5.8 %all-to-all-done = f32[96,4,128]{2,1,0:T(4,128)S(1)} async-done(((f32[96,4,128]{2,1,0:T(4,128)}), f32[96,4,128]{2,1,0:T(4,128)S(1)}, u32[]{:S(2)}, u32[]{:S(2)}) %all-to-all-start) | async-done | bytes 196640 | tf_op jit(solution)/shard_map/all_to_all | solution.py:397
  25.7 0.1 broadcast_in_dim.15
  25.8 11.4 %all_to_all.15 = f32[4,384,128]{2,1,0:T(8,128)S(1)} all-to-all(f32[4,384,128]{2,1,0:T(8,128)S(1)} %broadcast_in_dim.15), channel_id=1, replica_groups={{0,128,384,256},{4,132,388,260},{8,136,392,264},{12,140,396,268},{16,14..., dimensions={0} | all-to-all | bytes 1572864 | tf_op jit(solution)/shard_map/all_to_all | solution.py:405
  37.2 0.0 copy-done.1
  37.2 4.4 %propagate.1 = f32[256,128]{1,0:T(8,128)S(1)} custom-call(s32[1]{0:T(128)} %bitcast.own_ref, s32[2,128]{1,0:T(2,128)S(1)} %bitcast.15, f32[1536,128]{1,0:T(8,128)S(1)} %bitcast.10, bf16[1456,512]{1,0:T(8,128)(2,1)S(1)} %get-tuple-element.21.table_ref, f32[2,176,256]{2,1,0:T(8,128)S(1)} %get-tuple-element.22.factor_ref, ...), custom_call_target="tpu_custom_call" | custom-call | tf_op jit(solution)/shard_map/propagate/pallas_call | solution.py:357
  41.7 0.1 broadcast_in_dim.17
  41.7 27.1 %all_to_all.16 = f32[256,2,128]{2,1,0:T(2,128)S(1)} all-to-all(f32[256,2,128]{2,1,0:T(2,128)S(1)} %bitcast.18), channel_id=1, replica_groups=mesh['beam'=128,'pair'=2,'core'=2] {'beam','pair'}, dimensions={0} | all-to-all | bytes 524288 | tf_op jit(solution)/shard_map/all_to_all | solution.py:411
  68.8 0.4 probe.1
  69.2 6.3 %collective-permute-start = (f32[128,128]{1,0:T(8,128)S(1)}, f32[128,128]{1,0:T(8,128)S(1)}, u32[]{:S(2)}, u32[]{:S(2)}) collective-permute-start(f32[128,128]{1,0:T(8,128)S(1)} %get-tuple-element.26), channel_id=1, source_target_pairs={{0,1},{1,0},{2,3},{3,2},{4,5},{5,4},{6,7},{7,6},{8,9},{9,8},{10,11... | collective-permute-start | bytes 196616 | tf_op jit(solution)/shard_map/ppermute | solution.py:413
  75.5 0.9 %collective-permute-done = f32[128,128]{1,0:T(8,128)S(1)} collective-permute-done((f32[128,128]{1,0:T(8,128)S(1)}, f32[128,128]{1,0:T(8,128)S(1)}, u32[]{:S(2)}, u32[]{:S(2)}) %collective-permute-start) | collective-permute-done | bytes 65568 | tf_op jit(solution)/shard_map/ppermute | solution.py:413
  76.4 0.6 add.7
Async XLA Ops:
  1.6 35.6 %copy-start.1 = (s32[128,2]{0,1:T(2,128)S(1)}, s32[128,2]{0,1:T(2,128)}, u32[]{:S(2)}) copy-start(s32[128,2]{0,1:T(2,128)} %param.5) | copy-start | bytes 3076
  1.6 24.1 %all-to-all-start = ((f32[96,4,128]{2,1,0:T(4,128)}), f32[96,4,128]{2,1,0:T(4,128)S(1)}, u32[]{:S(2)}, u32[]{:S(2)}) async-start(f32[96,4,128]{2,1,0:T(4,128)} %copies.1), calls=%async_computation | async-start | bytes 393216 | tf_op jit(solution)/shard_map/all_to_all | solution.py:397
  15.2 0.7 copy-start
  15.9 0.7 copy-start.2
  16.6 0.7 copy-start.3
  69.2 7.2 %collective-permute-start = (f32[128,128]{1,0:T(8,128)S(1)}, f32[128,128]{1,0:T(8,128)S(1)}, u32[]{:S(2)}, u32[]{:S(2)}) collective-permute-start(f32[128,128]{1,0:T(8,128)S(1)} %get-tuple-element.26), channel_id=1, source_target_pairs={{0,1},{1,0},{2,3},{3,2},{4,5},{5,4},{6,7},{7,6},{8,9},{9,8},{10,11... | collective-permute-start | bytes 196616 | tf_op jit(solution)/shard_map/ppermute | solution.py:413

commit v12 on v11

--- a/solution.py
+++ b/solution.py
@@ -302,12 +302,26 @@
     out_ref[...] = from_left(table(IMAGE_LEFT), jnp.concatenate([real, imag], axis=0))
 
 
+def sort_kernel(pairs, in_ref, out_ref):
+    for x in range(FAR):
+        for part in range(2):
+            rows = in_ref[pl.ds(2 * NEAR * x + part, NEAR, 2), :]
+            for pair in range(pairs):
+                out_ref[pl.ds(2 * (FAR * pair + x) + part, NEAR, 2 * FAR * pairs), :] = rows
+
+
 def probe_kernel(configs, block_ref, coef_ref, mine_ref, other_ref):
     here = block_ref.shape[0] // (2 * K)
+    stride = 2 * FAR * here
     field = jnp.concatenate(
         [
             jnp.concatenate(
-                [block_ref[pl.ds(2 * config + part, K, 2 * here), :] for part in range(2)], axis=0
+                [
+                    block_ref[pl.ds(2 * (FAR * config + x) + part, NEAR, stride), :]
+                    for part in range(2)
+                    for x in range(FAR)
+                ],
+                axis=0,
             )
             for config in range(here)
         ],
@@ -326,6 +340,7 @@
     other_ref[...] = total[probes // 2 :]
 
 
+BEAM = ("x", "place")
 VMEM = pl.BlockSpec(memory_space=pltpu.VMEM)
 SMEM = pl.BlockSpec(memory_space=pltpu.SMEM)
 PARAMS = pltpu.CompilerParams(vmem_limit_bytes=24 * 1024 * 1024)
@@ -376,6 +391,17 @@
     )(block, coef)
 
 
+def sorted_rows(rows, pairs):
+    return pl.pallas_call(
+        functools.partial(sort_kernel, pairs),
+        out_shape=shape_of(F32, pairs * rows.shape[0], K),
+        in_specs=[VMEM],
+        out_specs=VMEM,
+        compiler_params=PARAMS,
+        name="sort",
+    )(rows)
+
+
 def copies_of(potential, count):
     return pl.pallas_call(
         copies_kernel,
@@ -389,26 +415,27 @@
 
 def per_device(groups, potential, tilts, aperture, positions):
     near, far = groups
-    devices = lax.axis_size("beam")
+    devices = lax.axis_size(BEAM)
     pairs, cores = lax.axis_size("pair"), lax.axis_size("core")
     configs = pairs * cores
     beams = tilts.shape[0]
 
-    part = lax.all_to_all(copies_of(potential, NEAR), "beam", 0, 0, axis_index_groups=near, tiled=True)
-
-    own = lax.axis_index("beam").reshape(1)
+    part = lax.all_to_all(copies_of(potential, NEAR), BEAM, 0, 0, axis_index_groups=near, tiled=True)
+
+    own = lax.axis_index(BEAM).reshape(1)
     slab = lax.axis_index(("pair", "core")).reshape(1)
     tilts = tilts.T
     coef, *tables = prepare(own, slab, tilts, aperture.reshape(1, beams), positions.T)
     part, coef, *tables = lax.optimization_barrier((part, coef, *tables))
     part = part.reshape(NEAR * PIECE, K)
     whole = lax.all_to_all(
-        jnp.broadcast_to(part[None], (FAR, *part.shape)), "beam", 0, 0, axis_index_groups=far
+        jnp.broadcast_to(part[None], (FAR, *part.shape)), BEAM, 0, 0, axis_index_groups=far
     ).reshape(devices * PIECE, K)
     image = propagate(own, tilts, whole, *tables)
 
-    rows = jnp.broadcast_to(image.reshape(K, 1, 2, K), (K, pairs, 2, K)).reshape(pairs * K, 2, K)
-    block = lax.all_to_all(rows, ("beam", "pair"), 0, 0, tiled=True).reshape(2 * pairs * beams, K)
+    rows = lax.all_to_all(image.reshape(FAR, NEAR * 2, K), "x", 0, 0)
+    rows = sorted_rows(rows.reshape(2 * K, K), pairs).reshape(NEAR * pairs, 2 * FAR, K)
+    block = lax.all_to_all(rows, ("place", "pair"), 0, 0, tiled=True).reshape(2 * pairs * beams, K)
     mine, other = probe(block, coef, configs)
     return mine + lax.ppermute(other, "core", [(0, 1), (1, 0)])
 
@@ -422,11 +449,11 @@
 
 
 def solution(mesh):
-    fine = jax.sharding.Mesh(mesh.devices.reshape(-1, 2, 2), ("beam", "pair", "core"))
+    fine = jax.sharding.Mesh(mesh.devices.reshape(FAR, NEAR, 2, 2), (*BEAM, "pair", "core"))
     return jax.shard_map(
         functools.partial(per_device, exchange_groups()),
         mesh=fine,
-        in_specs=(P(("pair", "core"), None, "beam"), P(), P(), P()),
-        out_specs=P(("pair", "core"), "beam"),
+        in_specs=(P(("pair", "core"), None, BEAM), P(), P(), P()),
+        out_specs=P(("pair", "core"), BEAM),
         check_vma=False,
     )

time: 77.4 us -> 82.6 us (1.067)
  blocking collectives: 38.5 us -> 42.8 us
    all_to_all x2 -> x3, blocking collectives: 38.5 us -> 42.8 us  [the longest x1 24.2 us: per_device(): lax.all_to_all(rows, ('place', 'pair'), 0, 0, tiled=True)]
  transfers between devices with their start and end apart: 2 -> 2, of which waited for: 2 -> 2; matrix products, arithmetic and copies ran while one was open for 0% -> 0% of each run, Pallas kernels for 4% -> 3%
where the time goes in v12:
time: 82.6 us; the launch traced here: 82.2 us
  blocking collectives  42.8 us (52%)
  starting transfers between devices  20.7 us (25%)
  Pallas kernels  8.55 us (10%)
  waiting for transfers between devices  6.65 us (8%)
  local copies, waits for them, and re-layouts  2.76 us (3%)
    all_to_all x1, blocking collectives, per_device(): lax.all_to_all(rows, ('place', 'pair'), 0, 0, tiled=True)  24.2 us
    all_to_all x1, starting transfers between devices, per_device(): lax.all_to_all(copies_of(potential, NEAR), BEAM, 0, 0, axis_index_groups=...  13.6 us
    all_to_all x1, blocking collectives, per_device(): lax.all_to_all(jnp.broadcast_to(part[None], (FAR, *part.shape)), BEAM, 0,...  11.4 us
    all_to_all x1, blocking collectives, per_device(): rows = lax.all_to_all(image.reshape(FAR, NEAR * 2, K), 'x', 0, 0)  7.21 us
    ppermute x1, starting transfers between devices, per_device(): return mine + lax.ppermute(other, 'core', [(0, 1), (1, 0)])  7.08 us
    all_to_all x1, waiting for transfers between devices, per_device(): lax.all_to_all(copies_of(potential, NEAR), BEAM, 0, 0, axis_index_groups=...  5.77 us
    pallas_call x1, Pallas kernels, propagate(): pl.pallas_call(propagate_kernel, out_shape=shape_of(F32, 2 * K, K), in_sp...  4.44 us
    unnamed x9, local copies, waits for them, and re-layouts  2.71 us
  transfers between devices with their start and end apart: 2, of which 2 were waited for; matrix products, arithmetic and copies ran while one was open for 0% of the time, Pallas kernels for 3%

profile of v12, /device:TPU:1, one launch (start us, length us, event | category | flops | bytes accessed | tf_op | source)
XLA Modules:
  0.0 82.2 jit_solution(6195991238338789374)
XLA Ops:
  0.0 0.7 copy.5.potential_ref
  0.7 0.9 %copies.1 = f32[96,4,128]{2,1,0:T(4,128)} custom-call(f32[1,3,512]{2,1,0:T(4,128)S(1)} %copy.5.potential_ref), custom_call_target="tpu_custom_call" | custom-call | tf_op jit(solution)/shard_map/copies/pallas_call | solution.py:406
  1.6 0.0 copy-start.1
  1.6 13.6 %all-to-all-start = ((f32[96,4,128]{2,1,0:T(4,128)}), f32[96,4,128]{2,1,0:T(4,128)S(1)}, u32[]{:S(2)}, u32[]{:S(2)}) async-start(f32[96,4,128]{2,1,0:T(4,128)} %copies.1), calls=%async_computation | async-start | bytes 393216 | tf_op jit(solution)/shard_map/all_to_all | solution.py:423
  15.2 0.0 copy-start
  15.2 0.7 copy-done
  15.9 0.0 copy-start.2
  15.9 0.7 copy-done.2
  16.6 0.0 copy-start.3
  16.6 0.7 copy-done.3
  17.3 2.7 %prepare.1 = (f32[2,256,128]{2,1,0:T(8,128)S(1)}, bf16[1456,512]{1,0:T(8,128)(2,1)S(1)}, f32[2,176,256]{2,1,0:T(8,128)S(1)}, f32[2,256,128]{2,1,0:T(8,128)S(1)}) custom-call(s32[1]{0:T(128)} %bitcast.own_ref, s32[1]{0:T(128)} %bitcast.2.slab_ref, s32[2,128]{1,0:T(2,128)S(1)} %bitcast.16, s32[2,128]{1,0:T(2,128)S(1)} %bitcast.17, s32[1,128]{1,0:T(1,128)S(1)} %bitcast.20, ...), custom_call_target="tpu_custom_call" | custom-call | tf_op jit(solution)/shard_map/prepare/pallas_call | solution.py:361
  20.0 5.8 %all-to-all-done = f32[96,4,128]{2,1,0:T(4,128)S(1)} async-done(((f32[96,4,128]{2,1,0:T(4,128)}), f32[96,4,128]{2,1,0:T(4,128)S(1)}, u32[]{:S(2)}, u32[]{:S(2)}) %all-to-all-start) | async-done | bytes 196640 | tf_op jit(solution)/shard_map/all_to_all | solution.py:423
  25.7 0.1 broadcast_in_dim.8
  25.8 11.4 %all_to_all.20 = f32[4,384,128]{2,1,0:T(8,128)S(1)} all-to-all(f32[4,384,128]{2,1,0:T(8,128)S(1)} %broadcast_in_dim.8), channel_id=1, replica_groups={{0,128,384,256},{4,132,388,260},{8,136,392,264},{12,140,396,268},{16,14..., dimensions={0} | all-to-all | bytes 1572864 | tf_op jit(solution)/shard_map/all_to_all | solution.py:431
  37.2 0.0 copy-done.1
  37.2 4.4 %propagate.1 = f32[256,128]{1,0:T(8,128)S(1)} custom-call(s32[1]{0:T(128)} %bitcast.own_ref, s32[2,128]{1,0:T(2,128)S(1)} %bitcast.18, f32[1536,128]{1,0:T(8,128)S(1)} %bitcast.11, bf16[1456,512]{1,0:T(8,128)(2,1)S(1)} %get-tuple-element.21.table_ref, f32[2,176,256]{2,1,0:T(8,128)S(1)} %get-tuple-element.22.factor_ref, ...), custom_call_target="tpu_custom_call" | custom-call | tf_op jit(solution)/shard_map/propagate/pallas_call | solution.py:372
  41.7 7.2 %all_to_all.21 = f32[4,64,128]{2,1,0:T(8,128)S(1)} all-to-all(f32[4,64,128]{2,1,0:T(8,128)S(1)} %bitcast.14), channel_id=1, replica_groups=mesh['x'=4,'place'=32,'pair'=2,'core'=2] {'x'}, dimensions={0} | all-to-all | bytes 262144 | tf_op jit(solution)/shard_map/all_to_all | solution.py:436
  48.9 0.1 sort.1
  49.0 24.2 %all_to_all.22 = f32[64,8,128]{2,1,0:T(8,128)S(1)} all-to-all(f32[64,8,128]{2,1,0:T(8,128)S(1)} %bitcast.13), channel_id=1, replica_groups=mesh['x'=4,'place'=32,'pair'=2,'core'=2] {'place','pair'}, dimensions={0} | all-to-all | bytes 524288 | tf_op jit(solution)/shard_map/all_to_all | solution.py:438
  73.2 0.4 probe.1
  73.6 7.1 %collective-permute-start = (f32[128,128]{1,0:T(8,128)S(1)}, f32[128,128]{1,0:T(8,128)S(1)}, u32[]{:S(2)}, u32[]{:S(2)}) collective-permute-start(f32[128,128]{1,0:T(8,128)S(1)} %get-tuple-element.26), channel_id=1, source_target_pairs={{0,1},{1,0},{2,3},{3,2},{4,5},{5,4},{6,7},{7,6},{8,9},{9,8},{10,11... | collective-permute-start | bytes 196616 | tf_op jit(solution)/shard_map/ppermute | solution.py:440
  80.7 0.9 %collective-permute-done = f32[128,128]{1,0:T(8,128)S(1)} collective-permute-done((f32[128,128]{1,0:T(8,128)S(1)}, f32[128,128]{1,0:T(8,128)S(1)}, u32[]{:S(2)}, u32[]{:S(2)}) %collective-permute-start) | collective-permute-done | bytes 65568 | tf_op jit(solution)/shard_map/ppermute | solution.py:440
  81.6 0.6 add.11
Async XLA Ops:
  1.6 35.6 %copy-start.1 = (s32[128,2]{0,1:T(2,128)S(1)}, s32[128,2]{0,1:T(2,128)}, u32[]{:S(2)}) copy-start(s32[128,2]{0,1:T(2,128)} %param.5) | copy-start | bytes 3076
  1.6 24.1 %all-to-all-start = ((f32[96,4,128]{2,1,0:T(4,128)}), f32[96,4,128]{2,1,0:T(4,128)S(1)}, u32[]{:S(2)}, u32[]{:S(2)}) async-start(f32[96,4,128]{2,1,0:T(4,128)} %copies.1), calls=%async_computation | async-start | bytes 393216 | tf_op jit(solution)/shard_map/all_to_all | solution.py:423
  15.2 0.7 copy-start
  15.9 0.7 copy-start.2
  16.6 0.7 copy-start.3
  73.6 8.0 %collective-permute-start = (f32[128,128]{1,0:T(8,128)S(1)}, f32[128,128]{1,0:T(8,128)S(1)}, u32[]{:S(2)}, u32[]{:S(2)}) collective-permute-start(f32[128,128]{1,0:T(8,128)S(1)} %get-tuple-element.26), channel_id=1, source_target_pairs={{0,1},{1,0},{2,3},{3,2},{4,5},{5,4},{6,7},{7,6},{8,9},{9,8},{10,11... | collective-permute-start | bytes 196616 | tf_op jit(solution)/shard_map/ppermute | solution.py:440

commit v13 on v12

--- a/solution.py
+++ b/solution.py
@@ -110,18 +110,12 @@
 
 
 def copies_kernel(potential_ref, out_ref):
-    values = potential_ref[0]
-    pick = iota((K, K), 0) + iota((K, K), 1) == K - 1
-    mirror = jnp.where(pick, 1.0, 0.0)
-    quarters = [values[:, K * i : K * (i + 1)] for i in range(4)]
-    for i in (1, 3):
-        quarters[i] = jnp.dot(
-            quarters[i], mirror, precision=lax.Precision.HIGHEST, preferred_element_type=F32
-        )
-    pieces = [
-        jnp.concatenate([quarter[layer : layer + 1] for quarter in quarters], axis=0)[None]
-        for layer in range(SLICES)
-    ]
+    mirror = jnp.where(iota((K, K), 0) + iota((K, K), 1) == K - 1, 1.0, 0.0)
+    pieces = []
+    for layer in range(SLICES):
+        rows = potential_ref[layer]
+        turned = jnp.dot(rows, mirror, precision=lax.Precision.HIGHEST, preferred_element_type=F32)
+        pieces.append(jnp.where((iota(rows.shape, 0) & 1) == 1, turned, rows)[None])
     out_ref[...] = jnp.concatenate(pieces * (out_ref.shape[0] // SLICES), axis=0)
 
 
@@ -179,7 +173,8 @@
         coef_ref[1, K * core : K * (core + 1), :] = cosine * weight_im + sine * weight_re
 
     m, other = iota((2 * K, 2 * K), 0), iota((2 * K, 2 * K), 1)
-    turn = (4 * (m >> 1) + 1) * centred(other & (K - 1)) + K * ((other >> 7) - (m & 1))
+    row = NEAR * ((m >> 1) & (FAR - 1)) + (m >> 3)
+    turn = (4 * row + 1) * centred(other & (K - 1)) + K * ((other >> 7) - (m & 1))
     left, right = iota((K, 2 * K), 0), iota((K, 2 * K), 1)
     for (row, rows, columns), table in (
         (AHEAD_LEFT, forward_table((ROWS, G), near, mixed, 1)),
@@ -302,14 +297,6 @@
     out_ref[...] = from_left(table(IMAGE_LEFT), jnp.concatenate([real, imag], axis=0))
 
 
-def sort_kernel(pairs, in_ref, out_ref):
-    for x in range(FAR):
-        for part in range(2):
-            rows = in_ref[pl.ds(2 * NEAR * x + part, NEAR, 2), :]
-            for pair in range(pairs):
-                out_ref[pl.ds(2 * (FAR * pair + x) + part, NEAR, 2 * FAR * pairs), :] = rows
-
-
 def probe_kernel(configs, block_ref, coef_ref, mine_ref, other_ref):
     here = block_ref.shape[0] // (2 * K)
     stride = 2 * FAR * here
@@ -317,7 +304,7 @@
         [
             jnp.concatenate(
                 [
-                    block_ref[pl.ds(2 * (FAR * config + x) + part, NEAR, stride), :]
+                    block_ref[pl.ds(2 * (here * x + config) + part, NEAR, stride), :]
                     for part in range(2)
                     for x in range(FAR)
                 ],
@@ -391,26 +378,15 @@
     )(block, coef)
 
 
-def sorted_rows(rows, pairs):
-    return pl.pallas_call(
-        functools.partial(sort_kernel, pairs),
-        out_shape=shape_of(F32, pairs * rows.shape[0], K),
-        in_specs=[VMEM],
-        out_specs=VMEM,
-        compiler_params=PARAMS,
-        name="sort",
-    )(rows)
-
-
 def copies_of(potential, count):
     return pl.pallas_call(
         copies_kernel,
         out_shape=shape_of(F32, count * SLICES, 4, K),
         in_specs=[VMEM],
         out_specs=VMEM,
-        compiler_params=PARAMS,
+        compiler_params=pltpu.CompilerParams(vmem_limit_bytes=60 * 1024 * 1024),
         name="copies",
-    )(potential)
+    )(potential.transpose(1, 0, 2).reshape(SLICES, 4, K))
 
 
 def per_device(groups, potential, tilts, aperture, positions):
@@ -433,9 +409,8 @@
     ).reshape(devices * PIECE, K)
     image = propagate(own, tilts, whole, *tables)
 
-    rows = lax.all_to_all(image.reshape(FAR, NEAR * 2, K), "x", 0, 0)
-    rows = sorted_rows(rows.reshape(2 * K, K), pairs).reshape(NEAR * pairs, 2 * FAR, K)
-    block = lax.all_to_all(rows, ("place", "pair"), 0, 0, tiled=True).reshape(2 * pairs * beams, K)
+    rows = jnp.broadcast_to(image.reshape(K, 1, 2, K), (K, pairs, 2, K)).reshape(pairs * K, 2, K)
+    block = lax.all_to_all(rows, ("place", "x", "pair"), 0, 0, tiled=True).reshape(2 * pairs * beams, K)
     mine, other = probe(block, coef, configs)
     return mine + lax.ppermute(other, "core", [(0, 1), (1, 0)])
 

time: 82.6 us -> 77.6 us (0.939)
  blocking collectives: 42.8 us -> 38.7 us
    all_to_all x2 -> x1, blocking collectives: 31.4 us -> 27.2 us  [per_device(): lax.all_to_all(rows, ('place', 'x', 'pair'), 0, 0, tiled=True)]
    unnamed x9 -> x8, local copies, waits for them, and re-layouts: 2.71 us -> 2.02 us
  transfers between devices with their start and end apart: 2 -> 2, of which waited for: 2 -> 2; matrix products, arithmetic and copies ran while one was open for 0% -> 0% of each run, Pallas kernels for 3% -> 4%
where the time goes in v13:
time: 77.6 us; the launch traced here: 77.2 us
  blocking collectives  38.7 us (50%)
  starting transfers between devices  19.9 us (26%)
  Pallas kernels  9.26 us (12%)
  waiting for transfers between devices  6.62 us (9%)
  local copies, waits for them, and re-layouts  2.14 us (3%)
    all_to_all x1, blocking collectives, per_device(): lax.all_to_all(rows, ('place', 'x', 'pair'), 0, 0, tiled=True)  27.2 us
    all_to_all x1, starting transfers between devices, per_device(): lax.all_to_all(copies_of(potential, NEAR), BEAM, 0, 0, axis_index_groups=...  13.6 us
    all_to_all x1, blocking collectives, per_device(): lax.all_to_all(jnp.broadcast_to(part[None], (FAR, *part.shape)), BEAM, 0,...  11.4 us
    ppermute x1, starting transfers between devices, per_device(): return mine + lax.ppermute(other, 'core', [(0, 1), (1, 0)])  6.26 us
    all_to_all x1, waiting for transfers between devices, per_device(): lax.all_to_all(copies_of(potential, NEAR), BEAM, 0, 0, axis_index_groups=...  5.74 us
    pallas_call x1, Pallas kernels, propagate(): pl.pallas_call(propagate_kernel, out_shape=shape_of(F32, 2 * K, K), in_sp...  4.48 us
    pallas_call x1, Pallas kernels, prepare(): pl.pallas_call(prepare_kernel, out_shape=out, in_specs=[SMEM] * 3 + [VMEM...  2.72 us
    unnamed x8, local copies, waits for them, and re-layouts  2.02 us
  transfers between devices with their start and end apart: 2, of which 2 were waited for; matrix products, arithmetic and copies ran while one was open for 0% of the time, Pallas kernels for 4%

profile of v13, /device:TPU:1, one launch (start us, length us, event | category | flops | bytes accessed | tf_op | source)
XLA Modules:
  0.0 77.2 jit_solution(16310292911263459335)
XLA Ops:
  0.0 1.6 %copies.1 = f32[96,4,128]{2,1,0:T(4,128)} custom-call(f32[3,4,128]{2,1,0:T(4,128)} %bitcast.21), custom_call_target="tpu_custom_call" | custom-call | tf_op jit(solution)/shard_map/copies/pallas_call | solution.py:382
  1.6 0.0 copy-start.1
  1.6 13.6 %all-to-all-start = ((f32[96,4,128]{2,1,0:T(4,128)}), f32[96,4,128]{2,1,0:T(4,128)S(1)}, u32[]{:S(2)}, u32[]{:S(2)}) async-start(f32[96,4,128]{2,1,0:T(4,128)} %copies.1), calls=%async_computation | async-start | bytes 393216 | tf_op jit(solution)/shard_map/all_to_all | solution.py:399
  15.3 0.0 copy-start
  15.3 0.7 copy-done
  15.9 0.0 copy-start.2
  15.9 0.7 copy-done.2
  16.6 0.0 copy-start.3
  16.6 0.7 copy-done.3
  17.3 2.7 %prepare.1 = (f32[2,256,128]{2,1,0:T(8,128)S(1)}, bf16[1456,512]{1,0:T(8,128)(2,1)S(1)}, f32[2,176,256]{2,1,0:T(8,128)S(1)}, f32[2,256,128]{2,1,0:T(8,128)S(1)}) custom-call(s32[1]{0:T(128)} %bitcast.own_ref, s32[1]{0:T(128)} %bitcast.3.slab_ref, s32[2,128]{1,0:T(2,128)S(1)} %bitcast.14, s32[2,128]{1,0:T(2,128)S(1)} %bitcast.15, s32[1,128]{1,0:T(1,128)S(1)} %bitcast.18, ...), custom_call_target="tpu_custom_call" | custom-call | tf_op jit(solution)/shard_map/prepare/pallas_call | solution.py:348
  20.0 5.7 %all-to-all-done = f32[96,4,128]{2,1,0:T(4,128)S(1)} async-done(((f32[96,4,128]{2,1,0:T(4,128)}), f32[96,4,128]{2,1,0:T(4,128)S(1)}, u32[]{:S(2)}, u32[]{:S(2)}) %all-to-all-start) | async-done | bytes 196640 | tf_op jit(solution)/shard_map/all_to_all | solution.py:399
  25.8 0.1 broadcast_in_dim.15
  25.8 11.4 %all_to_all.15 = f32[4,384,128]{2,1,0:T(8,128)S(1)} all-to-all(f32[4,384,128]{2,1,0:T(8,128)S(1)} %broadcast_in_dim.15), channel_id=1, replica_groups={{0,128,384,256},{4,132,388,260},{8,136,392,264},{12,140,396,268},{16,14..., dimensions={0} | all-to-all | bytes 1572864 | tf_op jit(solution)/shard_map/all_to_all | solution.py:407
  37.2 0.0 copy-done.1
  37.2 4.5 %propagate.1 = f32[256,128]{1,0:T(8,128)S(1)} custom-call(s32[1]{0:T(128)} %bitcast.own_ref, s32[2,128]{1,0:T(2,128)S(1)} %bitcast.16, f32[1536,128]{1,0:T(8,128)S(1)} %bitcast.11, bf16[1456,512]{1,0:T(8,128)(2,1)S(1)} %get-tuple-element.21.table_ref, f32[2,176,256]{2,1,0:T(8,128)S(1)} %get-tuple-element.22.factor_ref, ...), custom_call_target="tpu_custom_call" | custom-call | tf_op jit(solution)/shard_map/propagate/pallas_call | solution.py:359
  41.7 0.1 broadcast_in_dim.17
  41.8 27.2 %all_to_all.16 = f32[256,2,128]{2,1,0:T(2,128)S(1)} all-to-all(f32[256,2,128]{2,1,0:T(2,128)S(1)} %bitcast.19), channel_id=1, replica_groups=mesh['x'=4,'place'=32,'pair'=2,'core'=2] {'place','x','pair'}, dimensions={0} | all-to-all | bytes 524288 | tf_op jit(solution)/shard_map/all_to_all | solution.py:413
  69.0 0.4 probe.1
  69.5 6.3 %collective-permute-start = (f32[128,128]{1,0:T(8,128)S(1)}, f32[128,128]{1,0:T(8,128)S(1)}, u32[]{:S(2)}, u32[]{:S(2)}) collective-permute-start(f32[128,128]{1,0:T(8,128)S(1)} %get-tuple-element.26), channel_id=1, source_target_pairs={{0,1},{1,0},{2,3},{3,2},{4,5},{5,4},{6,7},{7,6},{8,9},{9,8},{10,11... | collective-permute-start | bytes 196616 | tf_op jit(solution)/shard_map/ppermute | solution.py:415
  75.7 0.9 %collective-permute-done = f32[128,128]{1,0:T(8,128)S(1)} collective-permute-done((f32[128,128]{1,0:T(8,128)S(1)}, f32[128,128]{1,0:T(8,128)S(1)}, u32[]{:S(2)}, u32[]{:S(2)}) %collective-permute-start) | collective-permute-done | bytes 65568 | tf_op jit(solution)/shard_map/ppermute | solution.py:415
  76.6 0.6 add.11
Async XLA Ops:
  1.6 35.6 %copy-start.1 = (s32[128,2]{0,1:T(2,128)S(1)}, s32[128,2]{0,1:T(2,128)}, u32[]{:S(2)}) copy-start(s32[128,2]{0,1:T(2,128)} %param.5) | copy-start | bytes 3076
  1.6 24.1 %all-to-all-start = ((f32[96,4,128]{2,1,0:T(4,128)}), f32[96,4,128]{2,1,0:T(4,128)S(1)}, u32[]{:S(2)}, u32[]{:S(2)}) async-start(f32[96,4,128]{2,1,0:T(4,128)} %copies.1), calls=%async_computation | async-start | bytes 393216 | tf_op jit(solution)/shard_map/all_to_all | solution.py:399
  15.3 0.7 copy-start
  15.9 0.7 copy-start.2
  16.6 0.7 copy-start.3
  69.5 7.1 %collective-permute-start = (f32[128,128]{1,0:T(8,128)S(1)}, f32[128,128]{1,0:T(8,128)S(1)}, u32[]{:S(2)}, u32[]{:S(2)}) collective-permute-start(f32[128,128]{1,0:T(8,128)S(1)} %get-tuple-element.26), channel_id=1, source_target_pairs={{0,1},{1,0},{2,3},{3,2},{4,5},{5,4},{6,7},{7,6},{8,9},{9,8},{10,11... | collective-permute-start | bytes 196616 | tf_op jit(solution)/shard_map/ppermute | solution.py:415

commit v14 on v13

--- a/solution.py
+++ b/solution.py
@@ -111,11 +111,10 @@
 
 def copies_kernel(potential_ref, out_ref):
     mirror = jnp.where(iota((K, K), 0) + iota((K, K), 1) == K - 1, 1.0, 0.0)
-    pieces = []
-    for layer in range(SLICES):
-        rows = potential_ref[layer]
-        turned = jnp.dot(rows, mirror, precision=lax.Precision.HIGHEST, preferred_element_type=F32)
-        pieces.append(jnp.where((iota(rows.shape, 0) & 1) == 1, turned, rows)[None])
+    rows = jnp.concatenate([potential_ref[layer] for layer in range(SLICES)], axis=0)
+    turned = jnp.dot(rows, mirror, precision=lax.Precision.HIGHEST, preferred_element_type=F32)
+    rows = jnp.where((iota(rows.shape, 0) & 1) == 1, turned, rows)
+    pieces = [rows[4 * layer : 4 * (layer + 1)][None] for layer in range(SLICES)]
     out_ref[...] = jnp.concatenate(pieces * (out_ref.shape[0] // SLICES), axis=0)
 
 

time: 77.6 us -> 77.6 us (level)
  no operation moved by 1% of the time
where the time goes in v14:
time: 77.6 us; the launch traced here: 77.2 us
  blocking collectives  38.7 us (50%)
  starting transfers between devices  19.9 us (26%)
  Pallas kernels  9.17 us (12%)
  waiting for transfers between devices  6.62 us (9%)
  local copies, waits for them, and re-layouts  2.14 us (3%)
    all_to_all x1, blocking collectives, per_device(): lax.all_to_all(rows, ('place', 'x', 'pair'), 0, 0, tiled=True)  27.2 us
    all_to_all x1, starting transfers between devices, per_device(): lax.all_to_all(copies_of(potential, NEAR), BEAM, 0, 0, axis_index_groups=...  13.6 us
    all_to_all x1, blocking collectives, per_device(): lax.all_to_all(jnp.broadcast_to(part[None], (FAR, *part.shape)), BEAM, 0,...  11.4 us
    ppermute x1, starting transfers between devices, per_device(): return mine + lax.ppermute(other, 'core', [(0, 1), (1, 0)])  6.25 us
    all_to_all x1, waiting for transfers between devices, per_device(): lax.all_to_all(copies_of(potential, NEAR), BEAM, 0, 0, axis_index_groups=...  5.74 us
    pallas_call x1, Pallas kernels, propagate(): pl.pallas_call(propagate_kernel, out_shape=shape_of(F32, 2 * K, K), in_sp...  4.47 us
    pallas_call x1, Pallas kernels, prepare(): pl.pallas_call(prepare_kernel, out_shape=out, in_specs=[SMEM] * 3 + [VMEM...  2.72 us
    unnamed x8, local copies, waits for them, and re-layouts  2.02 us
  transfers between devices with their start and end apart: 2, of which 2 were waited for; matrix products, arithmetic and copies ran while one was open for 0% of the time, Pallas kernels for 4%

profile of v14, /device:TPU:1, one launch (start us, length us, event | category | flops | bytes accessed | tf_op | source)
XLA Modules:
  0.0 77.2 jit_solution(18070964519924236308)
XLA Ops:
  0.0 1.6 %copies.1 = f32[96,4,128]{2,1,0:T(4,128)} custom-call(f32[3,4,128]{2,1,0:T(4,128)} %bitcast.21), custom_call_target="tpu_custom_call" | custom-call | tf_op jit(solution)/shard_map/copies/pallas_call | solution.py:381
  1.6 0.0 copy-start.1
  1.6 13.6 %all-to-all-start = ((f32[96,4,128]{2,1,0:T(4,128)}), f32[96,4,128]{2,1,0:T(4,128)S(1)}, u32[]{:S(2)}, u32[]{:S(2)}) async-start(f32[96,4,128]{2,1,0:T(4,128)} %copies.1), calls=%async_computation | async-start | bytes 393216 | tf_op jit(solution)/shard_map/all_to_all | solution.py:398
  15.2 0.0 copy-start
  15.2 0.7 copy-done
  15.9 0.0 copy-start.2
  15.9 0.7 copy-done.2
  16.5 0.0 copy-start.3
  16.5 0.7 copy-done.3
  17.2 2.7 %prepare.1 = (f32[2,256,128]{2,1,0:T(8,128)S(1)}, bf16[1456,512]{1,0:T(8,128)(2,1)S(1)}, f32[2,176,256]{2,1,0:T(8,128)S(1)}, f32[2,256,128]{2,1,0:T(8,128)S(1)}) custom-call(s32[1]{0:T(128)} %bitcast.own_ref, s32[1]{0:T(128)} %bitcast.3.slab_ref, s32[2,128]{1,0:T(2,128)S(1)} %bitcast.14, s32[2,128]{1,0:T(2,128)S(1)} %bitcast.15, s32[1,128]{1,0:T(1,128)S(1)} %bitcast.18, ...), custom_call_target="tpu_custom_call" | custom-call | tf_op jit(solution)/shard_map/prepare/pallas_call | solution.py:347
  19.9 5.7 %all-to-all-done = f32[96,4,128]{2,1,0:T(4,128)S(1)} async-done(((f32[96,4,128]{2,1,0:T(4,128)}), f32[96,4,128]{2,1,0:T(4,128)S(1)}, u32[]{:S(2)}, u32[]{:S(2)}) %all-to-all-start) | async-done | bytes 196640 | tf_op jit(solution)/shard_map/all_to_all | solution.py:398
  25.7 0.1 broadcast_in_dim.15
  25.7 11.4 %all_to_all.15 = f32[4,384,128]{2,1,0:T(8,128)S(1)} all-to-all(f32[4,384,128]{2,1,0:T(8,128)S(1)} %broadcast_in_dim.15), channel_id=1, replica_groups={{0,128,384,256},{4,132,388,260},{8,136,392,264},{12,140,396,268},{16,14..., dimensions={0} | all-to-all | bytes 1572864 | tf_op jit(solution)/shard_map/all_to_all | solution.py:406
  37.1 0.0 copy-done.1
  37.1 4.5 %propagate.1 = f32[256,128]{1,0:T(8,128)S(1)} custom-call(s32[1]{0:T(128)} %bitcast.own_ref, s32[2,128]{1,0:T(2,128)S(1)} %bitcast.16, f32[1536,128]{1,0:T(8,128)S(1)} %bitcast.11, bf16[1456,512]{1,0:T(8,128)(2,1)S(1)} %get-tuple-element.21.table_ref, f32[2,176,256]{2,1,0:T(8,128)S(1)} %get-tuple-element.22.factor_ref, ...), custom_call_target="tpu_custom_call" | custom-call | tf_op jit(solution)/shard_map/propagate/pallas_call | solution.py:358
  41.6 0.1 broadcast_in_dim.17
  41.7 27.2 %all_to_all.16 = f32[256,2,128]{2,1,0:T(2,128)S(1)} all-to-all(f32[256,2,128]{2,1,0:T(2,128)S(1)} %bitcast.19), channel_id=1, replica_groups=mesh['x'=4,'place'=32,'pair'=2,'core'=2] {'place','x','pair'}, dimensions={0} | all-to-all | bytes 524288 | tf_op jit(solution)/shard_map/all_to_all | solution.py:412
  68.9 0.4 probe.1
  69.4 6.3 %collective-permute-start = (f32[128,128]{1,0:T(8,128)S(1)}, f32[128,128]{1,0:T(8,128)S(1)}, u32[]{:S(2)}, u32[]{:S(2)}) collective-permute-start(f32[128,128]{1,0:T(8,128)S(1)} %get-tuple-element.26), channel_id=1, source_target_pairs={{0,1},{1,0},{2,3},{3,2},{4,5},{5,4},{6,7},{7,6},{8,9},{9,8},{10,11... | collective-permute-start | bytes 196616 | tf_op jit(solution)/shard_map/ppermute | solution.py:414
  75.6 0.9 %collective-permute-done = f32[128,128]{1,0:T(8,128)S(1)} collective-permute-done((f32[128,128]{1,0:T(8,128)S(1)}, f32[128,128]{1,0:T(8,128)S(1)}, u32[]{:S(2)}, u32[]{:S(2)}) %collective-permute-start) | collective-permute-done | bytes 65568 | tf_op jit(solution)/shard_map/ppermute | solution.py:414
  76.5 0.6 add.11
Async XLA Ops:
  1.6 35.6 %copy-start.1 = (s32[128,2]{0,1:T(2,128)S(1)}, s32[128,2]{0,1:T(2,128)}, u32[]{:S(2)}) copy-start(s32[128,2]{0,1:T(2,128)} %param.5) | copy-start | bytes 3076
  1.6 24.1 %all-to-all-start = ((f32[96,4,128]{2,1,0:T(4,128)}), f32[96,4,128]{2,1,0:T(4,128)S(1)}, u32[]{:S(2)}, u32[]{:S(2)}) async-start(f32[96,4,128]{2,1,0:T(4,128)} %copies.1), calls=%async_computation | async-start | bytes 393216 | tf_op jit(solution)/shard_map/all_to_all | solution.py:398
  15.2 0.7 copy-start
  15.9 0.7 copy-start.2
  16.5 0.7 copy-start.3
  69.4 7.1 %collective-permute-start = (f32[128,128]{1,0:T(8,128)S(1)}, f32[128,128]{1,0:T(8,128)S(1)}, u32[]{:S(2)}, u32[]{:S(2)}) collective-permute-start(f32[128,128]{1,0:T(8,128)S(1)} %get-tuple-element.26), channel_id=1, source_target_pairs={{0,1},{1,0},{2,3},{3,2},{4,5},{5,4},{6,7},{7,6},{8,9},{9,8},{10,11... | collective-permute-start | bytes 196616 | tf_op jit(solution)/shard_map/ppermute | solution.py:414

commit v15 on v11

--- a/solution.py
+++ b/solution.py
@@ -110,18 +110,11 @@
 
 
 def copies_kernel(potential_ref, out_ref):
-    values = potential_ref[0]
-    pick = iota((K, K), 0) + iota((K, K), 1) == K - 1
-    mirror = jnp.where(pick, 1.0, 0.0)
-    quarters = [values[:, K * i : K * (i + 1)] for i in range(4)]
-    for i in (1, 3):
-        quarters[i] = jnp.dot(
-            quarters[i], mirror, precision=lax.Precision.HIGHEST, preferred_element_type=F32
-        )
-    pieces = [
-        jnp.concatenate([quarter[layer : layer + 1] for quarter in quarters], axis=0)[None]
-        for layer in range(SLICES)
-    ]
+    mirror = jnp.where(iota((K, K), 0) + iota((K, K), 1) == K - 1, 1.0, 0.0)
+    rows = jnp.concatenate([potential_ref[layer] for layer in range(SLICES)], axis=0)
+    turned = jnp.dot(rows, mirror, precision=lax.Precision.HIGHEST, preferred_element_type=F32)
+    rows = jnp.where((iota(rows.shape, 0) & 1) == 1, turned, rows)
+    pieces = [rows[4 * layer : 4 * (layer + 1)][None] for layer in range(SLICES)]
     out_ref[...] = jnp.concatenate(pieces * (out_ref.shape[0] // SLICES), axis=0)
 
 
@@ -382,9 +375,9 @@
         out_shape=shape_of(F32, count * SLICES, 4, K),
         in_specs=[VMEM],
         out_specs=VMEM,
-        compiler_params=PARAMS,
+        compiler_params=pltpu.CompilerParams(vmem_limit_bytes=60 * 1024 * 1024),
         name="copies",
-    )(potential)
+    )(potential.transpose(1, 0, 2).reshape(SLICES, 4, K))
 
 
 def per_device(groups, potential, tilts, aperture, positions):

time: 77.4 us -> 77.4 us (level)
    unnamed x9 -> x8, local copies, waits for them, and re-layouts: 2.71 us -> 2.02 us
where the time goes in v15:
time: 77.4 us; the launch traced here: 77 us
  blocking collectives  38.5 us (50%)
  starting transfers between devices  19.9 us (26%)
  Pallas kernels  9.1 us (12%)
  waiting for transfers between devices  6.65 us (9%)
  local copies, waits for them, and re-layouts  2.14 us (3%)
    all_to_all x1, blocking collectives, per_device(): lax.all_to_all(rows, ('beam', 'pair'), 0, 0, tiled=True)  27.1 us
    all_to_all x1, starting transfers between devices, per_device(): lax.all_to_all(copies_of(potential, NEAR), 'beam', 0, 0, axis_index_group...  13.6 us
    all_to_all x1, blocking collectives, per_device(): lax.all_to_all(jnp.broadcast_to(part[None], (FAR, *part.shape)), 'beam',...  11.4 us
    ppermute x1, starting transfers between devices, per_device(): return mine + lax.ppermute(other, 'core', [(0, 1), (1, 0)])  6.31 us
    all_to_all x1, waiting for transfers between devices, per_device(): lax.all_to_all(copies_of(potential, NEAR), 'beam', 0, 0, axis_index_group...  5.77 us
    pallas_call x1, Pallas kernels, propagate(): pl.pallas_call(propagate_kernel, out_shape=shape_of(F32, 2 * K, K), in_sp...  4.48 us
    pallas_call x1, Pallas kernels, prepare(): pl.pallas_call(prepare_kernel, out_shape=out, in_specs=[SMEM] * 3 + [VMEM...  2.7 us
    unnamed x8, local copies, waits for them, and re-layouts  2.02 us
  transfers between devices with their start and end apart: 2, of which 2 were waited for; matrix products, arithmetic and copies ran while one was open for 0% of the time, Pallas kernels for 4%

profile of v15, /device:TPU:1, one launch (start us, length us, event | category | flops | bytes accessed | tf_op | source)
XLA Modules:
  0.0 77.0 jit_solution(15799945001926207014)
XLA Ops:
  0.0 1.6 %copies.1 = f32[96,4,128]{2,1,0:T(4,128)} custom-call(f32[3,4,128]{2,1,0:T(4,128)} %bitcast.21), custom_call_target="tpu_custom_call" | custom-call | tf_op jit(solution)/shard_map/copies/pallas_call | solution.py:373
  1.6 0.0 copy-start.1
  1.6 13.6 %all-to-all-start = ((f32[96,4,128]{2,1,0:T(4,128)}), f32[96,4,128]{2,1,0:T(4,128)S(1)}, u32[]{:S(2)}, u32[]{:S(2)}) async-start(f32[96,4,128]{2,1,0:T(4,128)} %copies.1), calls=%async_computation | async-start | bytes 393216 | tf_op jit(solution)/shard_map/all_to_all | solution.py:390
  15.2 0.0 copy-start
  15.2 0.7 copy-done
  15.8 0.0 copy-start.2
  15.9 0.7 copy-done.2
  16.5 0.0 copy-start.3
  16.5 0.7 copy-done.3
  17.2 2.7 %prepare.1 = (f32[2,256,128]{2,1,0:T(8,128)S(1)}, bf16[1456,512]{1,0:T(8,128)(2,1)S(1)}, f32[2,176,256]{2,1,0:T(8,128)S(1)}, f32[2,256,128]{2,1,0:T(8,128)S(1)}) custom-call(s32[1]{0:T(128)} %bitcast.own_ref, s32[1]{0:T(128)} %bitcast.3.slab_ref, s32[2,128]{1,0:T(2,128)S(1)} %bitcast.14, s32[2,128]{1,0:T(2,128)S(1)} %bitcast.15, s32[1,128]{1,0:T(1,128)S(1)} %bitcast.18, ...), custom_call_target="tpu_custom_call" | custom-call | tf_op jit(solution)/shard_map/prepare/pallas_call | solution.py:339
  19.9 5.8 %all-to-all-done = f32[96,4,128]{2,1,0:T(4,128)S(1)} async-done(((f32[96,4,128]{2,1,0:T(4,128)}), f32[96,4,128]{2,1,0:T(4,128)S(1)}, u32[]{:S(2)}, u32[]{:S(2)}) %all-to-all-start) | async-done | bytes 196640 | tf_op jit(solution)/shard_map/all_to_all | solution.py:390
  25.7 0.1 broadcast_in_dim.15
  25.7 11.4 %all_to_all.15 = f32[4,384,128]{2,1,0:T(8,128)S(1)} all-to-all(f32[4,384,128]{2,1,0:T(8,128)S(1)} %broadcast_in_dim.15), channel_id=1, replica_groups={{0,128,384,256},{4,132,388,260},{8,136,392,264},{12,140,396,268},{16,14..., dimensions={0} | all-to-all | bytes 1572864 | tf_op jit(solution)/shard_map/all_to_all | solution.py:398
  37.1 0.0 copy-done.1
  37.1 4.5 %propagate.1 = f32[256,128]{1,0:T(8,128)S(1)} custom-call(s32[1]{0:T(128)} %bitcast.own_ref, s32[2,128]{1,0:T(2,128)S(1)} %bitcast.16, f32[1536,128]{1,0:T(8,128)S(1)} %bitcast.11, bf16[1456,512]{1,0:T(8,128)(2,1)S(1)} %get-tuple-element.21.table_ref, f32[2,176,256]{2,1,0:T(8,128)S(1)} %get-tuple-element.22.factor_ref, ...), custom_call_target="tpu_custom_call" | custom-call | tf_op jit(solution)/shard_map/propagate/pallas_call | solution.py:350
  41.6 0.1 broadcast_in_dim.17
  41.7 27.1 %all_to_all.16 = f32[256,2,128]{2,1,0:T(2,128)S(1)} all-to-all(f32[256,2,128]{2,1,0:T(2,128)S(1)} %bitcast.19), channel_id=1, replica_groups=mesh['beam'=128,'pair'=2,'core'=2] {'beam','pair'}, dimensions={0} | all-to-all | bytes 524288 | tf_op jit(solution)/shard_map/all_to_all | solution.py:404
  68.8 0.4 probe.1
  69.2 6.3 %collective-permute-start = (f32[128,128]{1,0:T(8,128)S(1)}, f32[128,128]{1,0:T(8,128)S(1)}, u32[]{:S(2)}, u32[]{:S(2)}) collective-permute-start(f32[128,128]{1,0:T(8,128)S(1)} %get-tuple-element.26), channel_id=1, source_target_pairs={{0,1},{1,0},{2,3},{3,2},{4,5},{5,4},{6,7},{7,6},{8,9},{9,8},{10,11... | collective-permute-start | bytes 196616 | tf_op jit(solution)/shard_map/ppermute | solution.py:406
  75.5 0.9 %collective-permute-done = f32[128,128]{1,0:T(8,128)S(1)} collective-permute-done((f32[128,128]{1,0:T(8,128)S(1)}, f32[128,128]{1,0:T(8,128)S(1)}, u32[]{:S(2)}, u32[]{:S(2)}) %collective-permute-start) | collective-permute-done | bytes 65568 | tf_op jit(solution)/shard_map/ppermute | solution.py:406
  76.4 0.6 add.7
Async XLA Ops:
  1.6 35.6 %copy-start.1 = (s32[128,2]{0,1:T(2,128)S(1)}, s32[128,2]{0,1:T(2,128)}, u32[]{:S(2)}) copy-start(s32[128,2]{0,1:T(2,128)} %param.5) | copy-start | bytes 3076
  1.6 24.1 %all-to-all-start = ((f32[96,4,128]{2,1,0:T(4,128)}), f32[96,4,128]{2,1,0:T(4,128)S(1)}, u32[]{:S(2)}, u32[]{:S(2)}) async-start(f32[96,4,128]{2,1,0:T(4,128)} %copies.1), calls=%async_computation | async-start | bytes 393216 | tf_op jit(solution)/shard_map/all_to_all | solution.py:390
  15.2 0.7 copy-start
  15.8 0.7 copy-start.2
  16.5 0.7 copy-start.3
  69.2 7.2 %collective-permute-start = (f32[128,128]{1,0:T(8,128)S(1)}, f32[128,128]{1,0:T(8,128)S(1)}, u32[]{:S(2)}, u32[]{:S(2)}) collective-permute-start(f32[128,128]{1,0:T(8,128)S(1)} %get-tuple-element.26), channel_id=1, source_target_pairs={{0,1},{1,0},{2,3},{3,2},{4,5},{5,4},{6,7},{7,6},{8,9},{9,8},{10,11... | collective-permute-start | bytes 196616 | tf_op jit(solution)/shard_map/ppermute | solution.py:406
